TPU v7x, 256 devices: a whole 4x4x8 slice. The times are simulated.
256 devices in a mesh: dp: 8 (over y, core), seq: 32 (over x, z).
Axes of the slice: x: 4, y: 4, z: 8, core: 2. Of those that a mesh axis runs over, the one named last changes fastest.
Arguments:
- queries: bfloat16 [8, 4096, 1536], P('dp', 'seq'), may hold values from -6 to 6
- key_rows: bfloat16 [8, 4096, 512], P('dp', 'seq'), may hold values from -6 to 6
- value_rows: bfloat16 [8, 4096, 512], P('dp', 'seq'), may hold values from -6 to 6
- out_grad: bfloat16 [8, 4096, 1536], P('dp', 'seq'), may hold values from -6 to 6
- query_map: bfloat16 [12, 128, 64], replicated, may hold values from -40 to 40
- key_map: bfloat16 [12, 128, 64], replicated, may hold values from -40 to 40
Outputs:
- attended: bfloat16 [8, 4096, 1536], P('dp', 'seq')
- query_grad: bfloat16 [8, 4096, 1536], P('dp', 'seq')
- key_grad: bfloat16 [8, 4096, 512], P('dp', 'seq')
- value_grad: bfloat16 [8, 4096, 512], P('dp', 'seq')
- query_map_grad: float32 [12, 128, 64], replicated
- key_map_grad: float32 [12, 128, 64], replicated
All inputs are finite; a program needn't handle non-finite values.
Results may differ from a plain program's by a relative error of at most 0.013.
Values sent between devices are 32-bit elements; how exact they have to be, the bound alone decides.
No kernel may reach another device: no remote copies, remote signals or barrier semaphores. Data moves between devices by JAX's collectives and lax.ppermute only.
A program may use at most 128 MiB of HBM per device.

v0:
```python
import jax
import jax.numpy as jnp
from jax import lax
from jax.sharding import PartitionSpec as P

H = 12
KVH = 4
DH = 128


def entering(value, axis, join, neutral, backward):
    count, mine = (lax.axis_size(axis), lax.axis_index(axis))
    pieces = jax.tree.map(lambda part: lax.all_gather(part, axis), value)
    if backward:
        pieces = jax.tree.map(lambda part: part[::-1], pieces)
        mine = count - 1 - mine
    total = jax.tree.map(
        lambda part, zero: jnp.full_like(part, 0) + jnp.asarray(zero, part.dtype), value, neutral
    )

    def lap(position, total):
        longer = join(total, jax.tree.map(lambda part: part[position], pieces))
        return jax.tree.map(lambda new, old: jnp.where(position < mine, new, old), longer, total)

    return lax.fori_loop(0, count - 1, lap, total)


def mix(form, left, right):
    return jnp.einsum(form, left, right, preferred_element_type=jnp.float32)


def fine(form, left, right):
    return jnp.einsum(form, left, right, precision=lax.Precision.HIGHEST)


def feature_map(inputs, weight):
    doubled = jnp.concatenate([weight, -weight], axis=-1)
    scores = mix("thd,hdf->htf", inputs, doubled)
    heads, tokens, width = scores.shape
    halves = scores.reshape(heads, tokens, 2, width // 2)
    return jax.nn.softmax(halves, axis=-1).reshape(heads, tokens, width)


def prepare(query_block, key_block, value_block, query_map, key_map):
    tokens = query_block.shape[0]
    group_size = H // KVH
    query_heads = query_block.reshape(tokens, H, DH)
    key_heads = jnp.repeat(key_block.reshape(tokens, KVH, DH), group_size, axis=1)
    value_heads = jnp.repeat(value_block.reshape(tokens, KVH, DH), group_size, axis=1)
    prob_query = feature_map(query_heads, query_map)
    prob_key = feature_map(key_heads, key_map)
    feat_query = prob_query.astype(jnp.bfloat16)
    feat_key = prob_key.astype(jnp.bfloat16)
    local_state = mix("hsf,shd->hfd", feat_key, value_heads)
    local_norm = jnp.sum(feat_key.astype(jnp.float32), axis=1)
    return dict(
        query_heads=query_heads,
        key_heads=key_heads,
        value_heads=value_heads,
        prob_query=prob_query,
        prob_key=prob_key,
        feat_query=feat_query,
        feat_key=feat_key,
        local_state=local_state,
        local_norm=local_norm,
    )


def finish(prepared, grad_block, prefix_state, prefix_norm):
    feat_query = prepared["feat_query"]
    feat_key = prepared["feat_key"]
    value_heads = prepared["value_heads"]
    tokens = feat_query.shape[1]
    causal = jnp.arange(tokens)[:, None] >= jnp.arange(tokens)[None, :]
    scores = jnp.where(causal[None], mix("htf,hsf->hts", feat_query, feat_key), 0.0)
    scores_low = scores.astype(jnp.bfloat16)
    state_low = prefix_state.astype(jnp.bfloat16)
    denominator = jnp.sum(scores, axis=-1) + fine(
        "htf,hf->ht", feat_query.astype(jnp.float32), prefix_norm
    )
    numerator = mix("hts,shd->thd", scores_low, value_heads) + mix(
        "htf,hfd->thd", feat_query, state_low
    )
    row_scale = denominator.T[:, :, None]
    out_full = numerator / row_scale
    grad_full = grad_block.reshape(tokens, H, DH).astype(jnp.float32)
    grad_num = (grad_full / row_scale).astype(jnp.bfloat16)
    grad_den = -jnp.sum(grad_full * out_full, axis=-1) / denominator.T
    carry_state = mix("htf,thd->hfd", feat_query, grad_num)
    carry_norm = fine("htf,th->hf", feat_query.astype(jnp.float32), grad_den)
    attended = out_full.reshape(tokens, H * DH).astype(jnp.bfloat16)
    return dict(
        attended=attended,
        scores_low=scores_low,
        state_low=state_low,
        grad_num=grad_num,
        grad_den=grad_den,
        carry_state=carry_state,
        carry_norm=carry_norm,
    )


def map_back(softened, grad_feat, inputs, weight):
    heads, tokens, width = softened.shape
    halves = softened.reshape(heads, tokens, 2, width // 2)
    grad_halves = grad_feat.reshape(heads, tokens, 2, width // 2)
    inner = jnp.sum(halves * grad_halves, axis=-1, keepdims=True)
    grad_scores = halves * (grad_halves - inner)
    grad_low = (grad_scores[:, :, 0] - grad_scores[:, :, 1]).astype(jnp.bfloat16)
    weight_grad = mix("thd,htf->hdf", inputs, grad_low)
    input_grad = mix("htf,hdf->thd", grad_low, weight)
    return (weight_grad, input_grad)


def gradients(prepared, finished, prefix_norm, back_state, back_norm, query_map, key_map):
    feat_query = prepared["feat_query"]
    feat_key = prepared["feat_key"]
    value_heads = prepared["value_heads"]
    grad_num = finished["grad_num"]
    tokens = feat_query.shape[1]
    group_size = H // KVH
    causal = jnp.arange(tokens)[:, None] >= jnp.arange(tokens)[None, :]
    den_rows = finished["grad_den"].T
    dscore = jnp.where(
        causal[None], mix("thd,shd->hts", grad_num, value_heads) + den_rows[:, :, None], 0.0
    )
    dscore_low = dscore.astype(jnp.bfloat16)
    back_low = back_state.astype(jnp.bfloat16)
    grad_feat_query = (
        mix("hts,hsf->htf", dscore_low, feat_key)
        + mix("thd,hfd->htf", grad_num, finished["state_low"])
        + den_rows[:, :, None] * prefix_norm[:, None, :]
    )
    grad_feat_key = (
        mix("hts,htf->hsf", dscore_low, feat_query)
        + mix("shd,hfd->hsf", value_heads, back_low)
        + back_norm[:, None, :]
    )
    grad_value = mix("hts,thd->shd", finished["scores_low"], grad_num) + mix(
        "hsf,hfd->shd", feat_key, back_low
    )
    value_grad = (
        grad_value.reshape(tokens, KVH, group_size, DH)
        .sum(2)
        .reshape(tokens, KVH * DH)
        .astype(jnp.bfloat16)
    )
    query_weight_grad, query_input = map_back(
        prepared["prob_query"], grad_feat_query, prepared["query_heads"], query_map
    )
    key_weight_grad, key_input = map_back(
        prepared["prob_key"], grad_feat_key, prepared["key_heads"], key_map
    )
    query_grad = query_input.reshape(tokens, H * DH).astype(jnp.bfloat16)
    key_grad = (
        key_input.reshape(tokens, KVH, group_size, DH)
        .sum(2)
        .reshape(tokens, KVH * DH)
        .astype(jnp.bfloat16)
    )
    return (query_grad, key_grad, value_grad, query_weight_grad, key_weight_grad)


def add_pairs(earlier, later):
    return (earlier[0] + later[0], earlier[1] + later[1])


def shards(queries, key_rows, value_rows, out_grad, query_map, key_map):
    prepared = prepare(queries[0], key_rows[0], value_rows[0], query_map, key_map)
    local_state = prepared["local_state"]
    local_norm = prepared["local_norm"]
    empty = (jnp.zeros_like(local_state), jnp.zeros_like(local_norm))
    prefix_state, prefix_norm = entering((local_state, local_norm), "seq", add_pairs, empty, False)
    finished = finish(prepared, out_grad[0], prefix_state, prefix_norm)
    back_state, back_norm = entering(
        (finished["carry_state"], finished["carry_norm"]), "seq", add_pairs, empty, True
    )
    query_grad, key_grad, value_grad, query_weight_grad, key_weight_grad = gradients(
        prepared, finished, prefix_norm, back_state, back_norm, query_map, key_map
    )
    query_total, key_total = lax.psum((query_weight_grad, key_weight_grad), ("dp", "seq"))
    return (
        finished["attended"][None],
        query_grad[None],
        key_grad[None],
        value_grad[None],
        query_total,
        key_total,
    )


def solution(mesh):
    placed = (
        P("dp", "seq", None),
        P("dp", "seq", None),
        P("dp", "seq", None),
        P("dp", "seq", None),
        P(),
        P(),
    )
    return jax.shard_map(
        shards,
        mesh=mesh,
        in_specs=placed,
        out_specs=(
            P("dp", "seq", None),
            P("dp", "seq", None),
            P("dp", "seq", None),
            P("dp", "seq", None),
            P(),
            P(),
        ),
        check_vma=False,
    )
```

profile of v0, /device:TPU:1, one launch (start us, length us, event | category | flops | bytes accessed | tf_op | source)
XLA Modules:
  0.0 806.8 jit_solution(2084693603705930571)
XLA Ops:
  14.0 1.5 bitcast_reduce_fusion
  17.5 2.1 copy.111
  19.6 47.6 %all-gather.4 = f32[32,12,128]{2,1,0:T(8,128)} all-gather(f32[1,12,128]{2,1,0:T(8,128)S(1)} %bitcast.181), channel_id=3, replica_groups=mesh['dp'=8,'seq'=32] {'seq'}, dimensions={0}, use_global_device_ids=true | all-gather | bytes 202752 | tf_op jit(solution)/shard_map/all_gather | solution.py:13
  70.1 135.8 %all-gather.9.cloned.1.call-done = f32[384,128,128]{2,1,0:T(8,128)} async-done(((f32[12,128,128]{2,1,0:T(8,128)}), f32[384,128,128]{2,1,0:T(8,128)}) %all-gather.9.cloned.1.call-update) | async-done | bytes 25165840 | tf_op jit(solution)/shard_map/all_gather | solution.py:13
  205.9 65.5 %while.32 = (s32[]{:T(128)}, f32[12,128,128]{2,1,0:T(8,128)S(1)}, f32[12,128]{1,0:T(8,128)S(1)}, s32[]{:T(128)}, f32[32,12,128,128]{3,2,1,0:T(8,128)}, /*index=5*/f32[32,12,128]{2,1,0:T(8,128)}, s32[]{:T(128)}, s32[]{:T(128)}) while((s32[]{:T(128)}, f32[12,128,128]{2,1,0:T(8,128)S(1)}, f32[12,128]{1,0:T(8,128)S(1)}, s32[]{:T(128)}, ...), condition=%wide.region_6.7_spmd.clone, body=%wide.region_5.6_spmd.clone.sunk | while | flops 594436 | bytes 2377843 | solution.py:25
  205.9 1.4 add_select_fusion.8
  208.0 1.4 add_select_fusion.8
  210.1 1.4 add_select_fusion.8
  212.2 1.4 add_select_fusion.8
  214.3 1.4 add_select_fusion.8
  216.5 1.4 add_select_fusion.8
  218.6 1.4 add_select_fusion.8
  220.7 1.4 add_select_fusion.8
  222.8 1.4 add_select_fusion.8
  224.9 1.4 add_select_fusion.8
  227.0 1.4 add_select_fusion.8
  229.1 1.4 add_select_fusion.8
  231.2 1.4 add_select_fusion.8
  233.4 1.4 add_select_fusion.8
  235.5 1.4 add_select_fusion.8
  237.6 1.4 add_select_fusion.8
  239.7 1.4 add_select_fusion.8
  265.0 1.4 add_select_fusion.8
  267.1 1.4 add_select_fusion.8
  269.2 1.4 add_select_fusion.8
  272.4 3.1 multiply_reduce_fusion.2
  279.1 41.8 %all-gather.5 = f32[32,12,128]{2,1,0:T(8,128)} all-gather(f32[1,12,128]{2,1,0:T(8,128)S(1)} %bitcast.182), channel_id=5, replica_groups=mesh['dp'=8,'seq'=32] {'seq'}, dimensions={0}, use_global_device_ids=true | all-gather | bytes 202752 | tf_op jit(solution)/shard_map/all_gather | solution.py:13
  321.0 1.7 reverse
  326.8 1.4 multiply_reduce_fusion.1
  331.4 1.9 copy.123
  333.3 2.2 convolution_bitcast_fusion.4
  335.4 2.5 fusion.32
  337.9 121.9 %all-gather.11.cloned.1.call-done = f32[384,128,128]{2,1,0:T(8,128)} async-done(((f32[12,128,128]{2,1,0:T(8,128)}), f32[384,128,128]{2,1,0:T(8,128)}) %all-gather.11.cloned.1.call-update) | async-done | bytes 25165840 | tf_op jit(solution)/shard_map/all_gather | solution.py:13
  459.8 17.6 %rev.6 = f32[32,12,128,128]{3,2,1,0:T(8,128)} reverse(f32[32,12,128,128]{3,2,1,0:T(8,128)} %bitcast.163), dimensions={0} | reverse | bytes 50331648 | tf_op jit(solution)/shard_map/rev | solution.py:15
  477.4 65.5 %while.33 = (s32[]{:T(128)}, f32[12,128,128]{2,1,0:T(8,128)S(1)}, f32[12,128]{1,0:T(8,128)S(1)}, s32[]{:T(128)}, f32[32,12,128,128]{3,2,1,0:T(8,128)}, /*index=5*/f32[32,12,128]{2,1,0:T(8,128)}, s32[]{:T(128)}, s32[]{:T(128)}) while((s32[]{:T(128)}, f32[12,128,128]{2,1,0:T(8,128)S(1)}, f32[12,128]{1,0:T(8,128)S(1)}, s32[]{:T(128)}, ...), condition=%wide.region_11.12_spmd.clone, body=%wide.region_10.11_spmd.clone.sunk | while | flops 594436 | bytes 2377843 | solution.py:25
  477.4 1.4 add_select_fusion.10
  500.7 1.4 add_select_fusion.10
  502.8 1.4 add_select_fusion.10
  504.9 1.4 add_select_fusion.10
  507.0 1.4 add_select_fusion.10
  509.1 1.4 add_select_fusion.10
  511.2 1.4 add_select_fusion.10
  540.8 1.4 add_select_fusion.10
  543.3 1.4 multiply_reduce_fusion
  546.1 1.4 convolution_add_fusion.2
  549.6 247.1 %all-reduce.3.cloned.1.call-done = (f32[12,128,64]{1,2,0:T(8,128)}, f32[12,128,64]{1,2,0:T(8,128)}) async-done(((f32[12,128,64]{1,2,0:T(8,128)}, f32[12,128,64]{1,2,0:T(8,128)}), (f32[12,128,64]{1,2,0:T(8,128)}, f32[12,128,64]{1,2,0:T(8,128)})) %all-reduce.3.cloned.1.call-update) | async-done | bytes 786448 | tf_op jit(solution)/shard_map/psum | solution.py:181
  796.7 1.8 copy.179
  798.5 1.8 copy.180
  (188 shorter events, 118.6 us)
Async XLA Ops:
  7.2 198.7 %all-gather.9.cloned.1.call-start = ((), (), s32[]{:S(2)}) async-start(), calls=%async_computation | async-start | bytes 25952256 | tf_op jit(solution)/shard_map/all_gather | solution.py:13
  8.4 5.5 copy-start.4
  13.7 2.5 copy-start.13
  13.9 2.3 copy-start.16
  14.0 1.5 copy-start.5
  15.5 0.7 copy-start.11
  15.7 0.6 copy-start.14
  16.0 261.6 %copy-start = (bf16[12,128,128]{1,2,0:T(8,128)(2,1)}, bf16[12,128,128]{1,2,0:T(8,128)(2,1)S(1)}, u32[]{:S(2)}) copy-start(bf16[12,128,128]{1,2,0:T(8,128)(2,1)S(1)} %get-tuple-element.323) | copy-start | bytes 1179652
  16.1 261.5 %copy-start.2 = (bf16[128,4,3,128]{3,0,2,1:T(8,128)(2,1)}, bf16[128,4,3,128]{3,0,2,1:T(8,128)(2,1)S(1)}, u32[]{:S(2)}) copy-start(bf16[128,4,3,128]{3,0,2,1:T(8,128)(2,1)S(1)} %broadcast_in_dim.27) | copy-start | bytes 1179652
  17.4 442.4 %all-gather.11.cloned.1.call-start = ((), (), s32[]{:S(2)}) async-start(), calls=%async_computation.1 | async-start | bytes 25952256 | tf_op jit(solution)/shard_map/all_gather | solution.py:13
  67.2 0.6 copy-start.20
  68.1 0.7 copy-start.10
  68.1 209.6 %copy-start.19 = (f32[12,128]{1,0:T(8,128)}, f32[12,128]{1,0:T(8,128)S(1)}, u32[]{:S(2)}) copy-start(f32[12,128]{1,0:T(8,128)S(1)} %get-tuple-element.331) | copy-start | bytes 18436
  271.8 0.6 copy-start.17
  271.8 0.6 copy-start.18
  275.5 0.8 copy-start.7
  277.6 519.1 %all-reduce.3.cloned.1.call-start = ((), (), s32[]{:S(2)}) async-start(), calls=%async_computation.2 | async-start | bytes 1572864 | tf_op jit(solution)/shard_map/psum | solution.py:181
  324.8 0.7 copy-start.9
  459.8 83.1 %copy-start.3 = (bf16[128,4,3,128]{3,0,2,1:T(8,128)(2,1)S(1)}, bf16[128,4,3,128]{3,0,2,1:T(8,128)(2,1)}, u32[]{:S(2)}) copy-start(bf16[128,4,3,128]{3,0,2,1:T(8,128)(2,1)} %copy-done.2) | copy-start | bytes 1179652
  459.8 83.5 %copy-start.12 = (f32[12,128,2]{1,2,0:T(2,128)S(1)}, f32[12,128,2]{1,2,0:T(2,128)}, u32[]{:S(2)}) copy-start(f32[12,128,2]{1,2,0:T(2,128)} %copy-done.11) | copy-start | bytes 36868
  459.8 83.5 %copy-start.15 = (f32[12,128,2]{1,2,0:T(2,128)S(1)}, f32[12,128,2]{1,2,0:T(2,128)}, u32[]{:S(2)}) copy-start(f32[12,128,2]{1,2,0:T(2,128)} %copy-done.14) | copy-start | bytes 36868
  459.8 85.3 %copy-start.6 = (bf16[128,4,3,128]{3,0,2,1:T(8,128)(2,1)S(1)}, bf16[128,4,3,128]{3,0,2,1:T(8,128)(2,1)}, u32[]{:S(2)}) copy-start(bf16[128,4,3,128]{3,0,2,1:T(8,128)(2,1)} %copy-done.5) | copy-start | bytes 1179652
  459.8 86.3 %copy-start.1 = (bf16[12,128,128]{1,2,0:T(8,128)(2,1)S(1)}, bf16[12,128,128]{1,2,0:T(8,128)(2,1)}, u32[]{:S(2)}) copy-start(bf16[12,128,128]{1,2,0:T(8,128)(2,1)} %copy-done) | copy-start | bytes 1179652
  477.4 71.0 %copy-start.8 = (bf16[12,128,64]{1,2,0:T(8,128)(2,1)S(1)}, bf16[12,128,64]{1,2,0:T(8,128)(2,1)}, u32[]{:S(2)}) copy-start(bf16[12,128,64]{1,2,0:T(8,128)(2,1)} %param.15) | copy-start | bytes 589828
Sparse Core Ops, SparseCore 0:
  17.5 188.3 all-gather.8
  277.7 181.9 all-gather.10
  546.2 250.4 all-reduce.2
where the time goes:
time: 814 us; the launch traced here: 807 us
  waiting for transfers between devices  505 us (62%)
  other arithmetic  136 us (17%)
  blocking collectives  89.4 us (11%)
  local copies, waits for them, and re-layouts  36.3 us (4%)
  matrix products  25.4 us (3%)
  between operations  14.2 us (2%)
    all_gather x2, waiting for transfers between devices, entering(): pieces = jax.tree.map(lambda part: lax.all_gather(part, axis), value)  258 us
    psum x1, waiting for transfers between devices, shards(): lax.psum((query_weight_grad, key_weight_grad), ('dp', 'seq'))  247 us
    select_n x124, other arithmetic, lap(): jnp.where(position < mine, new, old)  131 us
    all_gather x2, blocking collectives, entering(): pieces = jax.tree.map(lambda part: lax.all_gather(part, axis), value)  89.4 us
    dot_general x18, matrix products, mix(): return jnp.einsum(form, left, right, preferred_element_type=jnp.float32)  24.3 us
    rev x2, local copies, waits for them, and re-layouts, entering(): pieces = jax.tree.map(lambda part: part[::-1], pieces)  19.3 us
  transfers between devices with their start and end apart: 3, of which 3 were waited for; matrix products, arithmetic and copies ran while one was open for 3% of the time, Pallas kernels for 0%

commit v1 on v0

--- a/solution.py
+++ b/solution.py
@@ -1,28 +1,11 @@
 import jax
 import jax.numpy as jnp
 from jax import lax
-from jax.sharding import PartitionSpec as P
+from jax.sharding import Mesh, PartitionSpec as P
 
 H = 12
 KVH = 4
 DH = 128
-
-
-def entering(value, axis, join, neutral, backward):
-    count, mine = (lax.axis_size(axis), lax.axis_index(axis))
-    pieces = jax.tree.map(lambda part: lax.all_gather(part, axis), value)
-    if backward:
-        pieces = jax.tree.map(lambda part: part[::-1], pieces)
-        mine = count - 1 - mine
-    total = jax.tree.map(
-        lambda part, zero: jnp.full_like(part, 0) + jnp.asarray(zero, part.dtype), value, neutral
-    )
-
-    def lap(position, total):
-        longer = join(total, jax.tree.map(lambda part: part[position], pieces))
-        return jax.tree.map(lambda new, old: jnp.where(position < mine, new, old), longer, total)
-
-    return lax.fori_loop(0, count - 1, lap, total)
 
 
 def mix(form, left, right):
@@ -66,36 +49,47 @@
     )
 
 
-def finish(prepared, grad_block, prefix_state, prefix_norm):
+def weigh(prepared, grad_block, prefix_norm):
     feat_query = prepared["feat_query"]
     feat_key = prepared["feat_key"]
-    value_heads = prepared["value_heads"]
     tokens = feat_query.shape[1]
     causal = jnp.arange(tokens)[:, None] >= jnp.arange(tokens)[None, :]
     scores = jnp.where(causal[None], mix("htf,hsf->hts", feat_query, feat_key), 0.0)
     scores_low = scores.astype(jnp.bfloat16)
-    state_low = prefix_state.astype(jnp.bfloat16)
     denominator = jnp.sum(scores, axis=-1) + fine(
         "htf,hf->ht", feat_query.astype(jnp.float32), prefix_norm
     )
-    numerator = mix("hts,shd->thd", scores_low, value_heads) + mix(
-        "htf,hfd->thd", feat_query, state_low
-    )
     row_scale = denominator.T[:, :, None]
-    out_full = numerator / row_scale
     grad_full = grad_block.reshape(tokens, H, DH).astype(jnp.float32)
     grad_num = (grad_full / row_scale).astype(jnp.bfloat16)
-    grad_den = -jnp.sum(grad_full * out_full, axis=-1) / denominator.T
     carry_state = mix("htf,thd->hfd", feat_query, grad_num)
+    return dict(
+        scores_low=scores_low,
+        denominator=denominator,
+        row_scale=row_scale,
+        grad_full=grad_full,
+        grad_num=grad_num,
+        carry_state=carry_state,
+    )
+
+
+def finish(prepared, weighed, prefix_state):
+    feat_query = prepared["feat_query"]
+    tokens = feat_query.shape[1]
+    state_low = prefix_state.astype(jnp.bfloat16)
+    numerator = mix("hts,shd->thd", weighed["scores_low"], prepared["value_heads"]) + mix(
+        "htf,hfd->thd", feat_query, state_low
+    )
+    out_full = numerator / weighed["row_scale"]
+    grad_den = -jnp.sum(weighed["grad_full"] * out_full, axis=-1) / weighed["denominator"].T
     carry_norm = fine("htf,th->hf", feat_query.astype(jnp.float32), grad_den)
     attended = out_full.reshape(tokens, H * DH).astype(jnp.bfloat16)
     return dict(
         attended=attended,
-        scores_low=scores_low,
+        scores_low=weighed["scores_low"],
         state_low=state_low,
-        grad_num=grad_num,
+        grad_num=weighed["grad_num"],
         grad_den=grad_den,
-        carry_state=carry_state,
         carry_norm=carry_norm,
     )
 
@@ -161,52 +155,101 @@
     return (query_grad, key_grad, value_grad, query_weight_grad, key_weight_grad)
 
 
-def add_pairs(earlier, later):
-    return (earlier[0] + later[0], earlier[1] + later[1])
+N_SEQ = 32
+ROWS = H * DH // N_SEQ
+SEQ = ("x", "z")
+
+
+def exchange(blocks, axes=SEQ):
+    return lax.all_to_all(blocks, axes, 0, 0, tiled=True)
+
+
+def to_all(rows):
+    padded = jnp.pad(rows, ((0, 16 - H), (0, 0)))
+    return jnp.broadcast_to(padded[None], (N_SEQ,) + padded.shape)
+
+
+def sum_before(parts):
+    inclusive = jnp.cumsum(parts, axis=0)
+    return jnp.concatenate([jnp.zeros_like(parts[:1]), inclusive[:-1]], 0)
+
+
+def sum_after(parts):
+    return sum_before(parts[::-1])[::-1]
+
+
+def summed_everywhere(values):
+    core = lax.axis_index("core")
+    halves = values.reshape(2, -1, DH)
+    mine = lax.dynamic_index_in_dim(halves, core, 0, False)
+    other = lax.dynamic_index_in_dim(halves, 1 - core, 0, False)
+    swap = [(0, 1), (1, 0)]
+    mine = mine + lax.ppermute(other, "core", swap)
+    part = exchange(mine.reshape(N_SEQ, -1, DH)).sum(0)
+    total = part
+    for step in range(1, 4):
+        total = total + lax.ppermute(part, "y", [(i, (i + step) % 4) for i in range(4)])
+    half = exchange(jnp.broadcast_to(total[None], (N_SEQ,) + total.shape)).reshape(-1, DH)
+    swapped = lax.ppermute(half, "core", swap)
+    low = jnp.where(core == 0, half, swapped)
+    high = jnp.where(core == 0, swapped, half)
+    return jnp.concatenate([low, high], 0)
 
 
 def shards(queries, key_rows, value_rows, out_grad, query_map, key_map):
+    me = lax.axis_index(SEQ)
+    order = jnp.arange(N_SEQ)[:, None, None]
     prepared = prepare(queries[0], key_rows[0], value_rows[0], query_map, key_map)
-    local_state = prepared["local_state"]
-    local_norm = prepared["local_norm"]
-    empty = (jnp.zeros_like(local_state), jnp.zeros_like(local_norm))
-    prefix_state, prefix_norm = entering((local_state, local_norm), "seq", add_pairs, empty, False)
-    finished = finish(prepared, out_grad[0], prefix_state, prefix_norm)
-    back_state, back_norm = entering(
-        (finished["carry_state"], finished["carry_norm"]), "seq", add_pairs, empty, True
-    )
+    local_state = prepared["local_state"].reshape(N_SEQ, ROWS, DH)
+    first = exchange(jnp.concatenate([local_state, to_all(prepared["local_norm"])], 1))
+    prefix_norm = jnp.sum(jnp.where(order < me, first[:, ROWS : ROWS + H], 0.0), 0)
+    weighed = weigh(prepared, out_grad[0], prefix_norm)
+    carry_state = weighed["carry_state"].reshape(N_SEQ, ROWS, DH)
+    second = exchange(jnp.concatenate([sum_before(first[:, :ROWS]), carry_state], 1))
+    prefix_state = second[:, :ROWS].reshape(H, DH, DH)
+    finished = finish(prepared, weighed, prefix_state)
+    third = exchange(
+        jnp.concatenate([sum_after(second[:, ROWS:]), to_all(finished["carry_norm"])], 1)
+    )
+    back_state = third[:, :ROWS].reshape(H, DH, DH)
+    back_norm = jnp.sum(jnp.where(order > me, third[:, ROWS : ROWS + H], 0.0), 0)
     query_grad, key_grad, value_grad, query_weight_grad, key_weight_grad = gradients(
         prepared, finished, prefix_norm, back_state, back_norm, query_map, key_map
     )
-    query_total, key_total = lax.psum((query_weight_grad, key_weight_grad), ("dp", "seq"))
+    weights = jnp.stack([query_weight_grad, key_weight_grad])
+    totals = summed_everywhere(weights.reshape(-1, DH)).reshape(weights.shape)
     return (
         finished["attended"][None],
         query_grad[None],
         key_grad[None],
         value_grad[None],
-        query_total,
-        key_total,
-    )
+        totals[0],
+        totals[1],
+    )
+
+
+ROWS_SPLIT = P(("y", "core"), ("x", "z"), None)
 
 
 def solution(mesh):
+    fine_mesh = Mesh(mesh.devices.reshape(4, 2, 4, 8), ("y", "core", "x", "z"))
     placed = (
-        P("dp", "seq", None),
-        P("dp", "seq", None),
-        P("dp", "seq", None),
-        P("dp", "seq", None),
+        ROWS_SPLIT,
+        ROWS_SPLIT,
+        ROWS_SPLIT,
+        ROWS_SPLIT,
         P(),
         P(),
     )
     return jax.shard_map(
         shards,
-        mesh=mesh,
+        mesh=fine_mesh,
         in_specs=placed,
         out_specs=(
-            P("dp", "seq", None),
-            P("dp", "seq", None),
-            P("dp", "seq", None),
-            P("dp", "seq", None),
+            ROWS_SPLIT,
+            ROWS_SPLIT,
+            ROWS_SPLIT,
+            ROWS_SPLIT,
             P(),
             P(),
         ),

time: 814 us -> 211 us (0.26)
  waiting for transfers between devices: 505 us -> 82.4 us
  other arithmetic: 136 us -> 13.8 us
  blocking collectives: 89.4 us -> 16.2 us
  starting transfers between devices: 0.12 us -> 51.8 us
  between operations: 14.2 us -> 1.32 us
  matrix products: 25.4 us -> 15.6 us
    all_gather x2 -> x0, waiting for transfers between devices: 258 us -> none  [entering(): pieces = jax.tree.map(lambda part: lax.all_gather(part, axis), value)]
    psum x1 -> x0, waiting for transfers between devices: 247 us -> none  [shards(): lax.psum((query_weight_grad, key_weight_grad), ('dp', 'seq'))]
    select_n x124 -> x1, other arithmetic: 131 us -> 0.05 us  [summed_everywhere(): high = jnp.where(core == 0, swapped, half)]
    all_gather x2 -> x0, blocking collectives: 89.4 us -> none  [entering(): pieces = jax.tree.map(lambda part: lax.all_gather(part, axis), value)]
    all_to_all x0 -> x4, waiting for transfers between devices: none -> 79.6 us  [exchange(): return lax.all_to_all(blocks, axes, 0, 0, tiled=True)]
    all_to_all x0 -> x4, starting transfers between devices: none -> 36.4 us  [exchange(): return lax.all_to_all(blocks, axes, 0, 0, tiled=True)]
    all_to_all x0 -> x1, blocking collectives: none -> 16.2 us  [exchange(): return lax.all_to_all(blocks, axes, 0, 0, tiled=True)]
    ppermute x0 -> x5, starting transfers between devices: none -> 15.4 us  [the longest x1 5.25 us: summed_everywhere(): swapped = lax.ppermute(half, 'core', swap)]
  transfers between devices with their start and end apart: 3 -> 9, of which waited for: 3 -> 7; matrix products, arithmetic and copies ran while one was open for 3% -> 8% of each run, Pallas kernels for 0% -> 0%
where the time goes in v1:
time: 211 us; the launch traced here: 210 us
  waiting for transfers between devices  82.4 us (39%)
  starting transfers between devices  51.8 us (25%)
  local copies, waits for them, and re-layouts  28.6 us (14%)
  blocking collectives  16.2 us (8%)
  matrix products  15.6 us (7%)
  other arithmetic  13.8 us (7%)
    all_to_all x4, waiting for transfers between devices, exchange(): return lax.all_to_all(blocks, axes, 0, 0, tiled=True)  79.6 us
    all_to_all x4, starting transfers between devices, exchange(): return lax.all_to_all(blocks, axes, 0, 0, tiled=True)  36.4 us
    all_to_all x1, blocking collectives, exchange(): return lax.all_to_all(blocks, axes, 0, 0, tiled=True)  16.2 us
    dot_general x18, matrix products, mix(): return jnp.einsum(form, left, right, preferred_element_type=jnp.float32)  14.4 us
    unnamed x70, local copies, waits for them, and re-layouts  11.4 us
    ppermute x1, starting transfers between devices, summed_everywhere(): swapped = lax.ppermute(half, 'core', swap)  5.25 us
    ppermute x1, starting transfers between devices, summed_everywhere(): mine = mine + lax.ppermute(other, 'core', swap)  5.06 us
    ppermute x3, starting transfers between devices, summed_everywhere(): lax.ppermute(part, 'y', [(i, (i + step) % 4) for i in range(4)])  5.06 us
  transfers between devices with their start and end apart: 9, of which 7 were waited for; matrix products, arithmetic and copies ran while one was open for 8% of the time, Pallas kernels for 0%

profile of v1, /device:TPU:1, one launch (start us, length us, event | category | flops | bytes accessed | tf_op | source)
XLA Modules:
  0.0 209.8 jit_solution(11341167762694828091)
XLA Ops:
  0.6 1.0 reshape_squeeze.11
  1.7 1.0 neg.14
  5.0 1.2 pad_maximum_fusion
  6.1 12.1 %all-to-all-start = ((f32[32,64,128]{2,1,0:T(8,128)}), f32[32,64,128]{2,1,0:T(8,128)}, u32[]{:S(2)}, u32[]{:S(2)}) async-start(f32[32,64,128]{2,1,0:T(8,128)} %pad_maximum_fusion), calls=%async_computation | async-start | bytes 2097152 | tf_op jit(solution)/shard_map/all_to_all | solution.py:164
  20.2 1.0 copy.117
  21.3 1.1 fusion.43
  22.4 20.5 %all-to-all-done = f32[32,64,128]{2,1,0:T(8,128)} async-done(((f32[32,64,128]{2,1,0:T(8,128)}), f32[32,64,128]{2,1,0:T(8,128)}, u32[]{:S(2)}, u32[]{:S(2)}) %all-to-all-start) | async-done | bytes 1048608 | tf_op jit(solution)/shard_map/all_to_all | solution.py:164
  42.9 1.1 fusion.29
  45.0 1.2 divide_convert_fusion
  46.6 1.2 fusion.6
  47.9 1.3 select_maximum_fusion
  49.2 8.7 %all-to-all-start.1 = ((f32[32,96,128]{2,1,0:T(8,128)}), f32[32,96,128]{2,1,0:T(8,128)}, u32[]{:S(2)}, u32[]{:S(2)}) async-start(f32[32,96,128]{2,1,0:T(8,128)} %select_maximum_fusion), calls=%async_computation.1 | async-start | bytes 3145728 | tf_op jit(solution)/shard_map/all_to_all | solution.py:164
  57.9 2.2 %convolution_bitcast_fusion.2 = f32[128,12,128]{0,2,1:T(8,128)} fusion(bf16[128,12,128]{2,0,1:T(8,128)(2,1)S(1)} %bitcast.161, bf16[12,128,128]{1,2,0:T(8,128)(2,1)} %get-tuple-element.41), kind=kOutput, calls=%fused_computation.9 | convolution fusion | flops 50331648 | bytes 1572864 | tf_op jit(solution)/shard_map/hts,shd->thd/dot_general | solution.py:12
  60.1 34.6 %all-to-all-done.1 = f32[32,96,128]{2,1,0:T(8,128)} async-done(((f32[32,96,128]{2,1,0:T(8,128)}), f32[32,96,128]{2,1,0:T(8,128)}, u32[]{:S(2)}, u32[]{:S(2)}) %all-to-all-start.1) | async-done | bytes 1572896 | tf_op jit(solution)/shard_map/all_to_all | solution.py:164
  94.7 1.2 slice.93
  95.9 2.6 %multiply_reduce_fusion.2 = (f32[128,12]{0,1:T(8,128)S(1)}, bf16[128,12,128]{0,2,1:T(8,128)(2,1)}) fusion(f32[128,12,128]{0,2,1:T(8,128)} %bitcast.171, f32[128,12]{0,1:T(8,128)} %copy-done.23, f32[128,12,128]{0,2,1:T(8,128)} %convolution_bitcast_fusion.2, bf16[12,128,128]{2,1,0:T(8,128)(2,1)S(1)} %bitcast.176, bf16[12,128,128]{1,2,0:T(8,128)(2,1)S(1)} %fusion.11), kind=kOutput, calls=%fused_computation.43 | convolution fusion | flops 51313152 | bytes 2764800 | tf_op jit(solution)/shard_map/htf,hfd->thd/dot_general | solution.py:12
  99.9 2.1 slice.60
  102.0 2.1 rev.6
  104.1 1.2 fusion.44
  105.3 0.9 concatenate.28
  106.3 2.1 %rev.7 = f32[32,48,128]{2,1,0:T(8,128)} reverse(f32[32,48,128]{2,1,0:T(8,128)} %concatenate.28), dimensions={0} | reverse | bytes 1572864 | tf_op jit(solution)/shard_map/rev | solution.py:178
  109.1 2.2 %pad_maximum_fusion.1 = f32[32,64,128]{2,1,0:T(8,128)} fusion(f32[32,16,128]{2,1,0:T(8,128)S(1)} %broadcast_in_dim.89, f32[32,48,128]{2,1,0:T(8,128)} %rev.7), kind=kLoop, calls=%fused_computation.20 | loop fusion | flops 262144 | bytes 2097152 | tf_op jit(solution)/shard_map/concatenate | solution.py:212
  111.3 7.8 %all-to-all-start.2 = ((f32[32,64,128]{2,1,0:T(8,128)}), f32[32,64,128]{2,1,0:T(8,128)}, u32[]{:S(2)}, u32[]{:S(2)}) async-start(f32[32,64,128]{2,1,0:T(8,128)} %pad_maximum_fusion.1), calls=%async_computation.2 | async-start | bytes 2097152 | tf_op jit(solution)/shard_map/all_to_all | solution.py:164
  119.9 1.0 fusion.5
  124.0 0.9 stack.9
  125.0 1.0 constant_dynamic-update-slice_fusion.1
  126.0 17.9 %all-to-all-done.2 = f32[32,64,128]{2,1,0:T(8,128)} async-done(((f32[32,64,128]{2,1,0:T(8,128)}), f32[32,64,128]{2,1,0:T(8,128)}, u32[]{:S(2)}, u32[]{:S(2)}) %all-to-all-start.2) | async-done | bytes 1048608 | tf_op jit(solution)/shard_map/all_to_all | solution.py:164
  143.9 1.2 slice.92
  145.4 1.1 fusion.28
  146.5 1.4 multiply_reduce_fusion
  149.0 1.0 convolution_bitcast_fusion.3
  150.0 1.3 copy.132
  151.5 5.1 %collective-permute-start = (f32[768,128]{1,0:T(8,128)S(1)}, f32[768,128]{1,0:T(8,128)S(1)}, u32[]{:S(2)}, u32[]{:S(2)}) collective-permute-start(f32[768,128]{1,0:T(8,128)S(1)} %dynamic-slice_bitcast_fusion), channel_id=1, source_target_pairs={{0,32},{32,0},{1,33},{33,1},{2,34},{34,2},{3,35},{35,3},{4,36},{36... | collective-permute-start | bytes 1179656 | tf_op jit(solution)/shard_map/ppermute | solution.py:187
  156.6 1.3 collective-permute-done
  158.0 16.2 %all_to_all.25 = f32[32,24,128]{2,1,0:T(8,128)S(1)} all-to-all(f32[32,24,128]{2,1,0:T(8,128)S(1)} %bitcast.180), channel_id=1, replica_groups=mesh['y'=4,'core'=2,'x'=4,'z'=8] {'x','z'}, dimensions={0} | all-to-all | bytes 786432 | tf_op jit(solution)/shard_map/all_to_all | solution.py:164
  174.2 1.4 collective-permute-start.1
  175.6 2.6 %collective-permute-start.2 = (f32[24,128]{1,0:T(8,128)S(1)}, f32[24,128]{1,0:T(8,128)S(1)}, u32[]{:S(2)}, u32[]{:S(2)}) collective-permute-start(f32[24,128]{1,0:T(8,128)S(1)} %reduce_sum.119), channel_id=1, source_target_pairs={{0,128},{64,192},{128,0},{192,64},{1,129},{65,193},{129,1},{193,65... | collective-permute-start | bytes 36872 | tf_op jit(solution)/shard_map/ppermute | solution.py:191
  178.2 1.1 collective-permute-start.3
  179.6 1.1 collective-permute-done.3
  180.7 0.8 broadcast_in_dim.91
  181.5 7.9 %all-to-all-start.4 = ((f32[32,24,128]{2,1,0:T(8,128)}), f32[32,24,128]{2,1,0:T(8,128)S(1)}, u32[]{:S(2)}, u32[]{:S(2)}) async-start(f32[32,24,128]{2,1,0:T(8,128)} %broadcast_in_dim.91), calls=%async_computation.4 | async-start | bytes 786432 | tf_op jit(solution)/shard_map/all_to_all | solution.py:164
  189.4 1.4 fusion.32
  191.2 0.9 copy.134
  192.1 0.9 copy.133
  193.0 6.6 %all-to-all-done.4 = f32[32,24,128]{2,1,0:T(8,128)S(1)} async-done(((f32[32,24,128]{2,1,0:T(8,128)}), f32[32,24,128]{2,1,0:T(8,128)S(1)}, u32[]{:S(2)}, u32[]{:S(2)}) %all-to-all-start.4) | async-done | bytes 393248 | tf_op jit(solution)/shard_map/all_to_all | solution.py:164
  199.6 5.3 %collective-permute-start.4 = (f32[768,128]{1,0:T(8,128)S(1)}, f32[768,128]{1,0:T(8,128)S(1)}, u32[]{:S(2)}, u32[]{:S(2)}) collective-permute-start(f32[768,128]{1,0:T(8,128)S(1)} %bitcast.179), channel_id=1, source_target_pairs={{0,32},{32,0},{1,33},{33,1},{2,34},{34,2},{3,35},{35,3},{4,36},{36... | collective-permute-start | bytes 1179656 | tf_op jit(solution)/shard_map/ppermute | solution.py:193
  207.6 1.0 copy.137
  208.8 1.0 copy.138
  (121 shorter events, 16.8 us)
Async XLA Ops:
  0.6 2.1 copy-start.2
  2.7 0.8 copy-start
  2.7 1.8 copy-start.22
  3.6 0.6 copy-start.18
  6.1 12.1 %copy-start.13 = (bf16[1,128,1536]{2,1,0:T(8,128)(2,1)S(1)}, bf16[1,128,1536]{2,1,0:T(8,128)(2,1)}, u32[]{:S(2)}) copy-start(bf16[1,128,1536]{2,1,0:T(8,128)(2,1)} %param.6) | copy-start | bytes 1179652
  6.1 12.4 %copy-start.4 = (bf16[12,128,64]{1,2,0:T(8,128)(2,1)S(1)}, bf16[12,128,64]{1,2,0:T(8,128)(2,1)}, u32[]{:S(2)}) copy-start(bf16[12,128,64]{1,2,0:T(8,128)(2,1)} %param.10) | copy-start | bytes 589828
  6.1 36.7 %all-to-all-start = ((f32[32,64,128]{2,1,0:T(8,128)}), f32[32,64,128]{2,1,0:T(8,128)}, u32[]{:S(2)}, u32[]{:S(2)}) async-start(f32[32,64,128]{2,1,0:T(8,128)} %pad_maximum_fusion), calls=%async_computation | async-start | bytes 2097152 | tf_op jit(solution)/shard_map/all_to_all | solution.py:164
  18.8 0.6 copy-start.16
  18.9 1.3 copy-start.15
  19.4 0.6 copy-start.20
  21.3 23.1 %copy-start.30 = (pred[128,128]{0,1:T(8,128)(4,1)}, pred[128,128]{0,1:T(8,128)(4,1)S(1)}, u32[]{:S(2)}) copy-start(pred[128,128]{0,1:T(8,128)(4,1)S(1)} %iota_compare_fusion.1) | copy-start | bytes 49156
  22.4 22.0 %copy-start.29 = (f32[12,128]{1,0:T(8,128)}, f32[12,128]{1,0:T(8,128)S(1)}, u32[]{:S(2)}) copy-start(f32[12,128]{1,0:T(8,128)S(1)} %get-tuple-element.40) | copy-start | bytes 18436
  43.9 0.6 copy-start.25
  44.4 0.6 copy-start.27
  45.0 1.2 copy-start.23
  49.2 45.5 %all-to-all-start.1 = ((f32[32,96,128]{2,1,0:T(8,128)}), f32[32,96,128]{2,1,0:T(8,128)}, u32[]{:S(2)}, u32[]{:S(2)}) async-start(f32[32,96,128]{2,1,0:T(8,128)} %select_maximum_fusion), calls=%async_computation.1 | async-start | bytes 3145728 | tf_op jit(solution)/shard_map/all_to_all | solution.py:164
  95.9 2.7 %copy-start.10 = (bf16[32,48,128]{2,1,0:T(8,128)(2,1)}, bf16[32,48,128]{2,1,0:T(8,128)(2,1)S(1)}, u32[]{:S(2)}) copy-start(bf16[32,48,128]{2,1,0:T(8,128)(2,1)S(1)} %slice.93) | copy-start | bytes 1179652
  95.9 2.7 %copy-start.24 = (f32[128,12]{0,1:T(8,128)S(1)}, f32[128,12]{0,1:T(8,128)}, u32[]{:S(2)}) copy-start(f32[128,12]{0,1:T(8,128)} %copy-done.23) | copy-start | bytes 18436
  98.6 1.4 copy-start.28
  111.3 32.5 %all-to-all-start.2 = ((f32[32,64,128]{2,1,0:T(8,128)}), f32[32,64,128]{2,1,0:T(8,128)}, u32[]{:S(2)}, u32[]{:S(2)}) async-start(f32[32,64,128]{2,1,0:T(8,128)} %pad_maximum_fusion.1), calls=%async_computation.2 | async-start | bytes 2097152 | tf_op jit(solution)/shard_map/all_to_all | solution.py:164
  119.1 2.8 %copy-start.11 = (bf16[32,48,128]{2,1,0:T(8,128)(2,1)S(1)}, bf16[32,48,128]{2,1,0:T(8,128)(2,1)}, u32[]{:S(2)}) copy-start(bf16[32,48,128]{2,1,0:T(8,128)(2,1)} %copy-done.10) | copy-start | bytes 1179652
  119.1 2.8 %copy-start.17 = (f32[12,128,2]{1,2,0:T(2,128)S(1)}, f32[12,128,2]{1,2,0:T(2,128)}, u32[]{:S(2)}) copy-start(f32[12,128,2]{1,2,0:T(2,128)} %copy-done.16) | copy-start | bytes 36868
  119.1 2.8 %copy-start.21 = (f32[12,128,2]{1,2,0:T(2,128)S(1)}, f32[12,128,2]{1,2,0:T(2,128)}, u32[]{:S(2)}) copy-start(f32[12,128,2]{1,2,0:T(2,128)} %copy-done.20) | copy-start | bytes 36868
  119.1 2.8 %copy-start.26 = (f32[12,128]{1,0:T(8,128)S(1)}, f32[12,128]{1,0:T(8,128)}, u32[]{:S(2)}) copy-start(f32[12,128]{1,0:T(8,128)} %copy-done.25) | copy-start | bytes 18436
  120.9 0.7 copy-start.12
  122.7 0.7 copy-start.8
  146.5 1.5 copy-start.19
  148.0 1.0 copy-start.1
  149.0 2.4 %copy-start.6 = (bf16[12,128,64]{1,2,0:T(8,128)(2,1)}, bf16[12,128,64]{1,2,0:T(8,128)(2,1)S(1)}, u32[]{:S(2)}) copy-start(bf16[12,128,64]{1,2,0:T(8,128)(2,1)S(1)} %fusion.31) | copy-start | bytes 589828
  151.5 6.4 %collective-permute-start = (f32[768,128]{1,0:T(8,128)S(1)}, f32[768,128]{1,0:T(8,128)S(1)}, u32[]{:S(2)}, u32[]{:S(2)}) collective-permute-start(f32[768,128]{1,0:T(8,128)S(1)} %dynamic-slice_bitcast_fusion), channel_id=1, source_target_pairs={{0,32},{32,0},{1,33},{33,1},{2,34},{34,2},{3,35},{35,3},{4,36},{36... | collective-permute-start | bytes 1179656 | tf_op jit(solution)/shard_map/ppermute | solution.py:187
  174.2 16.7 %copy-start.5 = (bf16[12,128,64]{1,2,0:T(8,128)(2,1)S(1)}, bf16[12,128,64]{1,2,0:T(8,128)(2,1)}, u32[]{:S(2)}) copy-start(bf16[12,128,64]{1,2,0:T(8,128)(2,1)} %param.10) | copy-start | bytes 589828
  174.2 16.7 %copy-start.9 = (bf16[12,128,64]{1,2,0:T(8,128)(2,1)S(1)}, bf16[12,128,64]{1,2,0:T(8,128)(2,1)}, u32[]{:S(2)}) copy-start(bf16[12,128,64]{1,2,0:T(8,128)(2,1)} %copy-done.8) | copy-start | bytes 589828
  174.2 5.1 %collective-permute-start.1 = (f32[24,128]{1,0:T(8,128)S(1)}, f32[24,128]{1,0:T(8,128)S(1)}, u32[]{:S(2)}, u32[]{:S(2)}) collective-permute-start(f32[24,128]{1,0:T(8,128)S(1)} %reduce_sum.119), channel_id=1, source_target_pairs={{0,64},{64,128},{128,192},{192,0},{1,65},{65,129},{129,193},{193,1... | collective-permute-start | bytes 36872 | tf_op jit(solution)/shard_map/ppermute | solution.py:191
  175.6 4.1 %collective-permute-start.2 = (f32[24,128]{1,0:T(8,128)S(1)}, f32[24,128]{1,0:T(8,128)S(1)}, u32[]{:S(2)}, u32[]{:S(2)}) collective-permute-start(f32[24,128]{1,0:T(8,128)S(1)} %reduce_sum.119), channel_id=1, source_target_pairs={{0,128},{64,192},{128,0},{192,64},{1,129},{65,193},{129,1},{193,65... | collective-permute-start | bytes 36872 | tf_op jit(solution)/shard_map/ppermute | solution.py:191
  178.2 2.5 %collective-permute-start.3 = (f32[24,128]{1,0:T(8,128)S(1)}, f32[24,128]{1,0:T(8,128)S(1)}, u32[]{:S(2)}, u32[]{:S(2)}) collective-permute-start(f32[24,128]{1,0:T(8,128)S(1)} %reduce_sum.119), channel_id=1, source_target_pairs={{0,192},{64,0},{128,64},{192,128},{1,193},{65,1},{129,65},{193,129... | collective-permute-start | bytes 36872 | tf_op jit(solution)/shard_map/ppermute | solution.py:191
  181.5 18.1 %all-to-all-start.4 = ((f32[32,24,128]{2,1,0:T(8,128)}), f32[32,24,128]{2,1,0:T(8,128)S(1)}, u32[]{:S(2)}, u32[]{:S(2)}) async-start(f32[32,24,128]{2,1,0:T(8,128)} %broadcast_in_dim.91), calls=%async_computation.4 | async-start | bytes 786432 | tf_op jit(solution)/shard_map/all_to_all | solution.py:164
  189.4 2.7 %copy-start.14 = (bf16[128,12,128]{0,2,1:T(8,128)(2,1)S(1)}, bf16[128,12,128]{0,2,1:T(8,128)(2,1)}, u32[]{:S(2)}) copy-start(bf16[128,12,128]{0,2,1:T(8,128)(2,1)} %get-tuple-element.35) | copy-start | bytes 1179652
  199.6 6.4 %copy-start.3 = (bf16[12,128,64]{1,2,0:T(8,128)(2,1)S(1)}, bf16[12,128,64]{1,2,0:T(8,128)(2,1)}, u32[]{:S(2)}) copy-start(bf16[12,128,64]{1,2,0:T(8,128)(2,1)} %param.11) | copy-start | bytes 589828
  199.6 6.4 %copy-start.7 = (bf16[12,128,64]{1,2,0:T(8,128)(2,1)S(1)}, bf16[12,128,64]{1,2,0:T(8,128)(2,1)}, u32[]{:S(2)}) copy-start(bf16[12,128,64]{1,2,0:T(8,128)(2,1)} %copy-done.6) | copy-start | bytes 589828
  199.6 7.7 %collective-permute-start.4 = (f32[768,128]{1,0:T(8,128)S(1)}, f32[768,128]{1,0:T(8,128)S(1)}, u32[]{:S(2)}, u32[]{:S(2)}) collective-permute-start(f32[768,128]{1,0:T(8,128)S(1)} %bitcast.179), channel_id=1, source_target_pairs={{0,32},{32,0},{1,33},{33,1},{2,34},{34,2},{3,35},{35,3},{4,36},{36... | collective-permute-start | bytes 1179656 | tf_op jit(solution)/shard_map/ppermute | solution.py:193

commit v2 on v0

v2 whole, which is shorter than its diff:
```python
import jax
import jax.numpy as jnp
from jax import lax
from jax.experimental import pallas as pl
from jax.experimental.pallas import tpu as pltpu
from jax.sharding import Mesh, PartitionSpec as P

H = 12
KVH = 4
GROUP = H // KVH
DH = 128
FH = 64
TOK = 128
N_SEQ = 32
ROWS = H * DH // N_SEQ
PAD = 16
SEQ = ("x", "z")
F32 = jnp.float32
BF16 = jnp.bfloat16


def nn(left, right):
    return lax.dot_general(left, right, (((1,), (0,)), ((), ())), preferred_element_type=F32)


def nt(left, right):
    return lax.dot_general(left, right, (((1,), (1,)), ((), ())), preferred_element_type=F32)


def tn(left, right):
    return lax.dot_general(left, right, (((0,), (0,)), ((), ())), preferred_element_type=F32)


def of_head(h):
    return slice(h * DH, (h + 1) * DH)


def pieces(h):
    row, end = h * DH, (h + 1) * DH
    while row < end:
        block, first = divmod(row, ROWS)
        count = min(ROWS - first, end - row)
        yield block, first, count, row - h * DH
        row += count


def put_head(ref, base, h, rows):
    for block, first, count, start in pieces(h):
        ref[block, base + first : base + first + count, :] = rows[start : start + count]


def get_head(ref, base, h):
    parts = [
        ref[block, base + first : base + first + count, :]
        for block, first, count, start in pieces(h)
    ]
    return jnp.concatenate(parts, axis=0)


def two_softmaxes(scores):
    high = jnp.exp(scores - jnp.max(scores, axis=0, keepdims=True))
    low = jnp.exp(jnp.min(scores, axis=0, keepdims=True) - scores)
    high = high * (1.0 / jnp.sum(high, axis=0, keepdims=True))
    low = low * (1.0 / jnp.sum(low, axis=0, keepdims=True))
    return jnp.concatenate([high, low], axis=0)


def causal():
    shape = (TOK, TOK)
    key = lax.broadcasted_iota(jnp.int32, shape, 0)
    query = lax.broadcasted_iota(jnp.int32, shape, 1)
    return key <= query


def back_through(prob, grad):
    p1, p2 = prob[:FH], prob[FH:]
    d1, d2 = grad[:FH], grad[FH:]
    inner1 = jnp.sum(p1 * d1, axis=0, keepdims=True)
    inner2 = jnp.sum(p2 * d2, axis=0, keepdims=True)
    return (p1 * (d1 - inner1) - p2 * (d2 - inner2)).astype(BF16)


def key_kernel(k_ref, v_ref, km_ref, send_ref, pk_ref, norm_ref):
    ones = jnp.ones((8, TOK), BF16)
    norm_ref[...] = jnp.zeros_like(norm_ref)
    for h in range(H):
        kv = of_head(h // GROUP)
        prob = two_softmaxes(nt(km_ref[h], k_ref[:, kv]))
        pk_ref[h] = prob
        feat = prob.astype(BF16)
        put_head(send_ref, 0, h, nn(feat, v_ref[:, kv]))
        norm_ref[h : h + 1, :] = nt(ones, feat)[0:1]
    send_ref[:, ROWS:, :] = jnp.broadcast_to(norm_ref[...][None], (N_SEQ, PAD, DH))


def query_kernel(q_ref, v_ref, qm_ref, pk_ref, pq_ref, low_ref, rows_ref, num_ref):
    mask = causal()
    rows_ref[...] = jnp.ones_like(rows_ref)
    for h in range(H):
        prob = two_softmaxes(nt(qm_ref[h], q_ref[:, of_head(h)]))
        pq_ref[h] = prob
        scores = jnp.where(mask, tn(pk_ref[h].astype(BF16), prob.astype(BF16)), 0.0)
        low = scores.astype(BF16)
        low_ref[h] = low
        rows_ref[h : h + 1, :] = jnp.sum(scores, axis=0, keepdims=True)
        num_ref[:, of_head(h)] = tn(low, v_ref[:, of_head(h // GROUP)])


def weigh_kernel(
    me_ref, got_ref, pq_ref, rows_ref, g_ref, send_ref, gn_ref, rden_ref, norm_ref
):
    me = me_ref[0]
    state = jnp.zeros((ROWS, DH), F32)
    norm = jnp.zeros((PAD, DH), F32)
    for j in range(N_SEQ):
        send_ref[j, :ROWS, :] = state
        state = state + got_ref[j, :ROWS, :]
        norm = norm + jnp.where(j < me, got_ref[j, ROWS:, :], 0.0)
    norm_ref[...] = norm
    columns = norm.T
    rden_ref[...] = rows_ref[...]
    for h in range(H):
        feat = pq_ref[h].astype(BF16).astype(F32)
        rden_ref[h : h + 1, :] += jnp.sum(feat * columns[:, h : h + 1], axis=0, keepdims=True)
    rden_ref[...] = 1.0 / rden_ref[...]
    scale = rden_ref[...].T
    for h in range(H):
        grad = (g_ref[:, of_head(h)].astype(F32) * scale[:, h : h + 1]).astype(BF16)
        gn_ref[:, of_head(h)] = grad
        put_head(send_ref, ROWS, h, nn(pq_ref[h].astype(BF16), grad))


def finish_kernel(
    got_ref, pq_ref, num_ref, rden_ref, g_ref, att_ref, send_ref, gd_ref, low_ref, col_ref
):
    state = jnp.zeros((ROWS, DH), F32)
    for j in reversed(range(N_SEQ)):
        send_ref[j, :ROWS, :] = state
        state = state + got_ref[j, ROWS:, :]
    scale = rden_ref[...].T
    col_ref[...] = jnp.zeros_like(col_ref)
    for h in range(H):
        low = get_head(got_ref, 0, h).astype(BF16)
        low_ref[h] = low
        out = num_ref[:, of_head(h)] + tn(pq_ref[h].astype(BF16), low)
        out = out * scale[:, h : h + 1]
        att_ref[:, of_head(h)] = out.astype(BF16)
        col_ref[:, h : h + 1] = jnp.sum(g_ref[:, of_head(h)].astype(F32) * out, axis=1, keepdims=True)
    grad = -col_ref[...].T[:PAD] * rden_ref[...]
    gd_ref[...] = grad
    top = grad.astype(BF16)
    rest = grad - top.astype(F32)
    middle = rest.astype(BF16)
    bottom = (rest - middle.astype(F32)).astype(BF16)
    split = jnp.concatenate([top, middle, bottom], axis=0)
    send_ref[:, ROWS:, :] = jnp.zeros((N_SEQ, PAD, DH), F32)
    for h in range(H):
        parts = nt(split, pq_ref[h].astype(BF16))
        norm = parts[h : h + 1] + parts[PAD + h : PAD + h + 1] + parts[2 * PAD + h : 2 * PAD + h + 1]
        send_ref[:, ROWS + h : ROWS + h + 1, :] = jnp.broadcast_to(norm[None], (N_SEQ, 1, DH))


def inner_kernel(
    q_ref, v_ref, qm_ref, pq_ref, pk_ref, low_ref, gn_ref, gd_ref, state_ref, norm_ref,
    qg_ref, qw_ref, part_ref, vpart_ref,
):
    mask = causal()
    columns = norm_ref[...].T
    for kv in range(KVH):
        value = v_ref[:, of_head(kv)]
        value_sum = None
        for h in range(kv * GROUP, (kv + 1) * GROUP):
            prob = pq_ref[h]
            grad = gn_ref[:, of_head(h)]
            den = gd_ref[h : h + 1, :]
            dscore = jnp.where(mask, nt(value, grad) + den, 0.0).astype(BF16)
            grad_feat = nn(pk_ref[h].astype(BF16), dscore) + nt(state_ref[h], grad)
            grad_feat = grad_feat + columns[:, h : h + 1] * den
            grad_u = back_through(prob, grad_feat)
            qw_ref[h] = nn(grad_u, q_ref[:, of_head(h)])
            qg_ref[:, of_head(h)] = tn(grad_u, qm_ref[h]).astype(BF16)
            part_ref[h] = nt(prob.astype(BF16), dscore)
            term = nn(low_ref[h], grad)
            value_sum = term if value_sum is None else value_sum + term
        vpart_ref[:, of_head(kv)] = value_sum


def outer_kernel(
    me_ref, core_ref, got_ref, part_ref, pk_ref, k_ref, v_ref, qw_ref,
    keep_ref, give_ref, gu_ref, low_ref,
):
    me = me_ref[0]
    first = core_ref[0] == 0
    norm = jnp.zeros((PAD, DH), F32)
    for j in range(N_SEQ):
        norm = norm + jnp.where(j > me, got_ref[j, ROWS:, :], 0.0)
    columns = norm.T
    for h in range(H):
        kv = of_head(h // GROUP)
        low = get_head(got_ref, 0, h).astype(BF16)
        low_ref[h] = low
        grad_feat = part_ref[h] + nt(low, v_ref[:, kv]) + columns[:, h : h + 1]
        grad_u = back_through(pk_ref[h], grad_feat)
        gu_ref[h] = grad_u
        key_weight = nn(grad_u, k_ref[:, kv])
        query_weight = qw_ref[h]
        keep_ref[h] = jnp.where(first, query_weight, key_weight)
        give_ref[h] = jnp.where(first, key_weight, query_weight)


def last_kernel(km_ref, pk_ref, gu_ref, low_ref, vpart_ref, kg_ref, vg_ref):
    for kv in range(KVH):
        value_sum = vpart_ref[:, of_head(kv)]
        key_sum = None
        for h in range(kv * GROUP, (kv + 1) * GROUP):
            value_sum = value_sum + tn(pk_ref[h].astype(BF16), low_ref[h])
            term = tn(gu_ref[h], km_ref[h])
            key_sum = term if key_sum is None else key_sum + term
        vg_ref[:, of_head(kv)] = value_sum.astype(BF16)
        kg_ref[:, of_head(kv)] = key_sum.astype(BF16)


def run(kernel, outs, scalars, *arrays, scratch=(), macs=0):
    vmem = pl.BlockSpec(memory_space=pltpu.VMEM)
    smem = pl.BlockSpec(memory_space=pltpu.SMEM)
    moved = sum(a.size * a.dtype.itemsize for a in arrays)
    return pl.pallas_call(
        kernel,
        out_shape=tuple(jax.ShapeDtypeStruct(shape, dtype) for shape, dtype in outs),
        in_specs=[smem] * len(scalars) + [vmem] * len(arrays),
        out_specs=tuple(vmem for _ in outs),
        scratch_shapes=list(scratch),
        cost_estimate=pl.CostEstimate(
            flops=2 * macs * H * DH**3, bytes_accessed=2 * moved, transcendentals=0
        ),
        compiler_params=pltpu.CompilerParams(vmem_limit_bytes=32 * 1024 * 1024),
    )(*scalars, *arrays)


def exchange(blocks, axes):
    return lax.all_to_all(blocks, axes, 0, 0, tiled=True)


def spread(rows, count):
    return jnp.broadcast_to(rows[None], (count,) + rows.shape)


def shards(queries, key_rows, value_rows, out_grad, query_map, key_map):
    q, k, v, g = queries[0], key_rows[0], value_rows[0], out_grad[0]
    qm, km = jnp.swapaxes(query_map, 1, 2), jnp.swapaxes(key_map, 1, 2)
    me = lax.axis_index(SEQ).astype(jnp.int32).reshape(1)
    core = lax.axis_index("core").astype(jnp.int32).reshape(1)
    square = (H, DH, DH)
    wide = (TOK, H * DH)
    narrow = (TOK, KVH * DH)
    half = (H, FH, DH)
    small = (PAD, DH)
    short = (N_SEQ, ROWS + PAD, DH)

    send, pk = run(
        key_kernel, [(short, F32), (square, F32)], (), k, v, km,
        scratch=[pltpu.VMEM(small, F32)], macs=2,
    )
    first = exchange(send, SEQ)
    pq, low, rows, num = run(
        query_kernel, [(square, F32), (square, BF16), (small, F32), (wide, F32)], (), q, v, qm, pk, macs=3
    )
    send, gn, rden, norm = run(
        weigh_kernel,
        [((N_SEQ, 2 * ROWS, DH), F32), (wide, BF16), (small, F32), (small, F32)],
        (me,), first, pq, rows, g, macs=1,
    )
    second = exchange(send, SEQ)
    attended, send, gd, state = run(
        finish_kernel,
        [(wide, BF16), (short, F32), (small, F32), (square, BF16)],
        (), second, pq, num, rden, g, scratch=[pltpu.VMEM((TOK, DH), F32)], macs=1,
    )
    third = exchange(send, SEQ)
    query_grad, query_weight, part, value_part = run(
        inner_kernel,
        [(wide, BF16), (half, F32), (square, F32), (narrow, F32)],
        (), q, v, qm, pq, pk, low, gn, gd, state, norm, macs=7,
    )
    keep, give, grad_u, back = run(
        outer_kernel,
        [(half, F32), (half, F32), (half, BF16), (square, BF16)],
        (me, core), third, part, pk, k, v, query_weight, macs=2,
    )
    swap = [(0, 1), (1, 0)]
    mine = keep + lax.ppermute(give, "core", swap)
    mine = exchange(mine.reshape(16, ROWS, DH), ("y", "x")).sum(0)
    mine = exchange(spread(mine, 8), "z").sum(0)
    mine = exchange(spread(mine, 16), ("y", "x")).reshape(half)
    key_grad, value_grad = run(
        last_kernel, [(narrow, BF16), (narrow, BF16)], (), km, pk, grad_u, back, value_part, macs=2
    )
    other = lax.ppermute(mine, "core", swap)
    query_total = jnp.where(core[0] == 0, mine, other)
    key_total = jnp.where(core[0] == 0, other, mine)
    return (
        attended[None],
        query_grad[None],
        key_grad[None],
        value_grad[None],
        jnp.swapaxes(query_total, 1, 2),
        jnp.swapaxes(key_total, 1, 2),
    )


ROWS_SPLIT = P(("y", "core"), ("x", "z"), None)


def solution(mesh):
    fine_mesh = Mesh(mesh.devices.reshape(4, 2, 4, 8), ("y", "core", "x", "z"))
    placed = (ROWS_SPLIT, ROWS_SPLIT, ROWS_SPLIT, ROWS_SPLIT, P(), P())
    return jax.shard_map(
        shards,
        mesh=fine_mesh,
        in_specs=placed,
        out_specs=placed,
        check_vma=False,
    )
```

time: 814 us -> 183 us (0.22)
  waiting for transfers between devices: 505 us -> 35 us
  other arithmetic: 136 us -> 1.02 us
  starting transfers between devices: 0.12 us -> 30.1 us
  matrix products: 25.4 us -> 0 us
  local copies, waits for them, and re-layouts: 36.3 us -> 16.3 us
  Pallas kernels: 0 us -> 16.7 us
  between operations: 14.2 us -> 0.81 us
    all_gather x2 -> x0, waiting for transfers between devices: 258 us -> none  [entering(): pieces = jax.tree.map(lambda part: lax.all_gather(part, axis), value)]
    psum x1 -> x0, waiting for transfers between devices: 247 us -> none  [shards(): lax.psum((query_weight_grad, key_weight_grad), ('dp', 'seq'))]
    select_n x124 -> x0, other arithmetic: 131 us -> none  [lap(): jnp.where(position < mine, new, old)]
    all_gather x2 -> x0, blocking collectives: 89.4 us -> none  [entering(): pieces = jax.tree.map(lambda part: lax.all_gather(part, axis), value)]
    all_to_all x0 -> x4, blocking collectives: none -> 82.1 us  [exchange(): return lax.all_to_all(blocks, axes, 0, 0, tiled=True)]
    all_to_all x0 -> x2, waiting for transfers between devices: none -> 33.4 us  [exchange(): return lax.all_to_all(blocks, axes, 0, 0, tiled=True)]
    dot_general x20 -> x0, matrix products: 25.4 us -> none  [the longest x18 24.3 us: mix(): return jnp.einsum(form, left, right, preferred_element_type=jnp.float32)]
    all_to_all x0 -> x2, starting transfers between devices: none -> 21 us  [exchange(): return lax.all_to_all(blocks, axes, 0, 0, tiled=True)]
  transfers between devices with their start and end apart: 3 -> 4, of which waited for: 3 -> 4; matrix products, arithmetic and copies ran while one was open for 3% -> 0% of each run, Pallas kernels for 0% -> 5%
where the time goes in v2:
time: 183 us; the launch traced here: 182 us
  blocking collectives  82.1 us (45%)
  waiting for transfers between devices  35 us (19%)
  starting transfers between devices  30.1 us (16%)
  Pallas kernels  16.7 us (9%)
  local copies, waits for them, and re-layouts  16.3 us (9%)
    all_to_all x4, blocking collectives, exchange(): return lax.all_to_all(blocks, axes, 0, 0, tiled=True)  82.1 us
    all_to_all x2, waiting for transfers between devices, exchange(): return lax.all_to_all(blocks, axes, 0, 0, tiled=True)  33.4 us
    all_to_all x2, starting transfers between devices, exchange(): return lax.all_to_all(blocks, axes, 0, 0, tiled=True)  21 us
    pallas_call x7, Pallas kernels, run(): pl.pallas_call(kernel, out_shape=tuple((jax.ShapeDtypeStruct(shape, dtype...  16.7 us
    unnamed x52, local copies, waits for them, and re-layouts  16.2 us
    ppermute x1, starting transfers between devices, shards(): mine = keep + lax.ppermute(give, 'core', swap)  5.01 us
    ppermute x1, starting transfers between devices, shards(): other = lax.ppermute(mine, 'core', swap)  4.14 us
  transfers between devices with their start and end apart: 4, of which 4 were waited for; matrix products, arithmetic and copies ran while one was open for 0% of the time, Pallas kernels for 5%

profile of v2, /device:TPU:1, one launch (start us, length us, event | category | flops | bytes accessed | tf_op | source)
XLA Modules:
  0.0 182.0 jit_solution(14812317235744500091)
XLA Ops:
  0.6 0.0 copy-start
  0.6 0.9 copy-done
  1.5 0.9 copy-done.8
  2.5 0.9 copy-done.14
  3.4 2.2 %shard_map.109 = (f32[32,64,128]{2,1,0:T(8,128)S(1)}, f32[12,128,128]{2,1,0:T(8,128)S(1)}) custom-call(bf16[128,512]{1,0:T(8,128)(2,1)S(1)} %bitcast.30, bf16[128,512]{1,0:T(8,128)(2,1)S(1)} %bitcast.18, bf16[12,64,128]{2,1,0:T(8,128)(2,1)S(1)} %bitcast.26), custom_call_target="tpu_custom_call" | custom-call | flops 100663296 | bytes 917504 | tf_op jit(solution)/shard_map/pallas_call | solution.py:227
  5.6 0.0 copy-start.5
  5.6 1.0 copy-done.5
  6.6 12.0 %all-to-all-start = ((f32[32,64,128]{2,1,0:T(8,128)}), f32[32,64,128]{2,1,0:T(8,128)S(1)}, u32[]{:S(2)}, u32[]{:S(2)}) async-start(f32[32,64,128]{2,1,0:T(8,128)} %copy-done.5), calls=%async_computation | async-start | bytes 2097152 | tf_op jit(solution)/shard_map/all_to_all | solution.py:241
  18.6 0.0 copy-done.1
  18.6 0.0 copy-done.3
  18.6 0.0 copy-start.12
  18.7 0.9 copy-done.12
  19.6 2.6 %shard_map.110 = (f32[12,128,128]{2,1,0:T(8,128)S(1)}, bf16[12,128,128]{2,1,0:T(8,128)(2,1)S(1)}, f32[16,128]{1,0:T(8,128)S(1)}, f32[128,1536]{1,0:T(8,128)S(1)}) custom-call(bf16[128,1536]{1,0:T(8,128)(2,1)S(1)} %bitcast.24, bf16[128,512]{1,0:T(8,128)(2,1)S(1)} %bitcast.19, bf16[12,64,128]{2,1,0:T(8,128)(2,1)S(1)} %bitcast.28, ...), custom_call_target="tpu_custom_call" | custom-call | flops 150994944 | bytes 3014656 | tf_op jit(solution)/shard_map/pallas_call | solution.py:227
  22.2 0.9 copy-done.6
  23.1 0.7 copy-done.18
  23.8 19.4 %all-to-all-done.got_ref = f32[32,64,128]{2,1,0:T(8,128)S(1)} async-done(((f32[32,64,128]{2,1,0:T(8,128)}), f32[32,64,128]{2,1,0:T(8,128)S(1)}, u32[]{:S(2)}, u32[]{:S(2)}) %all-to-all-start) | async-done | bytes 1048608 | tf_op jit(solution)/shard_map/all_to_all | solution.py:241
  43.2 1.0 shard_map.111
  44.3 0.0 copy-start.20
  44.3 0.7 copy-done.20
  45.0 44.4 %all_to_all.30.got_ref = f32[32,96,128]{2,1,0:T(8,128)S(1)} all-to-all(f32[32,96,128]{2,1,0:T(8,128)S(1)} %get-tuple-element.34), channel_id=1, replica_groups=mesh['y'=4,'core'=2,'x'=4,'z'=8] {'x','z'}, dimensions={0} | all-to-all | bytes 3145728 | tf_op jit(solution)/shard_map/all_to_all | solution.py:241
  89.4 2.0 %shard_map.112 = (bf16[128,1536]{1,0:T(8,128)(2,1)}, f32[32,64,128]{2,1,0:T(8,128)S(1)}, f32[16,128]{1,0:T(8,128)S(1)}, bf16[12,128,128]{2,1,0:T(8,128)(2,1)S(1)}) custom-call(f32[32,96,128]{2,1,0:T(8,128)S(1)} %all_to_all.30.got_ref, f32[12,128,128]{2,1,0:T(8,128)S(1)} %get-tuple-element.32.pq_ref, f32[128,1536]{1,0:T(8,128)S(1)} %copy-done.7, ...), custom_call_target="tpu_custom_call" | custom-call | flops 50331648 | bytes 7094272 | tf_op jit(solution)/shard_map/pallas_call | solution.py:227
  91.4 1.0 copy-done.4
  92.4 0.7 copy-done.22
  93.2 9.0 %all-to-all-start.2 = ((f32[32,64,128]{2,1,0:T(8,128)}), f32[32,64,128]{2,1,0:T(8,128)S(1)}, u32[]{:S(2)}, u32[]{:S(2)}) async-start(f32[32,64,128]{2,1,0:T(8,128)} %copy-done.4), calls=%async_computation.2 | async-start | bytes 2097152 | tf_op jit(solution)/shard_map/all_to_all | solution.py:241
  102.2 0.0 copy-start.19
  102.2 1.0 copy-done.19
  103.2 1.0 copy-done.21
  104.2 1.0 copy-done.23
  105.2 5.3 %shard_map.113 = (bf16[128,1536]{1,0:T(8,128)(2,1)}, f32[12,64,128]{2,1,0:T(8,128)S(1)}, f32[12,128,128]{2,1,0:T(8,128)S(1)}, f32[128,512]{1,0:T(8,128)S(1)}) custom-call(bf16[128,1536]{1,0:T(8,128)(2,1)S(1)} %bitcast.25, bf16[128,512]{1,0:T(8,128)(2,1)S(1)} %bitcast.20, bf16[12,64,128]{2,1,0:T(8,128)(2,1)S(1)} %bitcast.29, ...), custom_call_target="tpu_custom_call" | custom-call | flops 352321536 | bytes 6979584 | tf_op jit(solution)/shard_map/pallas_call | solution.py:227
  110.5 0.9 copy-done.10
  111.4 0.7 copy-done.16
  112.2 0.7 copy-done.24
  112.9 14.0 %all-to-all-done.2.got_ref = f32[32,64,128]{2,1,0:T(8,128)S(1)} async-done(((f32[32,64,128]{2,1,0:T(8,128)}), f32[32,64,128]{2,1,0:T(8,128)S(1)}, u32[]{:S(2)}, u32[]{:S(2)}) %all-to-all-start.2) | async-done | bytes 1048608 | tf_op jit(solution)/shard_map/all_to_all | solution.py:241
  126.9 0.0 copy-done.15
  126.9 1.1 copy-done.11
  128.0 1.0 copy-done.17
  129.0 2.3 %shard_map.114 = (f32[12,64,128]{2,1,0:T(8,128)S(1)}, f32[12,64,128]{2,1,0:T(8,128)S(1)}, bf16[12,64,128]{2,1,0:T(8,128)(2,1)S(1)}, bf16[12,128,128]{2,1,0:T(8,128)(2,1)S(1)}) custom-call(s32[1]{0:T(128)} %bitcast.me_ref, s32[1]{0:T(128)} %bitcast.9.core_ref, f32[32,64,128]{2,1,0:T(8,128)S(1)} %all-to-all-done.2.got_ref, f32[12,128,128]{2,1,0:T(8,128)S(1)} %copy-done.11, ...), custom_call_target="tpu_custom_call" | custom-call | flops 100663296 | bytes 6553600 | tf_op jit(solution)/shard_map/pallas_call | solution.py:227
  131.3 5.0 %collective-permute-start = (f32[12,64,128]{2,1,0:T(8,128)S(1)}, f32[12,64,128]{2,1,0:T(8,128)S(1)}, u32[]{:S(2)}, u32[]{:S(2)}) collective-permute-start(f32[12,64,128]{2,1,0:T(8,128)S(1)} %get-tuple-element.53), channel_id=1, source_target_pairs={{0,32},{32,0},{1,33},{33,1},{2,34},{34,2},{3,35},{35,3},{4,36},{36... | collective-permute-start | bytes 1179656 | tf_op jit(solution)/shard_map/ppermute | solution.py:291
  136.4 1.3 collective-permute-done
  137.8 0.0 copy-start.9
  137.8 0.0 copy-start.25
  137.8 14.0 %all_to_all.31 = f32[16,48,128]{2,1,0:T(8,128)S(1)} all-to-all(f32[16,48,128]{2,1,0:T(8,128)S(1)} %bitcast.34), channel_id=1, replica_groups=mesh['y'=4,'core'=2,'x'=4,'z'=8] {'y','x'}, dimensions={0} | all-to-all | bytes 786432 | tf_op jit(solution)/shard_map/all_to_all | solution.py:241
  151.8 12.6 %all_to_all.32 = f32[8,48,128]{2,1,0:T(8,128)S(1)} all-to-all(f32[8,48,128]{2,1,0:T(8,128)S(1)} %broadcast_in_dim.28), channel_id=1, replica_groups=mesh['y'=4,'core'=2,'x'=4,'z'=8] {'z'}, dimensions={0} | all-to-all | bytes 393216 | tf_op jit(solution)/shard_map/all_to_all | solution.py:241
  164.4 11.1 %all_to_all.33 = f32[16,48,128]{2,1,0:T(8,128)S(1)} all-to-all(f32[16,48,128]{2,1,0:T(8,128)S(1)} %broadcast_in_dim.29), channel_id=1, replica_groups=mesh['y'=4,'core'=2,'x'=4,'z'=8] {'y','x'}, dimensions={0} | all-to-all | bytes 786432 | tf_op jit(solution)/shard_map/all_to_all | solution.py:241
  175.6 4.1 %collective-permute-start.1 = (f32[12,64,128]{2,1,0:T(8,128)S(1)}, f32[12,64,128]{2,1,0:T(8,128)S(1)}, u32[]{:S(2)}, u32[]{:S(2)}) collective-permute-start(f32[12,64,128]{2,1,0:T(8,128)S(1)} %bitcast.32), channel_id=1, source_target_pairs={{0,32},{32,0},{1,33},{33,1},{2,34},{34,2},{3,35},{35,3},{4,36},{36... | collective-permute-start | bytes 1179656 | tf_op jit(solution)/shard_map/ppermute | solution.py:298
  179.7 1.1 shard_map.115
  180.8 0.2 collective-permute-done.1
  181.1 0.9 select_bitcast_fusion
  (29 shorter events, 0.2 us)
Async XLA Ops:
  0.6 0.9 copy-start
  1.5 0.9 copy-start.8
  2.5 0.9 copy-start.14
  3.4 15.3 %copy-start.1 = (bf16[1,128,512]{2,1,0:T(8,128)(2,1)S(1)}, bf16[1,128,512]{2,1,0:T(8,128)(2,1)}, u32[]{:S(2)}) copy-start(bf16[1,128,512]{2,1,0:T(8,128)(2,1)} %param.8) | copy-start | bytes 393220
  3.4 15.3 %copy-start.3 = (bf16[1,128,1536]{2,1,0:T(8,128)(2,1)S(1)}, bf16[1,128,1536]{2,1,0:T(8,128)(2,1)}, u32[]{:S(2)}) copy-start(bf16[1,128,1536]{2,1,0:T(8,128)(2,1)} %param.6) | copy-start | bytes 1179652
  5.6 1.0 copy-start.5
  6.6 36.6 %copy-start.2 = (bf16[1,128,1536]{2,1,0:T(8,128)(2,1)S(1)}, bf16[1,128,1536]{2,1,0:T(8,128)(2,1)}, u32[]{:S(2)}) copy-start(bf16[1,128,1536]{2,1,0:T(8,128)(2,1)} %param.9) | copy-start | bytes 1179652
  6.6 36.6 %all-to-all-start = ((f32[32,64,128]{2,1,0:T(8,128)}), f32[32,64,128]{2,1,0:T(8,128)S(1)}, u32[]{:S(2)}, u32[]{:S(2)}) async-start(f32[32,64,128]{2,1,0:T(8,128)} %copy-done.5), calls=%async_computation | async-start | bytes 2097152 | tf_op jit(solution)/shard_map/all_to_all | solution.py:241
  18.6 0.9 copy-start.12
  22.2 0.9 copy-start.6
  23.1 0.7 copy-start.18
  44.3 0.7 copy-start.20
  45.0 44.4 %copy-start.7 = (f32[128,1536]{1,0:T(8,128)S(1)}, f32[128,1536]{1,0:T(8,128)}, u32[]{:S(2)}) copy-start(f32[128,1536]{1,0:T(8,128)} %copy-done.6) | copy-start | bytes 2359300
  91.4 1.0 copy-start.4
  92.4 0.7 copy-start.22
  93.2 9.0 %copy-start.13 = (bf16[12,128,64]{1,2,0:T(8,128)(2,1)S(1)}, bf16[12,128,64]{1,2,0:T(8,128)(2,1)}, u32[]{:S(2)}) copy-start(bf16[12,128,64]{1,2,0:T(8,128)(2,1)} %param.10) | copy-start | bytes 589828
  93.2 33.7 %all-to-all-start.2 = ((f32[32,64,128]{2,1,0:T(8,128)}), f32[32,64,128]{2,1,0:T(8,128)S(1)}, u32[]{:S(2)}, u32[]{:S(2)}) async-start(f32[32,64,128]{2,1,0:T(8,128)} %copy-done.4), calls=%async_computation.2 | async-start | bytes 2097152 | tf_op jit(solution)/shard_map/all_to_all | solution.py:241
  102.2 1.0 copy-start.19
  103.2 1.0 copy-start.21
  104.2 1.0 copy-start.23
  105.2 21.7 %copy-start.15 = (bf16[1,128,512]{2,1,0:T(8,128)(2,1)S(1)}, bf16[1,128,512]{2,1,0:T(8,128)(2,1)}, u32[]{:S(2)}) copy-start(bf16[1,128,512]{2,1,0:T(8,128)(2,1)} %param.7) | copy-start | bytes 393220
  110.5 0.9 copy-start.10
  111.4 0.7 copy-start.16
  112.2 0.7 copy-start.24
  126.9 1.1 copy-start.11
  128.0 1.0 copy-start.17
  131.3 6.4 %collective-permute-start = (f32[12,64,128]{2,1,0:T(8,128)S(1)}, f32[12,64,128]{2,1,0:T(8,128)S(1)}, u32[]{:S(2)}, u32[]{:S(2)}) collective-permute-start(f32[12,64,128]{2,1,0:T(8,128)S(1)} %get-tuple-element.53), channel_id=1, source_target_pairs={{0,32},{32,0},{1,33},{33,1},{2,34},{34,2},{3,35},{35,3},{4,36},{36... | collective-permute-start | bytes 1179656 | tf_op jit(solution)/shard_map/ppermute | solution.py:291
  137.8 42.0 %copy-start.9 = (bf16[12,128,64]{1,2,0:T(8,128)(2,1)S(1)}, bf16[12,128,64]{1,2,0:T(8,128)(2,1)}, u32[]{:S(2)}) copy-start(bf16[12,128,64]{1,2,0:T(8,128)(2,1)} %param.11) | copy-start | bytes 589828
  137.8 41.9 %copy-start.25 = (f32[128,512]{1,0:T(8,128)S(1)}, f32[128,512]{1,0:T(8,128)}, u32[]{:S(2)}) copy-start(f32[128,512]{1,0:T(8,128)} %copy-done.24) | copy-start | bytes 786436
  175.6 5.5 %collective-permute-start.1 = (f32[12,64,128]{2,1,0:T(8,128)S(1)}, f32[12,64,128]{2,1,0:T(8,128)S(1)}, u32[]{:S(2)}, u32[]{:S(2)}) collective-permute-start(f32[12,64,128]{2,1,0:T(8,128)S(1)} %bitcast.32), channel_id=1, source_target_pairs={{0,32},{32,0},{1,33},{33,1},{2,34},{34,2},{3,35},{35,3},{4,36},{36... | collective-permute-start | bytes 1179656 | tf_op jit(solution)/shard_map/ppermute | solution.py:298

commit v3 on v2

--- a/solution.py
+++ b/solution.py
@@ -11,10 +11,12 @@
 DH = 128
 FH = 64
 TOK = 128
-N_SEQ = 32
-ROWS = H * DH // N_SEQ
+NX = 4
+NZ = 8
+ROWS = H * DH // NZ
 PAD = 16
-SEQ = ("x", "z")
+RING = (0, 1, 3, 5, 7, 6, 4, 2)
+SLOT = [RING.index(place) for place in range(NZ)]
 F32 = jnp.float32
 BF16 = jnp.bfloat16
 
@@ -46,12 +48,12 @@
 
 def put_head(ref, base, h, rows):
     for block, first, count, start in pieces(h):
-        ref[block, base + first : base + first + count, :] = rows[start : start + count]
+        ref[SLOT[block], base + first : base + first + count, :] = rows[start : start + count]
 
 
 def get_head(ref, base, h):
     parts = [
-        ref[block, base + first : base + first + count, :]
+        ref[SLOT[block], base + first : base + first + count, :]
         for block, first, count, start in pieces(h)
     ]
     return jnp.concatenate(parts, axis=0)
@@ -90,7 +92,7 @@
         feat = prob.astype(BF16)
         put_head(send_ref, 0, h, nn(feat, v_ref[:, kv]))
         norm_ref[h : h + 1, :] = nt(ones, feat)[0:1]
-    send_ref[:, ROWS:, :] = jnp.broadcast_to(norm_ref[...][None], (N_SEQ, PAD, DH))
+    send_ref[:, ROWS:, :] = jnp.broadcast_to(norm_ref[...][None], (NZ, PAD, DH))
 
 
 def query_kernel(q_ref, v_ref, qm_ref, pk_ref, pq_ref, low_ref, rows_ref, num_ref):
@@ -106,16 +108,37 @@
         num_ref[:, of_head(h)] = tn(low, v_ref[:, of_head(h // GROUP)])
 
 
+def total_kernel(got_ref, out_ref):
+    total = got_ref[0]
+    for j in range(1, NZ):
+        total = total + got_ref[j]
+    out_ref[...] = total
+
+
+def from_rows(x, one_ref, two_ref, three_ref, rows, earlier):
+    total = jnp.zeros((rows.stop - rows.start, DH), F32)
+    for step, ref in ((1, one_ref), (2, two_ref), (3, three_ref)):
+        wanted = x >= step if earlier else x < step
+        total = total + jnp.where(wanted, ref[rows, :], 0.0)
+    return total
+
+
+STATE = slice(0, ROWS)
+NORM = slice(ROWS, ROWS + PAD)
+
+
 def weigh_kernel(
-    me_ref, got_ref, pq_ref, rows_ref, g_ref, send_ref, gn_ref, rden_ref, norm_ref
+    x_ref, z_ref, got_ref, one_ref, two_ref, three_ref, pq_ref, rows_ref, g_ref,
+    send_ref, gn_ref, rden_ref, norm_ref,
 ):
-    me = me_ref[0]
-    state = jnp.zeros((ROWS, DH), F32)
-    norm = jnp.zeros((PAD, DH), F32)
-    for j in range(N_SEQ):
-        send_ref[j, :ROWS, :] = state
-        state = state + got_ref[j, :ROWS, :]
-        norm = norm + jnp.where(j < me, got_ref[j, ROWS:, :], 0.0)
+    x, z = x_ref[0], z_ref[0]
+    state = from_rows(x, one_ref, two_ref, three_ref, STATE, True)
+    norm = from_rows(x, one_ref, two_ref, three_ref, NORM, True)
+    for j in range(NZ):
+        send_ref[SLOT[j], STATE, :] = state
+        if j < NZ - 1:
+            state = state + got_ref[SLOT[j], STATE, :]
+            norm = norm + jnp.where(j < z, got_ref[SLOT[j], NORM, :], 0.0)
     norm_ref[...] = norm
     columns = norm.T
     rden_ref[...] = rows_ref[...]
@@ -131,12 +154,12 @@
 
 
 def finish_kernel(
-    got_ref, pq_ref, num_ref, rden_ref, g_ref, att_ref, send_ref, gd_ref, low_ref, col_ref
+    got_ref, pq_ref, num_ref, rden_ref, g_ref, att_ref, sum_ref, gd_ref, low_ref, col_ref
 ):
-    state = jnp.zeros((ROWS, DH), F32)
-    for j in reversed(range(N_SEQ)):
-        send_ref[j, :ROWS, :] = state
-        state = state + got_ref[j, ROWS:, :]
+    total = got_ref[0, ROWS:, :]
+    for j in range(1, NZ):
+        total = total + got_ref[j, ROWS:, :]
+    sum_ref[STATE, :] = total
     scale = rden_ref[...].T
     col_ref[...] = jnp.zeros_like(col_ref)
     for h in range(H):
@@ -153,11 +176,23 @@
     middle = rest.astype(BF16)
     bottom = (rest - middle.astype(F32)).astype(BF16)
     split = jnp.concatenate([top, middle, bottom], axis=0)
-    send_ref[:, ROWS:, :] = jnp.zeros((N_SEQ, PAD, DH), F32)
+    sum_ref[NORM, :] = jnp.zeros((PAD, DH), F32)
     for h in range(H):
         parts = nt(split, pq_ref[h].astype(BF16))
         norm = parts[h : h + 1] + parts[PAD + h : PAD + h + 1] + parts[2 * PAD + h : 2 * PAD + h + 1]
-        send_ref[:, ROWS + h : ROWS + h + 1, :] = jnp.broadcast_to(norm[None], (N_SEQ, 1, DH))
+        sum_ref[ROWS + h : ROWS + h + 1, :] = norm
+
+
+def suffix_kernel(x_ref, z_ref, got_ref, own_ref, one_ref, two_ref, three_ref, send_ref):
+    x, z = x_ref[0], z_ref[0]
+    state = from_rows(x, one_ref, two_ref, three_ref, STATE, False)
+    norm = from_rows(x, one_ref, two_ref, three_ref, NORM, False)
+    both = norm + own_ref[NORM, :]
+    for j in reversed(range(NZ)):
+        send_ref[SLOT[j], STATE, :] = state
+        send_ref[SLOT[j], NORM, :] = jnp.where(z > j, both, norm)
+        if j > 0:
+            state = state + got_ref[SLOT[j], ROWS:, :]
 
 
 def inner_kernel(
@@ -186,14 +221,13 @@
 
 
 def outer_kernel(
-    me_ref, core_ref, got_ref, part_ref, pk_ref, k_ref, v_ref, qw_ref,
+    core_ref, got_ref, part_ref, pk_ref, k_ref, v_ref, qw_ref,
     keep_ref, give_ref, gu_ref, low_ref,
 ):
-    me = me_ref[0]
     first = core_ref[0] == 0
-    norm = jnp.zeros((PAD, DH), F32)
-    for j in range(N_SEQ):
-        norm = norm + jnp.where(j > me, got_ref[j, ROWS:, :], 0.0)
+    norm = got_ref[0, NORM, :]
+    for j in range(1, NZ):
+        norm = norm + got_ref[j, NORM, :]
     columns = norm.T
     for h in range(H):
         kv = of_head(h // GROUP)
@@ -241,6 +275,14 @@
     return lax.all_to_all(blocks, axes, 0, 0, tiled=True)
 
 
+def turn(rows):
+    return [lax.ppermute(rows, "x", [(i, (i + step) % NX) for i in range(NX)]) for step in (1, 2, 3)]
+
+
+def exchange_z(blocks):
+    return lax.all_to_all(blocks, "z", 0, 0, axis_index_groups=[list(RING)], tiled=True)
+
+
 def spread(rows, count):
     return jnp.broadcast_to(rows[None], (count,) + rows.shape)
 
@@ -248,35 +290,39 @@
 def shards(queries, key_rows, value_rows, out_grad, query_map, key_map):
     q, k, v, g = queries[0], key_rows[0], value_rows[0], out_grad[0]
     qm, km = jnp.swapaxes(query_map, 1, 2), jnp.swapaxes(key_map, 1, 2)
-    me = lax.axis_index(SEQ).astype(jnp.int32).reshape(1)
-    core = lax.axis_index("core").astype(jnp.int32).reshape(1)
+    x, z, core = (lax.axis_index(a).astype(jnp.int32).reshape(1) for a in ("x", "z", "core"))
     square = (H, DH, DH)
     wide = (TOK, H * DH)
     narrow = (TOK, KVH * DH)
     half = (H, FH, DH)
     small = (PAD, DH)
-    short = (N_SEQ, ROWS + PAD, DH)
+    flat = (ROWS + PAD, DH)
+    short = (NZ,) + flat
 
     send, pk = run(
         key_kernel, [(short, F32), (square, F32)], (), k, v, km,
         scratch=[pltpu.VMEM(small, F32)], macs=2,
     )
-    first = exchange(send, SEQ)
+    first = exchange_z(send)
+    (total,) = run(total_kernel, [(flat, F32)], (), first)
+    others = turn(total)
     pq, low, rows, num = run(
         query_kernel, [(square, F32), (square, BF16), (small, F32), (wide, F32)], (), q, v, qm, pk, macs=3
     )
     send, gn, rden, norm = run(
         weigh_kernel,
-        [((N_SEQ, 2 * ROWS, DH), F32), (wide, BF16), (small, F32), (small, F32)],
-        (me,), first, pq, rows, g, macs=1,
-    )
-    second = exchange(send, SEQ)
-    attended, send, gd, state = run(
+        [((NZ, 2 * ROWS, DH), F32), (wide, BF16), (small, F32), (small, F32)],
+        (x, z), first, *others, pq, rows, g, macs=1,
+    )
+    second = exchange_z(send)
+    attended, total, gd, state = run(
         finish_kernel,
-        [(wide, BF16), (short, F32), (small, F32), (square, BF16)],
+        [(wide, BF16), (flat, F32), (small, F32), (square, BF16)],
         (), second, pq, num, rden, g, scratch=[pltpu.VMEM((TOK, DH), F32)], macs=1,
     )
-    third = exchange(send, SEQ)
+    others = turn(total)
+    (send,) = run(suffix_kernel, [(short, F32)], (x, z), second, total, *others)
+    third = exchange_z(send)
     query_grad, query_weight, part, value_part = run(
         inner_kernel,
         [(wide, BF16), (half, F32), (square, F32), (narrow, F32)],
@@ -285,12 +331,12 @@
     keep, give, grad_u, back = run(
         outer_kernel,
         [(half, F32), (half, F32), (half, BF16), (square, BF16)],
-        (me, core), third, part, pk, k, v, query_weight, macs=2,
+        (core,), third, part, pk, k, v, query_weight, macs=2,
     )
     swap = [(0, 1), (1, 0)]
     mine = keep + lax.ppermute(give, "core", swap)
-    mine = exchange(mine.reshape(16, ROWS, DH), ("y", "x")).sum(0)
-    mine = exchange(spread(mine, 8), "z").sum(0)
+    mine = exchange(mine.reshape(16, -1, DH), ("y", "x")).sum(0)
+    mine = exchange_z(spread(mine, 8)).sum(0)
     mine = exchange(spread(mine, 16), ("y", "x")).reshape(half)
     key_grad, value_grad = run(
         last_kernel, [(narrow, BF16), (narrow, BF16)], (), km, pk, grad_u, back, value_part, macs=2

time: 183 us -> 177 us (0.967)
  blocking collectives: 82.1 us -> 108 us
  waiting for transfers between devices: 35 us -> 16.5 us
  starting transfers between devices: 30.1 us -> 21 us
  local copies, waits for them, and re-layouts: 16.3 us -> 10.3 us
  Pallas kernels: 16.7 us -> 19.3 us
    all_to_all x0 -> x3, blocking collectives: none -> 81.5 us  [exchange_z(): lax.all_to_all(blocks, 'z', 0, 0, axis_index_groups=[list(RING)], tiled=T...]
    all_to_all x4 -> x2, blocking collectives: 82.1 us -> 26.3 us  [exchange(): return lax.all_to_all(blocks, axes, 0, 0, tiled=True)]
    all_to_all x2 -> x1, waiting for transfers between devices: 33.4 us -> 11 us  [exchange_z(): lax.all_to_all(blocks, 'z', 0, 0, axis_index_groups=[list(RING)], tiled=T...]
    all_to_all x2 -> x1, starting transfers between devices: 21 us -> 4.97 us  [exchange_z(): lax.all_to_all(blocks, 'z', 0, 0, axis_index_groups=[list(RING)], tiled=T...]
    ppermute x0 -> x6, starting transfers between devices: none -> 8.27 us  [turn(): lax.ppermute(rows, 'x', [(i, (i + step) % NX) for i in range(NX)])]
    unnamed x52 -> x38, local copies, waits for them, and re-layouts: 16.2 us -> 10.3 us
    ppermute x0 -> x6, waiting for transfers between devices: none -> 3.9 us  [turn(): lax.ppermute(rows, 'x', [(i, (i + step) % NX) for i in range(NX)])]
    pallas_call x7 -> x9, Pallas kernels: 16.7 us -> 19.3 us  [run(): pl.pallas_call(kernel, out_shape=tuple((jax.ShapeDtypeStruct(shape, dtype...]
  transfers between devices with their start and end apart: 4 -> 9, of which waited for: 4 -> 7; matrix products, arithmetic and copies ran while one was open for 0% -> 0% of each run, Pallas kernels for 5% -> 5%
where the time goes in v3:
time: 177 us
  blocking collectives  108 us (61%)
  starting transfers between devices  21 us (12%)
  Pallas kernels  19.3 us (11%)
  waiting for transfers between devices  16.5 us (9%)
  local copies, waits for them, and re-layouts  10.3 us (6%)
    all_to_all x3, blocking collectives, exchange_z(): lax.all_to_all(blocks, 'z', 0, 0, axis_index_groups=[list(RING)], tiled=T...  81.5 us
    all_to_all x2, blocking collectives, exchange(): return lax.all_to_all(blocks, axes, 0, 0, tiled=True)  26.3 us
    pallas_call x9, Pallas kernels, run(): pl.pallas_call(kernel, out_shape=tuple((jax.ShapeDtypeStruct(shape, dtype...  19.3 us
    all_to_all x1, waiting for transfers between devices, exchange_z(): lax.all_to_all(blocks, 'z', 0, 0, axis_index_groups=[list(RING)], tiled=T...  11 us
    unnamed x38, local copies, waits for them, and re-layouts  10.3 us
    ppermute x6, starting transfers between devices, turn(): lax.ppermute(rows, 'x', [(i, (i + step) % NX) for i in range(NX)])  8.27 us
    all_to_all x1, starting transfers between devices, exchange_z(): lax.all_to_all(blocks, 'z', 0, 0, axis_index_groups=[list(RING)], tiled=T...  4.97 us
    ppermute x1, starting transfers between devices, shards(): other = lax.ppermute(mine, 'core', swap)  4.65 us
  transfers between devices with their start and end apart: 9, of which 7 were waited for; matrix products, arithmetic and copies ran while one was open for 0% of the time, Pallas kernels for 5%

profile of v3, /device:TPU:1, one launch (start us, length us, event | category | flops | bytes accessed | tf_op | source)
XLA Modules:
  0.0 176.7 jit_solution(16694496911938853606)
XLA Ops:
  0.6 0.9 copy-done
  1.5 0.9 copy-done.4
  2.5 0.9 copy-done.9
  3.4 2.2 %shard_map.109 = (f32[8,208,128]{2,1,0:T(8,128)S(1)}, f32[12,128,128]{2,1,0:T(8,128)S(1)}) custom-call(bf16[128,512]{1,0:T(8,128)(2,1)S(1)} %bitcast.31, bf16[128,512]{1,0:T(8,128)(2,1)S(1)} %bitcast.19, bf16[12,64,128]{2,1,0:T(8,128)(2,1)S(1)} %bitcast.27), custom_call_target="tpu_custom_call" | custom-call | flops 100663296 | bytes 917504 | tf_op jit(solution)/shard_map/pallas_call | solution.py:261
  5.6 31.5 %all_to_all.30.got_ref = f32[8,208,128]{2,1,0:T(8,128)S(1)} all-to-all(f32[8,208,128]{2,1,0:T(8,128)S(1)} %get-tuple-element.30), channel_id=1, replica_groups={{0,1,3,5,7,6,4,2},{8,9,11,13,15,14,12,10},{16,17,19,21,23,22,20,18},{24..., dimensions={0} | all-to-all | bytes 1703936 | tf_op jit(solution)/shard_map/all_to_all | solution.py:283
  37.1 0.7 shard_map.110
  37.8 1.2 collective-permute-start
  39.0 2.4 %collective-permute-start.1 = (f32[208,128]{1,0:T(8,128)}, f32[208,128]{1,0:T(8,128)}, u32[]{:S(2)}, u32[]{:S(2)}) collective-permute-start(f32[208,128]{1,0:T(8,128)} %shard_map.110), channel_id=1, source_target_pairs={{0,16},{8,24},{16,0},{24,8},{1,17},{9,25},{17,1},{25,9},{2,18},{10... | collective-permute-start | bytes 319496 | tf_op jit(solution)/shard_map/ppermute | solution.py:279
  41.5 1.2 collective-permute-start.2
  42.6 0.0 copy-done.3
  42.6 2.6 %shard_map.111 = (f32[12,128,128]{2,1,0:T(8,128)S(1)}, bf16[12,128,128]{2,1,0:T(8,128)(2,1)S(1)}, f32[16,128]{1,0:T(8,128)S(1)}, f32[128,1536]{1,0:T(8,128)S(1)}) custom-call(bf16[128,1536]{1,0:T(8,128)(2,1)S(1)} %bitcast.25, bf16[128,512]{1,0:T(8,128)(2,1)S(1)} %bitcast.20, bf16[12,64,128]{2,1,0:T(8,128)(2,1)S(1)} %bitcast.29, ...), custom_call_target="tpu_custom_call" | custom-call | flops 150994944 | bytes 3014656 | tf_op jit(solution)/shard_map/pallas_call | solution.py:261
  45.2 0.0 copy-start.13
  45.3 0.0 collective-permute-done.one_ref
  45.3 0.0 collective-permute-done.1.two_ref
  45.3 0.3 collective-permute-done.2.three_ref
  45.6 2.0 %shard_map.112 = (f32[8,384,128]{2,1,0:T(8,128)S(1)}, bf16[128,1536]{1,0:T(8,128)(2,1)S(1)}, f32[16,128]{1,0:T(8,128)S(1)}, f32[16,128]{1,0:T(8,128)S(1)}) custom-call(s32[1]{0:T(128)} %bitcast.x_ref, s32[1]{0:T(128)} %bitcast.1.z_ref, f32[8,208,128]{2,1,0:T(8,128)S(1)} %all_to_all.30.got_ref, f32[208,128]{1,0:T(8,128)} %collective-permute-done.one_ref, ...), custom_call_target="tpu_custom_call" | custom-call | flops 50331648 | bytes 4718592 | tf_op jit(solution)/shard_map/pallas_call | solution.py:261
  47.7 39.3 %all_to_all.31.got_ref = f32[8,384,128]{2,1,0:T(8,128)S(1)} all-to-all(f32[8,384,128]{2,1,0:T(8,128)S(1)} %get-tuple-element.34), channel_id=1, replica_groups={{0,1,3,5,7,6,4,2},{8,9,11,13,15,14,12,10},{16,17,19,21,23,22,20,18},{24..., dimensions={0} | all-to-all | bytes 3145728 | tf_op jit(solution)/shard_map/all_to_all | solution.py:283
  86.9 2.1 %shard_map.113 = (bf16[128,1536]{1,0:T(8,128)(2,1)}, f32[208,128]{1,0:T(8,128)S(1)}, f32[16,128]{1,0:T(8,128)S(1)}, bf16[12,128,128]{2,1,0:T(8,128)(2,1)S(1)}) custom-call(f32[8,384,128]{2,1,0:T(8,128)S(1)} %all_to_all.31.got_ref, f32[12,128,128]{2,1,0:T(8,128)S(1)} %get-tuple-element.32.pq_ref, f32[128,1536]{1,0:T(8,128)S(1)} %get-tuple-element.35.num_ref, ...), custom_call_target="tpu_custom_call" | custom-call | flops 50331648 | bytes 7094272 | tf_op jit(solution)/shard_map/pallas_call | solution.py:261
  89.0 0.7 copy-done.17
  89.7 0.0 collective-permute-start.3
  89.7 3.5 %collective-permute-start.4 = (f32[208,128]{1,0:T(8,128)S(1)}, f32[208,128]{1,0:T(8,128)S(1)}, u32[]{:S(2)}, u32[]{:S(2)}) collective-permute-start(f32[208,128]{1,0:T(8,128)S(1)} %get-tuple-element.44.own_ref), channel_id=1, source_target_pairs={{0,16},{8,24},{16,0},{24,8},{1,17},{9,25},{17,1},{25,9},{2,18},{10... | collective-permute-start | bytes 319496 | tf_op jit(solution)/shard_map/ppermute | solution.py:279
  93.2 0.0 collective-permute-start.5
  93.2 1.3 collective-permute-done.3.one_ref
  94.5 1.9 %collective-permute-done.4.two_ref = f32[208,128]{1,0:T(8,128)S(1)} collective-permute-done((f32[208,128]{1,0:T(8,128)S(1)}, f32[208,128]{1,0:T(8,128)S(1)}, u32[]{:S(2)}, u32[]{:S(2)}) %collective-permute-start.4) | collective-permute-done | bytes 106528 | tf_op jit(solution)/shard_map/ppermute | solution.py:279
  96.4 0.3 collective-permute-done.5.three_ref
  96.8 1.0 shard_map.115
  97.7 5.0 %all-to-all-start.2 = ((f32[8,208,128]{2,1,0:T(8,128)}), f32[8,208,128]{2,1,0:T(8,128)S(1)}, u32[]{:S(2)}, u32[]{:S(2)}) async-start(f32[8,208,128]{2,1,0:T(8,128)} %shard_map.115), calls=%async_computation.2 | async-start | bytes 1703936 | tf_op jit(solution)/shard_map/all_to_all | solution.py:283
  102.7 1.0 copy-done.14
  103.7 1.0 copy-done.16
  104.7 1.0 copy-done.18
  105.7 5.3 %shard_map.114 = (bf16[128,1536]{1,0:T(8,128)(2,1)}, f32[12,64,128]{2,1,0:T(8,128)S(1)}, f32[12,128,128]{2,1,0:T(8,128)S(1)}, f32[128,512]{1,0:T(8,128)S(1)}) custom-call(bf16[128,1536]{1,0:T(8,128)(2,1)S(1)} %bitcast.26, bf16[128,512]{1,0:T(8,128)(2,1)S(1)} %bitcast.21, bf16[12,64,128]{2,1,0:T(8,128)(2,1)S(1)} %bitcast.30, ...), custom_call_target="tpu_custom_call" | custom-call | flops 352321536 | bytes 6979584 | tf_op jit(solution)/shard_map/pallas_call | solution.py:261
  111.0 0.9 copy-done.6
  111.9 0.7 copy-done.11
  112.7 11.0 %all-to-all-done.2.got_ref = f32[8,208,128]{2,1,0:T(8,128)S(1)} async-done(((f32[8,208,128]{2,1,0:T(8,128)}), f32[8,208,128]{2,1,0:T(8,128)S(1)}, u32[]{:S(2)}, u32[]{:S(2)}) %all-to-all-start.2) | async-done | bytes 852000 | tf_op jit(solution)/shard_map/all_to_all | solution.py:283
  123.7 1.1 copy-done.7
  124.8 1.0 copy-done.12
  125.8 2.3 %shard_map.116 = (f32[12,64,128]{2,1,0:T(8,128)S(1)}, f32[12,64,128]{2,1,0:T(8,128)S(1)}, bf16[12,64,128]{2,1,0:T(8,128)(2,1)S(1)}, bf16[12,128,128]{2,1,0:T(8,128)(2,1)S(1)}) custom-call(s32[1]{0:T(128)} %bitcast.10.core_ref, f32[8,208,128]{2,1,0:T(8,128)S(1)} %all-to-all-done.2.got_ref, f32[12,128,128]{2,1,0:T(8,128)S(1)} %copy-done.7, ...), custom_call_target="tpu_custom_call" | custom-call | flops 100663296 | bytes 6160384 | tf_op jit(solution)/shard_map/pallas_call | solution.py:261
  128.1 3.1 %collective-permute-start.6 = (f32[12,64,128]{2,1,0:T(8,128)S(1)}, f32[12,64,128]{2,1,0:T(8,128)S(1)}, u32[]{:S(2)}, u32[]{:S(2)}) collective-permute-start(f32[12,64,128]{2,1,0:T(8,128)S(1)} %get-tuple-element.53), channel_id=1, source_target_pairs={{0,32},{32,0},{1,33},{33,1},{2,34},{34,2},{3,35},{35,3},{4,36},{36... | collective-permute-start | bytes 1179656 | tf_op jit(solution)/shard_map/ppermute | solution.py:337
  131.2 1.3 collective-permute-done.6
  132.5 0.1 add.3
  132.6 0.0 copy-start.5
  132.6 15.1 %all_to_all.32 = f32[16,48,128]{2,1,0:T(8,128)S(1)} all-to-all(f32[16,48,128]{2,1,0:T(8,128)S(1)} %bitcast.35), channel_id=1, replica_groups=mesh['y'=4,'core'=2,'x'=4,'z'=8] {'y','x'}, dimensions={0} | all-to-all | bytes 786432 | tf_op jit(solution)/shard_map/all_to_all | solution.py:275
  147.7 10.7 %all_to_all.33 = f32[8,48,128]{2,1,0:T(8,128)S(1)} all-to-all(f32[8,48,128]{2,1,0:T(8,128)S(1)} %broadcast_in_dim.28), channel_id=1, replica_groups={{0,1,3,5,7,6,4,2},{8,9,11,13,15,14,12,10},{16,17,19,21,23,22,20,18},{24..., dimensions={0} | all-to-all | bytes 393216 | tf_op jit(solution)/shard_map/all_to_all | solution.py:283
  158.5 11.2 %all_to_all.34 = f32[16,48,128]{2,1,0:T(8,128)S(1)} all-to-all(f32[16,48,128]{2,1,0:T(8,128)S(1)} %broadcast_in_dim.29), channel_id=1, replica_groups=mesh['y'=4,'core'=2,'x'=4,'z'=8] {'y','x'}, dimensions={0} | all-to-all | bytes 786432 | tf_op jit(solution)/shard_map/all_to_all | solution.py:275
  169.7 4.6 %collective-permute-start.7 = (f32[12,64,128]{2,1,0:T(8,128)S(1)}, f32[12,64,128]{2,1,0:T(8,128)S(1)}, u32[]{:S(2)}, u32[]{:S(2)}) collective-permute-start(f32[12,64,128]{2,1,0:T(8,128)S(1)} %bitcast.33), channel_id=1, source_target_pairs={{0,32},{32,0},{1,33},{33,1},{2,34},{34,2},{3,35},{35,3},{4,36},{36... | collective-permute-start | bytes 1179656 | tf_op jit(solution)/shard_map/ppermute | solution.py:344
  174.4 1.1 shard_map.117
  175.5 0.2 collective-permute-done.7
  175.7 0.9 select_bitcast_fusion
  (28 shorter events, 0.1 us)
Async XLA Ops:
  0.6 0.9 copy-start
  1.5 0.9 copy-start.4
  2.5 0.9 copy-start.9
  3.4 39.2 %copy-start.1 = (bf16[1,128,512]{2,1,0:T(8,128)(2,1)S(1)}, bf16[1,128,512]{2,1,0:T(8,128)(2,1)}, u32[]{:S(2)}) copy-start(bf16[1,128,512]{2,1,0:T(8,128)(2,1)} %param.8) | copy-start | bytes 393220
  3.4 39.2 %copy-start.3 = (bf16[1,128,1536]{2,1,0:T(8,128)(2,1)S(1)}, bf16[1,128,1536]{2,1,0:T(8,128)(2,1)}, u32[]{:S(2)}) copy-start(bf16[1,128,1536]{2,1,0:T(8,128)(2,1)} %param.6) | copy-start | bytes 1179652
  3.4 39.2 %copy-start.8 = (bf16[12,128,64]{1,2,0:T(8,128)(2,1)S(1)}, bf16[12,128,64]{1,2,0:T(8,128)(2,1)}, u32[]{:S(2)}) copy-start(bf16[12,128,64]{1,2,0:T(8,128)(2,1)} %param.10) | copy-start | bytes 589828
  37.1 8.5 %copy-start.2 = (bf16[1,128,1536]{2,1,0:T(8,128)(2,1)S(1)}, bf16[1,128,1536]{2,1,0:T(8,128)(2,1)}, u32[]{:S(2)}) copy-start(bf16[1,128,1536]{2,1,0:T(8,128)(2,1)} %param.9) | copy-start | bytes 1179652
  37.8 7.5 %collective-permute-start = (f32[208,128]{1,0:T(8,128)}, f32[208,128]{1,0:T(8,128)}, u32[]{:S(2)}, u32[]{:S(2)}) collective-permute-start(f32[208,128]{1,0:T(8,128)} %shard_map.110), channel_id=1, source_target_pairs={{0,8},{8,16},{16,24},{24,0},{1,9},{9,17},{17,25},{25,1},{2,10},{10... | collective-permute-start | bytes 319496 | tf_op jit(solution)/shard_map/ppermute | solution.py:279
  39.0 6.3 %collective-permute-start.1 = (f32[208,128]{1,0:T(8,128)}, f32[208,128]{1,0:T(8,128)}, u32[]{:S(2)}, u32[]{:S(2)}) collective-permute-start(f32[208,128]{1,0:T(8,128)} %shard_map.110), channel_id=1, source_target_pairs={{0,16},{8,24},{16,0},{24,8},{1,17},{9,25},{17,1},{25,9},{2,18},{10... | collective-permute-start | bytes 319496 | tf_op jit(solution)/shard_map/ppermute | solution.py:279
  41.5 4.2 %collective-permute-start.2 = (f32[208,128]{1,0:T(8,128)}, f32[208,128]{1,0:T(8,128)}, u32[]{:S(2)}, u32[]{:S(2)}) collective-permute-start(f32[208,128]{1,0:T(8,128)} %shard_map.110), channel_id=1, source_target_pairs={{0,24},{8,0},{16,8},{24,16},{1,25},{9,1},{17,9},{25,17},{2,26},{10... | collective-permute-start | bytes 319496 | tf_op jit(solution)/shard_map/ppermute | solution.py:279
  45.2 41.7 %copy-start.13 = (bf16[12,128,128]{2,1,0:T(8,128)(2,1)}, bf16[12,128,128]{2,1,0:T(8,128)(2,1)S(1)}, u32[]{:S(2)}) copy-start(bf16[12,128,128]{2,1,0:T(8,128)(2,1)S(1)} %get-tuple-element.38.low_ref) | copy-start | bytes 1179652
  47.7 39.3 %copy-start.15 = (bf16[128,1536]{1,0:T(8,128)(2,1)}, bf16[128,1536]{1,0:T(8,128)(2,1)S(1)}, u32[]{:S(2)}) copy-start(bf16[128,1536]{1,0:T(8,128)(2,1)S(1)} %get-tuple-element.39.gn_ref) | copy-start | bytes 1179652
  89.0 0.7 copy-start.17
  89.7 4.8 %collective-permute-start.3 = (f32[208,128]{1,0:T(8,128)S(1)}, f32[208,128]{1,0:T(8,128)S(1)}, u32[]{:S(2)}, u32[]{:S(2)}) collective-permute-start(f32[208,128]{1,0:T(8,128)S(1)} %get-tuple-element.44.own_ref), channel_id=1, source_target_pairs={{0,8},{8,16},{16,24},{24,0},{1,9},{9,17},{17,25},{25,1},{2,10},{10... | collective-permute-start | bytes 319496 | tf_op jit(solution)/shard_map/ppermute | solution.py:279
  89.7 6.7 %collective-permute-start.4 = (f32[208,128]{1,0:T(8,128)S(1)}, f32[208,128]{1,0:T(8,128)S(1)}, u32[]{:S(2)}, u32[]{:S(2)}) collective-permute-start(f32[208,128]{1,0:T(8,128)S(1)} %get-tuple-element.44.own_ref), channel_id=1, source_target_pairs={{0,16},{8,24},{16,0},{24,8},{1,17},{9,25},{17,1},{25,9},{2,18},{10... | collective-permute-start | bytes 319496 | tf_op jit(solution)/shard_map/ppermute | solution.py:279
  93.2 3.6 %collective-permute-start.5 = (f32[208,128]{1,0:T(8,128)S(1)}, f32[208,128]{1,0:T(8,128)S(1)}, u32[]{:S(2)}, u32[]{:S(2)}) collective-permute-start(f32[208,128]{1,0:T(8,128)S(1)} %get-tuple-element.44.own_ref), channel_id=1, source_target_pairs={{0,24},{8,0},{16,8},{24,16},{1,25},{9,1},{17,9},{25,17},{2,26},{10... | collective-permute-start | bytes 319496 | tf_op jit(solution)/shard_map/ppermute | solution.py:279
  97.7 25.9 %all-to-all-start.2 = ((f32[8,208,128]{2,1,0:T(8,128)}), f32[8,208,128]{2,1,0:T(8,128)S(1)}, u32[]{:S(2)}, u32[]{:S(2)}) async-start(f32[8,208,128]{2,1,0:T(8,128)} %shard_map.115), calls=%async_computation.2 | async-start | bytes 1703936 | tf_op jit(solution)/shard_map/all_to_all | solution.py:283
  102.7 1.0 copy-start.14
  103.7 1.0 copy-start.16
  104.7 1.0 copy-start.18
  105.7 18.0 %copy-start.10 = (bf16[1,128,512]{2,1,0:T(8,128)(2,1)S(1)}, bf16[1,128,512]{2,1,0:T(8,128)(2,1)}, u32[]{:S(2)}) copy-start(bf16[1,128,512]{2,1,0:T(8,128)(2,1)} %param.7) | copy-start | bytes 393220
  111.0 0.9 copy-start.6
  111.9 0.7 copy-start.11
  123.7 1.1 copy-start.7
  124.8 1.0 copy-start.12
  128.1 4.4 %collective-permute-start.6 = (f32[12,64,128]{2,1,0:T(8,128)S(1)}, f32[12,64,128]{2,1,0:T(8,128)S(1)}, u32[]{:S(2)}, u32[]{:S(2)}) collective-permute-start(f32[12,64,128]{2,1,0:T(8,128)S(1)} %get-tuple-element.53), channel_id=1, source_target_pairs={{0,32},{32,0},{1,33},{33,1},{2,34},{34,2},{3,35},{35,3},{4,36},{36... | collective-permute-start | bytes 1179656 | tf_op jit(solution)/shard_map/ppermute | solution.py:337
  132.6 41.8 %copy-start.5 = (bf16[12,128,64]{1,2,0:T(8,128)(2,1)S(1)}, bf16[12,128,64]{1,2,0:T(8,128)(2,1)}, u32[]{:S(2)}) copy-start(bf16[12,128,64]{1,2,0:T(8,128)(2,1)} %param.11) | copy-start | bytes 589828
  169.7 6.0 %collective-permute-start.7 = (f32[12,64,128]{2,1,0:T(8,128)S(1)}, f32[12,64,128]{2,1,0:T(8,128)S(1)}, u32[]{:S(2)}, u32[]{:S(2)}) collective-permute-start(f32[12,64,128]{2,1,0:T(8,128)S(1)} %bitcast.33), channel_id=1, source_target_pairs={{0,32},{32,0},{1,33},{33,1},{2,34},{34,2},{3,35},{35,3},{4,36},{36... | collective-permute-start | bytes 1179656 | tf_op jit(solution)/shard_map/ppermute | solution.py:344

commit v4 on v3

--- a/solution.py
+++ b/solution.py
@@ -283,6 +283,10 @@
     return lax.all_to_all(blocks, "z", 0, 0, axis_index_groups=[list(RING)], tiled=True)
 
 
+def exchange_after(blocks, token):
+    return exchange_z(lax.dynamic_update_slice(blocks, token, (0, ROWS + H, 0)))
+
+
 def spread(rows, count):
     return jnp.broadcast_to(rows[None], (count,) + rows.shape)
 
@@ -303,7 +307,9 @@
         key_kernel, [(short, F32), (square, F32)], (), k, v, km,
         scratch=[pltpu.VMEM(small, F32)], macs=2,
     )
-    first = exchange_z(send)
+    first = lax.cond(core[0] == 0, exchange_z, lambda blocks: blocks, send)
+    token = lax.ppermute(first[:1, ROWS + H :, :], "core", [(0, 1)])
+    first = lax.cond(core[0] == 0, lambda blocks, token: blocks, exchange_after, first, token)
     (total,) = run(total_kernel, [(flat, F32)], (), first)
     others = turn(total)
     pq, low, rows, num = run(

time: 177 us -> 169 us (0.955)
  blocking collectives: 108 us -> 81.2 us
  waiting for transfers between devices: 16.5 us -> 41.2 us
  starting transfers between devices: 21 us -> 14.2 us
    ppermute x0 -> x1, waiting for transfers between devices: none -> 27.2 us  [shards(): token = lax.ppermute(first[:1, ROWS + H:, :], 'core', [(0, 1)])]
    all_to_all x3, blocking collectives: 81.5 us -> 55.2 us  [exchange_z(): lax.all_to_all(blocks, 'z', 0, 0, axis_index_groups=[list(RING)], tiled=T...]
    all_to_all x1, waiting for transfers between devices: 11 us -> 4.11 us  [exchange_z(): lax.all_to_all(blocks, 'z', 0, 0, axis_index_groups=[list(RING)], tiled=T...]
    ppermute x6, waiting for transfers between devices: 3.9 us -> 8.02 us  [turn(): lax.ppermute(rows, 'x', [(i, (i + step) % NX) for i in range(NX)])]
    ppermute x6, starting transfers between devices: 8.27 us -> 5.15 us  [turn(): lax.ppermute(rows, 'x', [(i, (i + step) % NX) for i in range(NX)])]
    ppermute x1, starting transfers between devices: 3.07 us -> 0.01 us  [shards(): mine = keep + lax.ppermute(give, 'core', swap)]
  transfers between devices with their start and end apart: 9 -> 10, of which waited for: 7 -> 9; matrix products, arithmetic and copies ran while one was open for 0% -> 0% of each run, Pallas kernels for 5% -> 5%
where the time goes in v4:
time: 169 us
  blocking collectives  81.2 us (48%)
  waiting for transfers between devices  41.2 us (24%)
  Pallas kernels  20 us (12%)
  starting transfers between devices  14.2 us (8%)
  local copies, waits for them, and re-layouts  10.3 us (6%)
    all_to_all x3, blocking collectives, exchange_z(): lax.all_to_all(blocks, 'z', 0, 0, axis_index_groups=[list(RING)], tiled=T...  55.2 us
    ppermute x1, waiting for transfers between devices, shards(): token = lax.ppermute(first[:1, ROWS + H:, :], 'core', [(0, 1)])  27.2 us
    all_to_all x2, blocking collectives, exchange(): return lax.all_to_all(blocks, axes, 0, 0, tiled=True)  26 us
    pallas_call x9, Pallas kernels, run(): pl.pallas_call(kernel, out_shape=tuple((jax.ShapeDtypeStruct(shape, dtype...  20 us
    unnamed x38, local copies, waits for them, and re-layouts  10.3 us
    ppermute x6, waiting for transfers between devices, turn(): lax.ppermute(rows, 'x', [(i, (i + step) % NX) for i in range(NX)])  8.02 us
    ppermute x6, starting transfers between devices, turn(): lax.ppermute(rows, 'x', [(i, (i + step) % NX) for i in range(NX)])  5.15 us
    ppermute x1, starting transfers between devices, shards(): other = lax.ppermute(mine, 'core', swap)  4.18 us
  transfers between devices with their start and end apart: 10, of which 9 were waited for; matrix products, arithmetic and copies ran while one was open for 0% of the time, Pallas kernels for 5%

profile of v4, /device:TPU:1, one launch (start us, length us, event | category | flops | bytes accessed | tf_op | source)
XLA Modules:
  0.0 168.8 jit_solution(14499080893322295990)
XLA Ops:
  0.6 0.0 copy-start
  0.7 0.9 copy-done
  1.6 0.9 copy-done.4
  2.5 0.9 copy-done.9
  3.4 2.2 %shard_map.109 = (f32[8,208,128]{2,1,0:T(8,128)S(1)}, f32[12,128,128]{2,1,0:T(8,128)S(1)}) custom-call(bf16[128,512]{1,0:T(8,128)(2,1)S(1)} %bitcast.31, bf16[128,512]{1,0:T(8,128)(2,1)S(1)} %bitcast.19, bf16[12,64,128]{2,1,0:T(8,128)(2,1)S(1)} %bitcast.27), custom_call_target="tpu_custom_call" | custom-call | flops 100663296 | bytes 917504 | tf_op jit(solution)/shard_map/pallas_call | solution.py:261
  5.6 1.3 collective-permute-start
  6.9 27.2 %collective-permute-done = f32[1,4,128]{2,1,0:T(4,128)S(1)} collective-permute-done((f32[1,4,128]{2,1,0:T(4,128)S(1)}, f32[1,4,128]{2,1,0:T(4,128)S(1)}, u32[]{:S(2)}, u32[]{:S(2)}) %collective-permute-start) | collective-permute-done | bytes 2080 | tf_op jit(solution)/shard_map/ppermute | solution.py:311
  34.1 18.6 %conditional.3 = (f32[8,208,128]{2,1,0:T(8,128)}) conditional(s32[]{:T(128)} %convert_element_type.4, (f32[8,208,128]{2,1,0:T(8,128)S(1)}, f32[1,4,128]{2,1,0:T(4,128)S(1)}) %tuple.20, f32[8,208,128]{2,1,0:T(8,128)S(1)} %get-tuple-element.71), branch_computations={%region_2.0_spmd, %region_3.0_spmd} | conditional | bytes 1708040 | solution.py:312
  34.1 18.6 %all_to_all.34 = f32[8,208,128]{2,1,0:T(8,128)} all-to-all(f32[8,208,128]{2,1,0:T(8,128)S(1)} %constant_dynamic-update-slice_fusion), channel_id=1, replica_groups={{0,1,3,5,7,6,4,2},{8,9,11,13,15,14,12,10},{16,17,19,21,23,22,20,18},{24..., dimensions={0} | all-to-all | bytes 1703936 | tf_op jit(solution)/shard_map/cond/branch_0_fun/all_to_all | solution.py:283
  52.7 1.2 shard_map.110
  54.0 2.6 %collective-permute-start.3 = (f32[208,128]{1,0:T(8,128)S(1)}, f32[208,128]{1,0:T(8,128)S(1)}, u32[]{:S(2)}, u32[]{:S(2)}) collective-permute-start(f32[208,128]{1,0:T(8,128)S(1)} %shard_map.110), channel_id=1, source_target_pairs={{0,24},{8,0},{16,8},{24,16},{1,25},{9,1},{17,9},{25,17},{2,26},{10... | collective-permute-start | bytes 319496 | tf_op jit(solution)/shard_map/ppermute | solution.py:279
  56.5 0.5 collective-permute-start.2
  57.0 0.6 collective-permute-start.1
  57.6 2.6 %shard_map.111 = (f32[12,128,128]{2,1,0:T(8,128)S(1)}, bf16[12,128,128]{2,1,0:T(8,128)(2,1)S(1)}, f32[16,128]{1,0:T(8,128)S(1)}, f32[128,1536]{1,0:T(8,128)S(1)}) custom-call(bf16[128,1536]{1,0:T(8,128)(2,1)S(1)} %bitcast.25, bf16[128,512]{1,0:T(8,128)(2,1)S(1)} %bitcast.20, bf16[12,64,128]{2,1,0:T(8,128)(2,1)S(1)} %bitcast.29, ...), custom_call_target="tpu_custom_call" | custom-call | flops 150994944 | bytes 3014656 | tf_op jit(solution)/shard_map/pallas_call | solution.py:261
  60.3 0.0 copy-start.13
  60.3 1.4 collective-permute-done.2.two_ref
  61.7 1.3 collective-permute-done.1.one_ref
  63.0 2.2 %shard_map.112 = (f32[8,384,128]{2,1,0:T(8,128)S(1)}, bf16[128,1536]{1,0:T(8,128)(2,1)S(1)}, f32[16,128]{1,0:T(8,128)S(1)}, f32[16,128]{1,0:T(8,128)S(1)}) custom-call(s32[1]{0:T(128)} %bitcast.x_ref, s32[1]{0:T(128)} %bitcast.1.z_ref, f32[8,208,128]{2,1,0:T(8,128)} %get-tuple-element.72.got_ref, f32[208,128]{1,0:T(8,128)} %collective-permute-done.1.one_ref, ...), custom_call_target="tpu_custom_call" | custom-call | flops 50331648 | bytes 4718592 | tf_op jit(solution)/shard_map/pallas_call | solution.py:261
  65.2 25.8 %all_to_all.35.got_ref = f32[8,384,128]{2,1,0:T(8,128)S(1)} all-to-all(f32[8,384,128]{2,1,0:T(8,128)S(1)} %get-tuple-element.49), channel_id=1, replica_groups={{0,1,3,5,7,6,4,2},{8,9,11,13,15,14,12,10},{16,17,19,21,23,22,20,18},{24..., dimensions={0} | all-to-all | bytes 3145728 | tf_op jit(solution)/shard_map/all_to_all | solution.py:283
  91.0 2.0 %shard_map.113 = (bf16[128,1536]{1,0:T(8,128)(2,1)}, f32[208,128]{1,0:T(8,128)S(1)}, f32[16,128]{1,0:T(8,128)S(1)}, bf16[12,128,128]{2,1,0:T(8,128)(2,1)S(1)}) custom-call(f32[8,384,128]{2,1,0:T(8,128)S(1)} %all_to_all.35.got_ref, f32[12,128,128]{2,1,0:T(8,128)S(1)} %get-tuple-element.47.pq_ref, f32[128,1536]{1,0:T(8,128)S(1)} %get-tuple-element.50.num_ref, ...), custom_call_target="tpu_custom_call" | custom-call | flops 50331648 | bytes 7094272 | tf_op jit(solution)/shard_map/pallas_call | solution.py:261
  93.0 0.7 copy-done.17
  93.8 0.3 collective-permute-start.6
  94.1 0.5 collective-permute-start.5
  94.6 0.7 collective-permute-start.4
  95.2 2.4 %collective-permute-done.6.three_ref = f32[208,128]{1,0:T(8,128)S(1)} collective-permute-done((f32[208,128]{1,0:T(8,128)S(1)}, f32[208,128]{1,0:T(8,128)S(1)}, u32[]{:S(2)}, u32[]{:S(2)}) %collective-permute-start.6) | collective-permute-done | bytes 106528 | tf_op jit(solution)/shard_map/ppermute | solution.py:279
  97.6 1.6 collective-permute-done.5.two_ref
  99.2 1.4 collective-permute-done.4.one_ref
  100.6 1.0 shard_map.115
  101.5 3.5 %all-to-all-start.3 = ((f32[8,208,128]{2,1,0:T(8,128)}), f32[8,208,128]{2,1,0:T(8,128)S(1)}, u32[]{:S(2)}, u32[]{:S(2)}) async-start(f32[8,208,128]{2,1,0:T(8,128)} %shard_map.115), calls=%async_computation.3 | async-start | bytes 1703936 | tf_op jit(solution)/shard_map/all_to_all | solution.py:283
  105.1 1.0 copy-done.14
  106.1 1.0 copy-done.16
  107.1 1.0 copy-done.18
  108.1 5.3 %shard_map.114 = (bf16[128,1536]{1,0:T(8,128)(2,1)}, f32[12,64,128]{2,1,0:T(8,128)S(1)}, f32[12,128,128]{2,1,0:T(8,128)S(1)}, f32[128,512]{1,0:T(8,128)S(1)}) custom-call(bf16[128,1536]{1,0:T(8,128)(2,1)S(1)} %bitcast.26, bf16[128,512]{1,0:T(8,128)(2,1)S(1)} %bitcast.21, bf16[12,64,128]{2,1,0:T(8,128)(2,1)S(1)} %bitcast.30, ...), custom_call_target="tpu_custom_call" | custom-call | flops 352321536 | bytes 6979584 | tf_op jit(solution)/shard_map/pallas_call | solution.py:261
  113.4 0.9 copy-done.6
  114.3 0.7 copy-done.11
  115.1 4.1 %all-to-all-done.3.got_ref = f32[8,208,128]{2,1,0:T(8,128)S(1)} async-done(((f32[8,208,128]{2,1,0:T(8,128)}), f32[8,208,128]{2,1,0:T(8,128)S(1)}, u32[]{:S(2)}, u32[]{:S(2)}) %all-to-all-start.3) | async-done | bytes 852000 | tf_op jit(solution)/shard_map/all_to_all | solution.py:283
  119.2 1.1 copy-done.7
  120.3 1.0 copy-done.12
  121.3 2.3 %shard_map.116 = (f32[12,64,128]{2,1,0:T(8,128)S(1)}, f32[12,64,128]{2,1,0:T(8,128)S(1)}, bf16[12,64,128]{2,1,0:T(8,128)(2,1)S(1)}, bf16[12,128,128]{2,1,0:T(8,128)(2,1)S(1)}) custom-call(s32[1]{0:T(128)} %bitcast.10.core_ref, f32[8,208,128]{2,1,0:T(8,128)S(1)} %all-to-all-done.3.got_ref, f32[12,128,128]{2,1,0:T(8,128)S(1)} %copy-done.7, ...), custom_call_target="tpu_custom_call" | custom-call | flops 100663296 | bytes 6160384 | tf_op jit(solution)/shard_map/pallas_call | solution.py:261
  123.6 1.7 %collective-permute-done.7 = f32[12,64,128]{2,1,0:T(8,128)S(1)} collective-permute-done((f32[12,64,128]{2,1,0:T(8,128)S(1)}, f32[12,64,128]{2,1,0:T(8,128)S(1)}, u32[]{:S(2)}, u32[]{:S(2)}) %collective-permute-start.7) | collective-permute-done | bytes 393248 | tf_op jit(solution)/shard_map/ppermute | solution.py:343
  125.3 0.1 add.3
  125.4 14.3 %all_to_all.36 = f32[16,48,128]{2,1,0:T(8,128)S(1)} all-to-all(f32[16,48,128]{2,1,0:T(8,128)S(1)} %bitcast.35), channel_id=1, replica_groups=mesh['y'=4,'core'=2,'x'=4,'z'=8] {'y','x'}, dimensions={0} | all-to-all | bytes 786432 | tf_op jit(solution)/shard_map/all_to_all | solution.py:275
  139.8 10.8 %all_to_all.37 = f32[8,48,128]{2,1,0:T(8,128)S(1)} all-to-all(f32[8,48,128]{2,1,0:T(8,128)S(1)} %broadcast_in_dim.28), channel_id=1, replica_groups={{0,1,3,5,7,6,4,2},{8,9,11,13,15,14,12,10},{16,17,19,21,23,22,20,18},{24..., dimensions={0} | all-to-all | bytes 393216 | tf_op jit(solution)/shard_map/all_to_all | solution.py:283
  150.6 11.6 %all_to_all.38 = f32[16,48,128]{2,1,0:T(8,128)S(1)} all-to-all(f32[16,48,128]{2,1,0:T(8,128)S(1)} %broadcast_in_dim.29), channel_id=1, replica_groups=mesh['y'=4,'core'=2,'x'=4,'z'=8] {'y','x'}, dimensions={0} | all-to-all | bytes 786432 | tf_op jit(solution)/shard_map/all_to_all | solution.py:275
  162.3 4.2 %collective-permute-start.8 = (f32[12,64,128]{2,1,0:T(8,128)S(1)}, f32[12,64,128]{2,1,0:T(8,128)S(1)}, u32[]{:S(2)}, u32[]{:S(2)}) collective-permute-start(f32[12,64,128]{2,1,0:T(8,128)S(1)} %bitcast.33), channel_id=1, source_target_pairs={{0,32},{32,0},{1,33},{33,1},{2,34},{34,2},{3,35},{35,3},{4,36},{36... | collective-permute-start | bytes 1179656 | tf_op jit(solution)/shard_map/ppermute | solution.py:350
  166.5 1.1 shard_map.117
  167.6 0.2 collective-permute-done.8
  167.8 0.9 select_bitcast_fusion
  (34 shorter events, 0.2 us)
Async XLA Ops:
  0.6 0.9 copy-start
  1.5 0.9 copy-start.4
  2.5 0.9 copy-start.9
  5.6 28.5 %collective-permute-start = (f32[1,4,128]{2,1,0:T(4,128)S(1)}, f32[1,4,128]{2,1,0:T(4,128)S(1)}, u32[]{:S(2)}, u32[]{:S(2)}) collective-permute-start(f32[1,4,128]{2,1,0:T(4,128)S(1)} %slice.4), channel_id=1, source_target_pairs={{0,32},{1,33},{2,34},{3,35},{4,36},{5,37},{6,38},{7,39},{8,40},{9,... | collective-permute-start | bytes 6152 | tf_op jit(solution)/shard_map/ppermute | solution.py:311
  34.1 23.6 %copy-start.1 = (bf16[1,128,512]{2,1,0:T(8,128)(2,1)S(1)}, bf16[1,128,512]{2,1,0:T(8,128)(2,1)}, u32[]{:S(2)}) copy-start(bf16[1,128,512]{2,1,0:T(8,128)(2,1)} %param.12) | copy-start | bytes 393220
  34.1 23.6 %copy-start.3 = (bf16[1,128,1536]{2,1,0:T(8,128)(2,1)S(1)}, bf16[1,128,1536]{2,1,0:T(8,128)(2,1)}, u32[]{:S(2)}) copy-start(bf16[1,128,1536]{2,1,0:T(8,128)(2,1)} %param.10) | copy-start | bytes 1179652
  34.1 23.6 %copy-start.8 = (bf16[12,128,64]{1,2,0:T(8,128)(2,1)S(1)}, bf16[12,128,64]{1,2,0:T(8,128)(2,1)}, u32[]{:S(2)}) copy-start(bf16[12,128,64]{1,2,0:T(8,128)(2,1)} %param.14) | copy-start | bytes 589828
  52.7 10.3 %copy-start.2 = (bf16[1,128,1536]{2,1,0:T(8,128)(2,1)S(1)}, bf16[1,128,1536]{2,1,0:T(8,128)(2,1)}, u32[]{:S(2)}) copy-start(bf16[1,128,1536]{2,1,0:T(8,128)(2,1)} %param.13) | copy-start | bytes 1179652
  54.0 6.3 %collective-permute-start.3 = (f32[208,128]{1,0:T(8,128)S(1)}, f32[208,128]{1,0:T(8,128)S(1)}, u32[]{:S(2)}, u32[]{:S(2)}) collective-permute-start(f32[208,128]{1,0:T(8,128)S(1)} %shard_map.110), channel_id=1, source_target_pairs={{0,24},{8,0},{16,8},{24,16},{1,25},{9,1},{17,9},{25,17},{2,26},{10... | collective-permute-start | bytes 319496 | tf_op jit(solution)/shard_map/ppermute | solution.py:279
  56.5 5.2 %collective-permute-start.2 = (f32[208,128]{1,0:T(8,128)S(1)}, f32[208,128]{1,0:T(8,128)S(1)}, u32[]{:S(2)}, u32[]{:S(2)}) collective-permute-start(f32[208,128]{1,0:T(8,128)S(1)} %shard_map.110), channel_id=1, source_target_pairs={{0,16},{8,24},{16,0},{24,8},{1,17},{9,25},{17,1},{25,9},{2,18},{10... | collective-permute-start | bytes 319496 | tf_op jit(solution)/shard_map/ppermute | solution.py:279
  57.0 6.0 %collective-permute-start.1 = (f32[208,128]{1,0:T(8,128)S(1)}, f32[208,128]{1,0:T(8,128)}, u32[]{:S(2)}, u32[]{:S(2)}) collective-permute-start(f32[208,128]{1,0:T(8,128)S(1)} %shard_map.110), channel_id=1, source_target_pairs={{0,8},{8,16},{16,24},{24,0},{1,9},{9,17},{17,25},{25,1},{2,10},{10... | collective-permute-start | bytes 319496 | tf_op jit(solution)/shard_map/ppermute | solution.py:279
  60.3 30.7 %copy-start.13 = (bf16[12,128,128]{2,1,0:T(8,128)(2,1)}, bf16[12,128,128]{2,1,0:T(8,128)(2,1)S(1)}, u32[]{:S(2)}) copy-start(bf16[12,128,128]{2,1,0:T(8,128)(2,1)S(1)} %get-tuple-element.53.low_ref) | copy-start | bytes 1179652
  65.2 25.8 %copy-start.15 = (bf16[128,1536]{1,0:T(8,128)(2,1)}, bf16[128,1536]{1,0:T(8,128)(2,1)S(1)}, u32[]{:S(2)}) copy-start(bf16[128,1536]{1,0:T(8,128)(2,1)S(1)} %get-tuple-element.54.gn_ref) | copy-start | bytes 1179652
  93.0 0.7 copy-start.17
  93.8 3.9 %collective-permute-start.6 = (f32[208,128]{1,0:T(8,128)S(1)}, f32[208,128]{1,0:T(8,128)S(1)}, u32[]{:S(2)}, u32[]{:S(2)}) collective-permute-start(f32[208,128]{1,0:T(8,128)S(1)} %get-tuple-element.59.own_ref), channel_id=1, source_target_pairs={{0,24},{8,0},{16,8},{24,16},{1,25},{9,1},{17,9},{25,17},{2,26},{10... | collective-permute-start | bytes 319496 | tf_op jit(solution)/shard_map/ppermute | solution.py:279
  94.1 5.1 %collective-permute-start.5 = (f32[208,128]{1,0:T(8,128)S(1)}, f32[208,128]{1,0:T(8,128)S(1)}, u32[]{:S(2)}, u32[]{:S(2)}) collective-permute-start(f32[208,128]{1,0:T(8,128)S(1)} %get-tuple-element.59.own_ref), channel_id=1, source_target_pairs={{0,16},{8,24},{16,0},{24,8},{1,17},{9,25},{17,1},{25,9},{2,18},{10... | collective-permute-start | bytes 319496 | tf_op jit(solution)/shard_map/ppermute | solution.py:279
  94.6 6.0 %collective-permute-start.4 = (f32[208,128]{1,0:T(8,128)S(1)}, f32[208,128]{1,0:T(8,128)S(1)}, u32[]{:S(2)}, u32[]{:S(2)}) collective-permute-start(f32[208,128]{1,0:T(8,128)S(1)} %get-tuple-element.59.own_ref), channel_id=1, source_target_pairs={{0,8},{8,16},{16,24},{24,0},{1,9},{9,17},{17,25},{25,1},{2,10},{10... | collective-permute-start | bytes 319496 | tf_op jit(solution)/shard_map/ppermute | solution.py:279
  101.5 17.6 %all-to-all-start.3 = ((f32[8,208,128]{2,1,0:T(8,128)}), f32[8,208,128]{2,1,0:T(8,128)S(1)}, u32[]{:S(2)}, u32[]{:S(2)}) async-start(f32[8,208,128]{2,1,0:T(8,128)} %shard_map.115), calls=%async_computation.3 | async-start | bytes 1703936 | tf_op jit(solution)/shard_map/all_to_all | solution.py:283
  105.1 1.0 copy-start.14
  106.1 1.0 copy-start.16
  107.1 1.0 copy-start.18
  108.1 11.1 %copy-start.10 = (bf16[1,128,512]{2,1,0:T(8,128)(2,1)S(1)}, bf16[1,128,512]{2,1,0:T(8,128)(2,1)}, u32[]{:S(2)}) copy-start(bf16[1,128,512]{2,1,0:T(8,128)(2,1)} %param.11) | copy-start | bytes 393220
  113.4 0.9 copy-start.6
  114.3 0.7 copy-start.11
  119.2 1.1 copy-start.7
  120.3 1.0 copy-start.12
  123.6 1.7 %collective-permute-start.7 = (f32[12,64,128]{2,1,0:T(8,128)S(1)}, f32[12,64,128]{2,1,0:T(8,128)S(1)}, u32[]{:S(2)}, u32[]{:S(2)}) collective-permute-start(f32[12,64,128]{2,1,0:T(8,128)S(1)} %get-tuple-element.68), channel_id=1, source_target_pairs={{0,32},{32,0},{1,33},{33,1},{2,34},{34,2},{3,35},{35,3},{4,36},{36... | collective-permute-start | bytes 1179656 | tf_op jit(solution)/shard_map/ppermute | solution.py:343
  125.4 41.1 %copy-start.5 = (bf16[12,128,64]{1,2,0:T(8,128)(2,1)S(1)}, bf16[12,128,64]{1,2,0:T(8,128)(2,1)}, u32[]{:S(2)}) copy-start(bf16[12,128,64]{1,2,0:T(8,128)(2,1)} %param.15) | copy-start | bytes 589828
  162.3 5.5 %collective-permute-start.8 = (f32[12,64,128]{2,1,0:T(8,128)S(1)}, f32[12,64,128]{2,1,0:T(8,128)S(1)}, u32[]{:S(2)}, u32[]{:S(2)}) collective-permute-start(f32[12,64,128]{2,1,0:T(8,128)S(1)} %bitcast.33), channel_id=1, source_target_pairs={{0,32},{32,0},{1,33},{33,1},{2,34},{34,2},{3,35},{35,3},{4,36},{36... | collective-permute-start | bytes 1179656 | tf_op jit(solution)/shard_map/ppermute | solution.py:350

commit v5 on v4

--- a/solution.py
+++ b/solution.py
@@ -82,15 +82,17 @@
     return (p1 * (d1 - inner1) - p2 * (d2 - inner2)).astype(BF16)
 
 
-def key_kernel(k_ref, v_ref, km_ref, send_ref, pk_ref, norm_ref):
+def key_kernel(k_ref, km_ref, pk_ref):
+    for h in range(H):
+        pk_ref[h] = two_softmaxes(nt(km_ref[h], k_ref[:, of_head(h // GROUP)]))
+
+
+def state_kernel(pk_ref, v_ref, send_ref, norm_ref):
     ones = jnp.ones((8, TOK), BF16)
     norm_ref[...] = jnp.zeros_like(norm_ref)
     for h in range(H):
-        kv = of_head(h // GROUP)
-        prob = two_softmaxes(nt(km_ref[h], k_ref[:, kv]))
-        pk_ref[h] = prob
-        feat = prob.astype(BF16)
-        put_head(send_ref, 0, h, nn(feat, v_ref[:, kv]))
+        feat = pk_ref[h].astype(BF16)
+        put_head(send_ref, 0, h, nn(feat, v_ref[:, of_head(h // GROUP)]))
         norm_ref[h : h + 1, :] = nt(ones, feat)[0:1]
     send_ref[:, ROWS:, :] = jnp.broadcast_to(norm_ref[...][None], (NZ, PAD, DH))
 
@@ -99,13 +101,13 @@
     mask = causal()
     rows_ref[...] = jnp.ones_like(rows_ref)
     for h in range(H):
-        prob = two_softmaxes(nt(qm_ref[h], q_ref[:, of_head(h)]))
-        pq_ref[h] = prob
-        scores = jnp.where(mask, tn(pk_ref[h].astype(BF16), prob.astype(BF16)), 0.0)
-        low = scores.astype(BF16)
-        low_ref[h] = low
+        pq_ref[h] = two_softmaxes(nt(qm_ref[h], q_ref[:, of_head(h)]))
+    for h in range(H):
+        scores = jnp.where(mask, tn(pk_ref[h].astype(BF16), pq_ref[h].astype(BF16)), 0.0)
+        low_ref[h] = scores.astype(BF16)
         rows_ref[h : h + 1, :] = jnp.sum(scores, axis=0, keepdims=True)
-        num_ref[:, of_head(h)] = tn(low, v_ref[:, of_head(h // GROUP)])
+    for h in range(H):
+        num_ref[:, of_head(h)] = tn(low_ref[h], v_ref[:, of_head(h // GROUP)])
 
 
 def total_kernel(got_ref, out_ref):
@@ -150,11 +152,13 @@
     for h in range(H):
         grad = (g_ref[:, of_head(h)].astype(F32) * scale[:, h : h + 1]).astype(BF16)
         gn_ref[:, of_head(h)] = grad
-        put_head(send_ref, ROWS, h, nn(pq_ref[h].astype(BF16), grad))
+    for h in range(H):
+        put_head(send_ref, ROWS, h, nn(pq_ref[h].astype(BF16), gn_ref[:, of_head(h)]))
 
 
 def finish_kernel(
-    got_ref, pq_ref, num_ref, rden_ref, g_ref, att_ref, sum_ref, gd_ref, low_ref, col_ref
+    got_ref, pq_ref, num_ref, rden_ref, g_ref, att_ref, sum_ref, gd_ref, low_ref, col_ref,
+    out_ref,
 ):
     total = got_ref[0, ROWS:, :]
     for j in range(1, NZ):
@@ -163,10 +167,12 @@
     scale = rden_ref[...].T
     col_ref[...] = jnp.zeros_like(col_ref)
     for h in range(H):
-        low = get_head(got_ref, 0, h).astype(BF16)
-        low_ref[h] = low
-        out = num_ref[:, of_head(h)] + tn(pq_ref[h].astype(BF16), low)
-        out = out * scale[:, h : h + 1]
+        low_ref[h] = get_head(got_ref, 0, h).astype(BF16)
+    for h in range(H):
+        out = num_ref[:, of_head(h)] + tn(pq_ref[h].astype(BF16), low_ref[h])
+        out_ref[:, of_head(h)] = out * scale[:, h : h + 1]
+    for h in range(H):
+        out = out_ref[:, of_head(h)]
         att_ref[:, of_head(h)] = out.astype(BF16)
         col_ref[:, h : h + 1] = jnp.sum(g_ref[:, of_head(h)].astype(F32) * out, axis=1, keepdims=True)
     grad = -col_ref[...].T[:PAD] * rden_ref[...]
@@ -197,32 +203,33 @@
 
 def inner_kernel(
     q_ref, v_ref, qm_ref, pq_ref, pk_ref, low_ref, gn_ref, gd_ref, state_ref, norm_ref,
-    qg_ref, qw_ref, part_ref, vpart_ref,
+    qg_ref, both_ref, vpart_ref, score_ref, feat_ref, gu_ref,
 ):
     mask = causal()
     columns = norm_ref[...].T
+    for h in range(H):
+        dscore = nt(v_ref[:, of_head(h // GROUP)], gn_ref[:, of_head(h)]) + gd_ref[h : h + 1, :]
+        score_ref[h] = jnp.where(mask, dscore, 0.0).astype(BF16)
+    for h in range(H):
+        grad_feat = nn(pk_ref[h].astype(BF16), score_ref[h])
+        grad_feat = grad_feat + nt(state_ref[h], gn_ref[:, of_head(h)])
+        feat_ref[h] = grad_feat + columns[:, h : h + 1] * gd_ref[h : h + 1, :]
+    for h in range(H):
+        gu_ref[h] = back_through(pq_ref[h], feat_ref[h])
+    for h in range(H):
+        both_ref[h, DH:, :] = nn(gu_ref[h], q_ref[:, of_head(h)])
+    for h in range(H):
+        qg_ref[:, of_head(h)] = tn(gu_ref[h], qm_ref[h]).astype(BF16)
+    for h in range(H):
+        both_ref[h, :DH, :] = nt(pq_ref[h].astype(BF16), score_ref[h])
     for kv in range(KVH):
-        value = v_ref[:, of_head(kv)]
-        value_sum = None
-        for h in range(kv * GROUP, (kv + 1) * GROUP):
-            prob = pq_ref[h]
-            grad = gn_ref[:, of_head(h)]
-            den = gd_ref[h : h + 1, :]
-            dscore = jnp.where(mask, nt(value, grad) + den, 0.0).astype(BF16)
-            grad_feat = nn(pk_ref[h].astype(BF16), dscore) + nt(state_ref[h], grad)
-            grad_feat = grad_feat + columns[:, h : h + 1] * den
-            grad_u = back_through(prob, grad_feat)
-            qw_ref[h] = nn(grad_u, q_ref[:, of_head(h)])
-            qg_ref[:, of_head(h)] = tn(grad_u, qm_ref[h]).astype(BF16)
-            part_ref[h] = nt(prob.astype(BF16), dscore)
-            term = nn(low_ref[h], grad)
-            value_sum = term if value_sum is None else value_sum + term
-        vpart_ref[:, of_head(kv)] = value_sum
+        heads = range(kv * GROUP, (kv + 1) * GROUP)
+        vpart_ref[:, of_head(kv)] = sum(nn(low_ref[h], gn_ref[:, of_head(h)]) for h in heads)
 
 
 def outer_kernel(
-    core_ref, got_ref, part_ref, pk_ref, k_ref, v_ref, qw_ref,
-    keep_ref, give_ref, gu_ref, low_ref,
+    core_ref, got_ref, both_ref, pk_ref, k_ref, v_ref,
+    keep_ref, give_ref, gu_ref, low_ref, feat_ref,
 ):
     first = core_ref[0] == 0
     norm = got_ref[0, NORM, :]
@@ -230,14 +237,15 @@
         norm = norm + got_ref[j, NORM, :]
     columns = norm.T
     for h in range(H):
-        kv = of_head(h // GROUP)
-        low = get_head(got_ref, 0, h).astype(BF16)
-        low_ref[h] = low
-        grad_feat = part_ref[h] + nt(low, v_ref[:, kv]) + columns[:, h : h + 1]
-        grad_u = back_through(pk_ref[h], grad_feat)
-        gu_ref[h] = grad_u
-        key_weight = nn(grad_u, k_ref[:, kv])
-        query_weight = qw_ref[h]
+        low_ref[h] = get_head(got_ref, 0, h).astype(BF16)
+    for h in range(H):
+        grad_feat = both_ref[h, :DH, :] + nt(low_ref[h], v_ref[:, of_head(h // GROUP)])
+        feat_ref[h] = grad_feat + columns[:, h : h + 1]
+    for h in range(H):
+        gu_ref[h] = back_through(pk_ref[h], feat_ref[h])
+    for h in range(H):
+        key_weight = nn(gu_ref[h], k_ref[:, of_head(h // GROUP)])
+        query_weight = both_ref[h, DH:, :]
         keep_ref[h] = jnp.where(first, query_weight, key_weight)
         give_ref[h] = jnp.where(first, key_weight, query_weight)
 
@@ -303,10 +311,8 @@
     flat = (ROWS + PAD, DH)
     short = (NZ,) + flat
 
-    send, pk = run(
-        key_kernel, [(short, F32), (square, F32)], (), k, v, km,
-        scratch=[pltpu.VMEM(small, F32)], macs=2,
-    )
+    (pk,) = run(key_kernel, [(square, F32)], (), k, km, macs=1)
+    (send,) = run(state_kernel, [(short, F32)], (), pk, v, scratch=[pltpu.VMEM(small, F32)], macs=1)
     first = lax.cond(core[0] == 0, exchange_z, lambda blocks: blocks, send)
     token = lax.ppermute(first[:1, ROWS + H :, :], "core", [(0, 1)])
     first = lax.cond(core[0] == 0, lambda blocks, token: blocks, exchange_after, first, token)
@@ -324,20 +330,21 @@
     attended, total, gd, state = run(
         finish_kernel,
         [(wide, BF16), (flat, F32), (small, F32), (square, BF16)],
-        (), second, pq, num, rden, g, scratch=[pltpu.VMEM((TOK, DH), F32)], macs=1,
+        (), second, pq, num, rden, g, scratch=[pltpu.VMEM((TOK, DH), F32), pltpu.VMEM(wide, F32)], macs=1,
     )
     others = turn(total)
     (send,) = run(suffix_kernel, [(short, F32)], (x, z), second, total, *others)
     third = exchange_z(send)
-    query_grad, query_weight, part, value_part = run(
+    query_grad, both, value_part = run(
         inner_kernel,
-        [(wide, BF16), (half, F32), (square, F32), (narrow, F32)],
-        (), q, v, qm, pq, pk, low, gn, gd, state, norm, macs=7,
+        [(wide, BF16), ((H, DH + FH, DH), F32), (narrow, F32)],
+        (), q, v, qm, pq, pk, low, gn, gd, state, norm,
+        scratch=[pltpu.VMEM(square, BF16), pltpu.VMEM(square, F32), pltpu.VMEM(half, BF16)], macs=7,
     )
     keep, give, grad_u, back = run(
         outer_kernel,
         [(half, F32), (half, F32), (half, BF16), (square, BF16)],
-        (core,), third, part, pk, k, v, query_weight, macs=2,
+        (core,), third, both, pk, k, v, scratch=[pltpu.VMEM(square, F32)], macs=2,
     )
     swap = [(0, 1), (1, 0)]
     mine = keep + lax.ppermute(give, "core", swap)

time: 169 us -> 165 us (0.976)
  Pallas kernels: 20 us -> 11.3 us
  waiting for transfers between devices: 41.2 us -> 47 us
    pallas_call x9 -> x10, Pallas kernels: 20 us -> 11.3 us  [run(): pl.pallas_call(kernel, out_shape=tuple((jax.ShapeDtypeStruct(shape, dtype...]
    all_to_all x1, waiting for transfers between devices: 4.11 us -> 8.13 us  [exchange_z(): lax.all_to_all(blocks, 'z', 0, 0, axis_index_groups=[list(RING)], tiled=T...]
    ppermute x6, waiting for transfers between devices: 8.02 us -> 9.76 us  [turn(): lax.ppermute(rows, 'x', [(i, (i + step) % NX) for i in range(NX)])]
    unnamed x38 -> x34, local copies, waits for them, and re-layouts: 10.3 us -> 8.77 us
  transfers between devices with their start and end apart: 10 -> 10, of which waited for: 9 -> 9; matrix products, arithmetic and copies ran while one was open for 0% -> 0% of each run, Pallas kernels for 5% -> 2%
where the time goes in v5:
time: 165 us; the launch traced here: 164 us
  blocking collectives  81.2 us (49%)
  waiting for transfers between devices  47 us (28%)
  starting transfers between devices  14.3 us (9%)
  Pallas kernels  11.3 us (7%)
  local copies, waits for them, and re-layouts  8.83 us (5%)
    all_to_all x3, blocking collectives, exchange_z(): lax.all_to_all(blocks, 'z', 0, 0, axis_index_groups=[list(RING)], tiled=T...  55.2 us
    ppermute x1, waiting for transfers between devices, shards(): token = lax.ppermute(first[:1, ROWS + H:, :], 'core', [(0, 1)])  27.2 us
    all_to_all x2, blocking collectives, exchange(): return lax.all_to_all(blocks, axes, 0, 0, tiled=True)  26 us
    pallas_call x10, Pallas kernels, run(): pl.pallas_call(kernel, out_shape=tuple((jax.ShapeDtypeStruct(shape, dtype...  11.3 us
    ppermute x6, waiting for transfers between devices, turn(): lax.ppermute(rows, 'x', [(i, (i + step) % NX) for i in range(NX)])  9.76 us
    unnamed x34, local copies, waits for them, and re-layouts  8.77 us
    all_to_all x1, waiting for transfers between devices, exchange_z(): lax.all_to_all(blocks, 'z', 0, 0, axis_index_groups=[list(RING)], tiled=T...  8.13 us
    ppermute x6, starting transfers between devices, turn(): lax.ppermute(rows, 'x', [(i, (i + step) % NX) for i in range(NX)])  5.15 us
  transfers between devices with their start and end apart: 10, of which 9 were waited for; matrix products, arithmetic and copies ran while one was open for 0% of the time, Pallas kernels for 2%

profile of v5, /device:TPU:1, one launch (start us, length us, event | category | flops | bytes accessed | tf_op | source)
XLA Modules:
  0.0 164.4 jit_solution(3015522230058880041)
XLA Ops:
  0.6 0.0 copy-start.6
  0.7 0.9 copy-done.6
  1.6 0.9 copy-done.9
  2.5 0.4 shard_map.109.pk_ref
  2.9 0.0 copy-start
  2.9 0.9 copy-done
  3.8 0.5 shard_map.110
  4.3 1.3 collective-permute-start
  5.6 27.2 %collective-permute-done = f32[1,4,128]{2,1,0:T(4,128)S(1)} collective-permute-done((f32[1,4,128]{2,1,0:T(4,128)S(1)}, f32[1,4,128]{2,1,0:T(4,128)S(1)}, u32[]{:S(2)}, u32[]{:S(2)}) %collective-permute-start) | collective-permute-done | bytes 2080 | tf_op jit(solution)/shard_map/ppermute | solution.py:317
  32.8 18.6 %conditional.3 = (f32[8,208,128]{2,1,0:T(8,128)}) conditional(s32[]{:T(128)} %convert_element_type.4, (f32[8,208,128]{2,1,0:T(8,128)S(1)}, f32[1,4,128]{2,1,0:T(4,128)S(1)}) %tuple.20, f32[8,208,128]{2,1,0:T(8,128)S(1)} %get-tuple-element.65), branch_computations={%region_2.0_spmd, %region_3.0_spmd} | conditional | bytes 1708040 | solution.py:318
  32.8 18.6 %all_to_all.34 = f32[8,208,128]{2,1,0:T(8,128)} all-to-all(f32[8,208,128]{2,1,0:T(8,128)S(1)} %constant_dynamic-update-slice_fusion), channel_id=1, replica_groups={{0,1,3,5,7,6,4,2},{8,9,11,13,15,14,12,10},{16,17,19,21,23,22,20,18},{24..., dimensions={0} | all-to-all | bytes 1703936 | tf_op jit(solution)/shard_map/cond/branch_0_fun/all_to_all | solution.py:291
  51.4 1.2 shard_map.111
  52.7 2.6 %collective-permute-start.3 = (f32[208,128]{1,0:T(8,128)S(1)}, f32[208,128]{1,0:T(8,128)S(1)}, u32[]{:S(2)}, u32[]{:S(2)}) collective-permute-start(f32[208,128]{1,0:T(8,128)S(1)} %shard_map.111), channel_id=1, source_target_pairs={{0,24},{8,0},{16,8},{24,16},{1,25},{9,1},{17,9},{25,17},{2,26},{10... | collective-permute-start | bytes 319496 | tf_op jit(solution)/shard_map/ppermute | solution.py:287
  55.2 0.5 collective-permute-start.2
  55.7 0.6 collective-permute-start.1
  56.4 0.9 shard_map.112
  57.3 3.3 %collective-permute-done.2.two_ref = f32[208,128]{1,0:T(8,128)S(1)} collective-permute-done((f32[208,128]{1,0:T(8,128)S(1)}, f32[208,128]{1,0:T(8,128)S(1)}, u32[]{:S(2)}, u32[]{:S(2)}) %collective-permute-start.2) | collective-permute-done | bytes 106528 | tf_op jit(solution)/shard_map/ppermute | solution.py:287
  60.5 1.2 collective-permute-done.1.one_ref
  61.7 2.3 %shard_map.113 = (f32[8,384,128]{2,1,0:T(8,128)S(1)}, bf16[128,1536]{1,0:T(8,128)(2,1)S(1)}, f32[16,128]{1,0:T(8,128)S(1)}, f32[16,128]{1,0:T(8,128)S(1)}) custom-call(s32[1]{0:T(128)} %bitcast.x_ref, s32[1]{0:T(128)} %bitcast.1.z_ref, f32[8,208,128]{2,1,0:T(8,128)} %get-tuple-element.66.got_ref, f32[208,128]{1,0:T(8,128)} %collective-permute-done.1.one_ref, ...), custom_call_target="tpu_custom_call" | custom-call | flops 50331648 | bytes 4718592 | tf_op jit(solution)/shard_map/pallas_call | solution.py:269
  64.0 25.8 %all_to_all.35.got_ref = f32[8,384,128]{2,1,0:T(8,128)S(1)} all-to-all(f32[8,384,128]{2,1,0:T(8,128)S(1)} %get-tuple-element.44), channel_id=1, replica_groups={{0,1,3,5,7,6,4,2},{8,9,11,13,15,14,12,10},{16,17,19,21,23,22,20,18},{24..., dimensions={0} | all-to-all | bytes 3145728 | tf_op jit(solution)/shard_map/all_to_all | solution.py:291
  89.8 1.2 shard_map.114
  91.0 0.7 copy-done.15
  91.8 0.3 collective-permute-start.6
  92.1 0.5 collective-permute-start.5
  92.6 0.7 collective-permute-start.4
  93.2 2.4 %collective-permute-done.6.three_ref = f32[208,128]{1,0:T(8,128)S(1)} collective-permute-done((f32[208,128]{1,0:T(8,128)S(1)}, f32[208,128]{1,0:T(8,128)S(1)}, u32[]{:S(2)}, u32[]{:S(2)}) %collective-permute-start.6) | collective-permute-done | bytes 106528 | tf_op jit(solution)/shard_map/ppermute | solution.py:287
  95.6 1.6 collective-permute-done.5.two_ref
  97.2 1.4 collective-permute-done.4.one_ref
  98.6 1.0 shard_map.116
  99.5 3.5 %all-to-all-start.3 = ((f32[8,208,128]{2,1,0:T(8,128)}), f32[8,208,128]{2,1,0:T(8,128)S(1)}, u32[]{:S(2)}, u32[]{:S(2)}) async-start(f32[8,208,128]{2,1,0:T(8,128)} %shard_map.116), calls=%async_computation.3 | async-start | bytes 1703936 | tf_op jit(solution)/shard_map/all_to_all | solution.py:291
  103.1 1.0 copy-done.12
  104.1 1.0 copy-done.14
  105.1 1.0 copy-done.16
  106.1 1.9 %shard_map.115 = (bf16[128,1536]{1,0:T(8,128)(2,1)}, f32[12,192,128]{2,1,0:T(8,128)S(1)}, f32[128,512]{1,0:T(8,128)S(1)}) custom-call(bf16[128,1536]{1,0:T(8,128)(2,1)S(1)} %bitcast.26, bf16[128,512]{1,0:T(8,128)(2,1)S(1)} %bitcast.21, bf16[12,64,128]{2,1,0:T(8,128)(2,1)S(1)} %bitcast.30, f32[12,128,128]{2,1,0:T(8,128)S(1)} %get-tuple-element.42.pq_ref, ...), custom_call_target="tpu_custom_call" | custom-call | flops 352321536 | bytes 6979584 | tf_op jit(solution)/shard_map/pallas_call | solution.py:269
  108.0 1.0 copy-done.4
  109.0 8.1 %all-to-all-done.3.got_ref = f32[8,208,128]{2,1,0:T(8,128)S(1)} async-done(((f32[8,208,128]{2,1,0:T(8,128)}), f32[8,208,128]{2,1,0:T(8,128)S(1)}, u32[]{:S(2)}, u32[]{:S(2)}) %all-to-all-start.3) | async-done | bytes 852000 | tf_op jit(solution)/shard_map/all_to_all | solution.py:291
  117.2 1.3 copy-done.5
  118.4 0.8 shard_map.117
  119.2 0.1 collective-permute-start.7
  119.3 1.7 %collective-permute-done.7 = f32[12,64,128]{2,1,0:T(8,128)S(1)} collective-permute-done((f32[12,64,128]{2,1,0:T(8,128)S(1)}, f32[12,64,128]{2,1,0:T(8,128)S(1)}, u32[]{:S(2)}, u32[]{:S(2)}) %collective-permute-start.7) | collective-permute-done | bytes 393248 | tf_op jit(solution)/shard_map/ppermute | solution.py:350
  121.0 0.1 add.3
  121.1 14.3 %all_to_all.36 = f32[16,48,128]{2,1,0:T(8,128)S(1)} all-to-all(f32[16,48,128]{2,1,0:T(8,128)S(1)} %bitcast.35), channel_id=1, replica_groups=mesh['y'=4,'core'=2,'x'=4,'z'=8] {'y','x'}, dimensions={0} | all-to-all | bytes 786432 | tf_op jit(solution)/shard_map/all_to_all | solution.py:283
  135.5 10.8 %all_to_all.37 = f32[8,48,128]{2,1,0:T(8,128)S(1)} all-to-all(f32[8,48,128]{2,1,0:T(8,128)S(1)} %broadcast_in_dim.28), channel_id=1, replica_groups={{0,1,3,5,7,6,4,2},{8,9,11,13,15,14,12,10},{16,17,19,21,23,22,20,18},{24..., dimensions={0} | all-to-all | bytes 393216 | tf_op jit(solution)/shard_map/all_to_all | solution.py:291
  146.3 11.6 %all_to_all.38 = f32[16,48,128]{2,1,0:T(8,128)S(1)} all-to-all(f32[16,48,128]{2,1,0:T(8,128)S(1)} %broadcast_in_dim.29), channel_id=1, replica_groups=mesh['y'=4,'core'=2,'x'=4,'z'=8] {'y','x'}, dimensions={0} | all-to-all | bytes 786432 | tf_op jit(solution)/shard_map/all_to_all | solution.py:283
  158.0 4.2 %collective-permute-start.8 = (f32[12,64,128]{2,1,0:T(8,128)S(1)}, f32[12,64,128]{2,1,0:T(8,128)S(1)}, u32[]{:S(2)}, u32[]{:S(2)}) collective-permute-start(f32[12,64,128]{2,1,0:T(8,128)S(1)} %bitcast.33), channel_id=1, source_target_pairs={{0,32},{32,0},{1,33},{33,1},{2,34},{34,2},{3,35},{35,3},{4,36},{36... | collective-permute-start | bytes 1179656 | tf_op jit(solution)/shard_map/ppermute | solution.py:357
  162.1 1.1 shard_map.118
  163.3 0.2 collective-permute-done.8
  163.5 0.9 select_bitcast_fusion
  (31 shorter events, 0.2 us)
Async XLA Ops:
  0.6 0.9 copy-start.6
  1.6 0.9 copy-start.9
  2.9 0.9 copy-start
  4.3 28.5 %collective-permute-start = (f32[1,4,128]{2,1,0:T(4,128)S(1)}, f32[1,4,128]{2,1,0:T(4,128)S(1)}, u32[]{:S(2)}, u32[]{:S(2)}) collective-permute-start(f32[1,4,128]{2,1,0:T(4,128)S(1)} %slice.4), channel_id=1, source_target_pairs={{0,32},{1,33},{2,34},{3,35},{4,36},{5,37},{6,38},{7,39},{8,40},{9,... | collective-permute-start | bytes 6152 | tf_op jit(solution)/shard_map/ppermute | solution.py:317
  32.8 23.6 %copy-start.1 = (bf16[1,128,512]{2,1,0:T(8,128)(2,1)S(1)}, bf16[1,128,512]{2,1,0:T(8,128)(2,1)}, u32[]{:S(2)}) copy-start(bf16[1,128,512]{2,1,0:T(8,128)(2,1)} %param.12) | copy-start | bytes 393220
  32.8 23.6 %copy-start.3 = (bf16[1,128,1536]{2,1,0:T(8,128)(2,1)S(1)}, bf16[1,128,1536]{2,1,0:T(8,128)(2,1)}, u32[]{:S(2)}) copy-start(bf16[1,128,1536]{2,1,0:T(8,128)(2,1)} %param.10) | copy-start | bytes 1179652
  32.8 23.6 %copy-start.8 = (bf16[12,128,64]{1,2,0:T(8,128)(2,1)S(1)}, bf16[12,128,64]{1,2,0:T(8,128)(2,1)}, u32[]{:S(2)}) copy-start(bf16[12,128,64]{1,2,0:T(8,128)(2,1)} %param.14) | copy-start | bytes 589828
  51.4 10.3 %copy-start.2 = (bf16[1,128,1536]{2,1,0:T(8,128)(2,1)S(1)}, bf16[1,128,1536]{2,1,0:T(8,128)(2,1)}, u32[]{:S(2)}) copy-start(bf16[1,128,1536]{2,1,0:T(8,128)(2,1)} %param.13) | copy-start | bytes 1179652
  52.7 4.6 %collective-permute-start.3 = (f32[208,128]{1,0:T(8,128)S(1)}, f32[208,128]{1,0:T(8,128)S(1)}, u32[]{:S(2)}, u32[]{:S(2)}) collective-permute-start(f32[208,128]{1,0:T(8,128)S(1)} %shard_map.111), channel_id=1, source_target_pairs={{0,24},{8,0},{16,8},{24,16},{1,25},{9,1},{17,9},{25,17},{2,26},{10... | collective-permute-start | bytes 319496 | tf_op jit(solution)/shard_map/ppermute | solution.py:287
  55.2 5.3 %collective-permute-start.2 = (f32[208,128]{1,0:T(8,128)S(1)}, f32[208,128]{1,0:T(8,128)S(1)}, u32[]{:S(2)}, u32[]{:S(2)}) collective-permute-start(f32[208,128]{1,0:T(8,128)S(1)} %shard_map.111), channel_id=1, source_target_pairs={{0,16},{8,24},{16,0},{24,8},{1,17},{9,25},{17,1},{25,9},{2,18},{10... | collective-permute-start | bytes 319496 | tf_op jit(solution)/shard_map/ppermute | solution.py:287
  55.7 6.0 %collective-permute-start.1 = (f32[208,128]{1,0:T(8,128)S(1)}, f32[208,128]{1,0:T(8,128)}, u32[]{:S(2)}, u32[]{:S(2)}) collective-permute-start(f32[208,128]{1,0:T(8,128)S(1)} %shard_map.111), channel_id=1, source_target_pairs={{0,8},{8,16},{16,24},{24,0},{1,9},{9,17},{17,25},{25,1},{2,10},{10... | collective-permute-start | bytes 319496 | tf_op jit(solution)/shard_map/ppermute | solution.py:287
  57.3 32.5 %copy-start.11 = (bf16[12,128,128]{2,1,0:T(8,128)(2,1)}, bf16[12,128,128]{2,1,0:T(8,128)(2,1)S(1)}, u32[]{:S(2)}) copy-start(bf16[12,128,128]{2,1,0:T(8,128)(2,1)S(1)} %get-tuple-element.48.low_ref) | copy-start | bytes 1179652
  64.0 25.8 %copy-start.13 = (bf16[128,1536]{1,0:T(8,128)(2,1)}, bf16[128,1536]{1,0:T(8,128)(2,1)S(1)}, u32[]{:S(2)}) copy-start(bf16[128,1536]{1,0:T(8,128)(2,1)S(1)} %get-tuple-element.49.gn_ref) | copy-start | bytes 1179652
  91.0 0.7 copy-start.15
  91.8 3.9 %collective-permute-start.6 = (f32[208,128]{1,0:T(8,128)S(1)}, f32[208,128]{1,0:T(8,128)S(1)}, u32[]{:S(2)}, u32[]{:S(2)}) collective-permute-start(f32[208,128]{1,0:T(8,128)S(1)} %get-tuple-element.54.own_ref), channel_id=1, source_target_pairs={{0,24},{8,0},{16,8},{24,16},{1,25},{9,1},{17,9},{25,17},{2,26},{10... | collective-permute-start | bytes 319496 | tf_op jit(solution)/shard_map/ppermute | solution.py:287
  92.1 5.1 %collective-permute-start.5 = (f32[208,128]{1,0:T(8,128)S(1)}, f32[208,128]{1,0:T(8,128)S(1)}, u32[]{:S(2)}, u32[]{:S(2)}) collective-permute-start(f32[208,128]{1,0:T(8,128)S(1)} %get-tuple-element.54.own_ref), channel_id=1, source_target_pairs={{0,16},{8,24},{16,0},{24,8},{1,17},{9,25},{17,1},{25,9},{2,18},{10... | collective-permute-start | bytes 319496 | tf_op jit(solution)/shard_map/ppermute | solution.py:287
  92.6 6.0 %collective-permute-start.4 = (f32[208,128]{1,0:T(8,128)S(1)}, f32[208,128]{1,0:T(8,128)S(1)}, u32[]{:S(2)}, u32[]{:S(2)}) collective-permute-start(f32[208,128]{1,0:T(8,128)S(1)} %get-tuple-element.54.own_ref), channel_id=1, source_target_pairs={{0,8},{8,16},{16,24},{24,0},{1,9},{9,17},{17,25},{25,1},{2,10},{10... | collective-permute-start | bytes 319496 | tf_op jit(solution)/shard_map/ppermute | solution.py:287
  99.5 17.6 %all-to-all-start.3 = ((f32[8,208,128]{2,1,0:T(8,128)}), f32[8,208,128]{2,1,0:T(8,128)S(1)}, u32[]{:S(2)}, u32[]{:S(2)}) async-start(f32[8,208,128]{2,1,0:T(8,128)} %shard_map.116), calls=%async_computation.3 | async-start | bytes 1703936 | tf_op jit(solution)/shard_map/all_to_all | solution.py:291
  103.1 1.0 copy-start.12
  104.1 1.0 copy-start.14
  105.1 1.0 copy-start.16
  106.1 11.1 %copy-start.10 = (bf16[1,128,512]{2,1,0:T(8,128)(2,1)S(1)}, bf16[1,128,512]{2,1,0:T(8,128)(2,1)}, u32[]{:S(2)}) copy-start(bf16[1,128,512]{2,1,0:T(8,128)(2,1)} %param.11) | copy-start | bytes 393220
  108.0 1.0 copy-start.4
  117.2 1.3 copy-start.5
  119.2 1.8 %collective-permute-start.7 = (f32[12,64,128]{2,1,0:T(8,128)S(1)}, f32[12,64,128]{2,1,0:T(8,128)S(1)}, u32[]{:S(2)}, u32[]{:S(2)}) collective-permute-start(f32[12,64,128]{2,1,0:T(8,128)S(1)} %get-tuple-element.62), channel_id=1, source_target_pairs={{0,32},{32,0},{1,33},{33,1},{2,34},{34,2},{3,35},{35,3},{4,36},{36... | collective-permute-start | bytes 1179656 | tf_op jit(solution)/shard_map/ppermute | solution.py:350
  121.1 41.1 %copy-start.7 = (bf16[12,128,64]{1,2,0:T(8,128)(2,1)S(1)}, bf16[12,128,64]{1,2,0:T(8,128)(2,1)}, u32[]{:S(2)}) copy-start(bf16[12,128,64]{1,2,0:T(8,128)(2,1)} %param.15) | copy-start | bytes 589828
  158.0 5.5 %collective-permute-start.8 = (f32[12,64,128]{2,1,0:T(8,128)S(1)}, f32[12,64,128]{2,1,0:T(8,128)S(1)}, u32[]{:S(2)}, u32[]{:S(2)}) collective-permute-start(f32[12,64,128]{2,1,0:T(8,128)S(1)} %bitcast.33), channel_id=1, source_target_pairs={{0,32},{32,0},{1,33},{33,1},{2,34},{34,2},{3,35},{35,3},{4,36},{36... | collective-permute-start | bytes 1179656 | tf_op jit(solution)/shard_map/ppermute | solution.py:357

commit v6 on v5

--- a/solution.py
+++ b/solution.py
@@ -15,7 +15,7 @@
 NZ = 8
 ROWS = H * DH // NZ
 PAD = 16
-RING = (0, 1, 3, 5, 7, 6, 4, 2)
+RING = (0, 4, 2, 6, 1, 5, 3, 7)
 SLOT = [RING.index(place) for place in range(NZ)]
 F32 = jnp.float32
 BF16 = jnp.bfloat16
@@ -127,6 +127,7 @@
 
 STATE = slice(0, ROWS)
 NORM = slice(ROWS, ROWS + PAD)
+CHUNKS = [slice(start, start + 48) for start in range(0, ROWS, 48)]
 
 
 def weigh_kernel(
@@ -134,21 +135,25 @@
     send_ref, gn_ref, rden_ref, norm_ref,
 ):
     x, z = x_ref[0], z_ref[0]
-    state = from_rows(x, one_ref, two_ref, three_ref, STATE, True)
     norm = from_rows(x, one_ref, two_ref, three_ref, NORM, True)
-    for j in range(NZ):
-        send_ref[SLOT[j], STATE, :] = state
-        if j < NZ - 1:
-            state = state + got_ref[SLOT[j], STATE, :]
-            norm = norm + jnp.where(j < z, got_ref[SLOT[j], NORM, :], 0.0)
+    for j in range(NZ - 1):
+        norm = norm + jnp.where(j < z, got_ref[SLOT[j], NORM, :], 0.0)
     norm_ref[...] = norm
+    for rows in CHUNKS:
+        state = from_rows(x, one_ref, two_ref, three_ref, rows, True)
+        for j in range(NZ):
+            send_ref[SLOT[j], rows, :] = state
+            if j < NZ - 1:
+                state = state + got_ref[SLOT[j], rows, :]
     columns = norm.T
-    rden_ref[...] = rows_ref[...]
-    for h in range(H):
-        feat = pq_ref[h].astype(BF16).astype(F32)
-        rden_ref[h : h + 1, :] += jnp.sum(feat * columns[:, h : h + 1], axis=0, keepdims=True)
-    rden_ref[...] = 1.0 / rden_ref[...]
-    scale = rden_ref[...].T
+    sums = [
+        jnp.sum(pq_ref[h].astype(BF16).astype(F32) * columns[:, h : h + 1], axis=0, keepdims=True)
+        for h in range(H)
+    ]
+    sums = jnp.concatenate(sums + [jnp.zeros((PAD - H, TOK), F32)], axis=0)
+    inverse = 1.0 / (rows_ref[...] + sums)
+    rden_ref[...] = inverse
+    scale = inverse.T
     for h in range(H):
         grad = (g_ref[:, of_head(h)].astype(F32) * scale[:, h : h + 1]).astype(BF16)
         gn_ref[:, of_head(h)] = grad
@@ -252,14 +257,12 @@
 
 def last_kernel(km_ref, pk_ref, gu_ref, low_ref, vpart_ref, kg_ref, vg_ref):
     for kv in range(KVH):
-        value_sum = vpart_ref[:, of_head(kv)]
-        key_sum = None
-        for h in range(kv * GROUP, (kv + 1) * GROUP):
-            value_sum = value_sum + tn(pk_ref[h].astype(BF16), low_ref[h])
-            term = tn(gu_ref[h], km_ref[h])
-            key_sum = term if key_sum is None else key_sum + term
-        vg_ref[:, of_head(kv)] = value_sum.astype(BF16)
-        kg_ref[:, of_head(kv)] = key_sum.astype(BF16)
+        heads = range(kv * GROUP, (kv + 1) * GROUP)
+        total = sum(tn(pk_ref[h].astype(BF16), low_ref[h]) for h in heads)
+        vg_ref[:, of_head(kv)] = (vpart_ref[:, of_head(kv)] + total).astype(BF16)
+    for kv in range(KVH):
+        heads = range(kv * GROUP, (kv + 1) * GROUP)
+        kg_ref[:, of_head(kv)] = sum(tn(gu_ref[h], km_ref[h]) for h in heads).astype(BF16)
 
 
 def run(kernel, outs, scalars, *arrays, scratch=(), macs=0):

time: 165 us -> 162 us (0.982)
  waiting for transfers between devices: 47 us -> 45.1 us
where the time goes in v6:
time: 162 us; the launch traced here: 161 us
  blocking collectives  79.8 us (49%)
  waiting for transfers between devices  45.1 us (28%)
  starting transfers between devices  14.6 us (9%)
  Pallas kernels  11.3 us (7%)
  local copies, waits for them, and re-layouts  8.83 us (5%)
    all_to_all x3, blocking collectives, exchange_z(): lax.all_to_all(blocks, 'z', 0, 0, axis_index_groups=[list(RING)], tiled=T...  54.1 us
    ppermute x1, waiting for transfers between devices, shards(): token = lax.ppermute(first[:1, ROWS + H:, :], 'core', [(0, 1)])  26.3 us
    all_to_all x2, blocking collectives, exchange(): return lax.all_to_all(blocks, axes, 0, 0, tiled=True)  25.7 us
    pallas_call x10, Pallas kernels, run(): pl.pallas_call(kernel, out_shape=tuple((jax.ShapeDtypeStruct(shape, dtype...  11.3 us
    ppermute x6, waiting for transfers between devices, turn(): lax.ppermute(rows, 'x', [(i, (i + step) % NX) for i in range(NX)])  9.76 us
    unnamed x34, local copies, waits for them, and re-layouts  8.78 us
    all_to_all x1, waiting for transfers between devices, exchange_z(): lax.all_to_all(blocks, 'z', 0, 0, axis_index_groups=[list(RING)], tiled=T...  7.01 us
    ppermute x6, starting transfers between devices, turn(): lax.ppermute(rows, 'x', [(i, (i + step) % NX) for i in range(NX)])  5.15 us
  transfers between devices with their start and end apart: 10, of which 9 were waited for; matrix products, arithmetic and copies ran while one was open for 0% of the time, Pallas kernels for 2%

profile of v6, /device:TPU:1, one launch (start us, length us, event | category | flops | bytes accessed | tf_op | source)
XLA Modules:
  0.0 161.4 jit_solution(13881394549697801440)
XLA Ops:
  0.6 0.0 copy-start.6
  0.7 0.9 copy-done.6
  1.6 0.9 copy-done.9
  2.5 0.4 shard_map.109.pk_ref
  2.9 0.0 copy-start
  2.9 0.9 copy-done
  3.8 0.5 shard_map.110
  4.3 1.3 collective-permute-start
  5.6 26.3 %collective-permute-done = f32[1,4,128]{2,1,0:T(4,128)S(1)} collective-permute-done((f32[1,4,128]{2,1,0:T(4,128)S(1)}, f32[1,4,128]{2,1,0:T(4,128)S(1)}, u32[]{:S(2)}, u32[]{:S(2)}) %collective-permute-start) | collective-permute-done | bytes 2080 | tf_op jit(solution)/shard_map/ppermute | solution.py:320
  31.9 17.9 %conditional.3 = (f32[8,208,128]{2,1,0:T(8,128)}) conditional(s32[]{:T(128)} %convert_element_type.4, (f32[8,208,128]{2,1,0:T(8,128)S(1)}, f32[1,4,128]{2,1,0:T(4,128)S(1)}) %tuple.20, f32[8,208,128]{2,1,0:T(8,128)S(1)} %get-tuple-element.65), branch_computations={%region_2.0_spmd, %region_3.0_spmd} | conditional | bytes 1708040 | solution.py:321
  31.9 17.9 %all_to_all.34 = f32[8,208,128]{2,1,0:T(8,128)} all-to-all(f32[8,208,128]{2,1,0:T(8,128)S(1)} %constant_dynamic-update-slice_fusion), channel_id=1, replica_groups={{0,4,2,6,1,5,3,7},{8,12,10,14,9,13,11,15},{16,20,18,22,17,21,19,23},{24..., dimensions={0} | all-to-all | bytes 1703936 | tf_op jit(solution)/shard_map/cond/branch_0_fun/all_to_all | solution.py:294
  49.9 1.2 shard_map.111
  51.1 2.6 %collective-permute-start.3 = (f32[208,128]{1,0:T(8,128)S(1)}, f32[208,128]{1,0:T(8,128)S(1)}, u32[]{:S(2)}, u32[]{:S(2)}) collective-permute-start(f32[208,128]{1,0:T(8,128)S(1)} %shard_map.111), channel_id=1, source_target_pairs={{0,24},{8,0},{16,8},{24,16},{1,25},{9,1},{17,9},{25,17},{2,26},{10... | collective-permute-start | bytes 319496 | tf_op jit(solution)/shard_map/ppermute | solution.py:290
  53.7 0.5 collective-permute-start.2
  54.2 0.6 collective-permute-start.1
  54.8 0.9 shard_map.112
  55.7 3.3 %collective-permute-done.2.two_ref = f32[208,128]{1,0:T(8,128)S(1)} collective-permute-done((f32[208,128]{1,0:T(8,128)S(1)}, f32[208,128]{1,0:T(8,128)S(1)}, u32[]{:S(2)}, u32[]{:S(2)}) %collective-permute-start.2) | collective-permute-done | bytes 106528 | tf_op jit(solution)/shard_map/ppermute | solution.py:290
  59.0 1.1 collective-permute-done.1.one_ref
  60.2 2.3 %shard_map.113 = (f32[8,384,128]{2,1,0:T(8,128)S(1)}, bf16[128,1536]{1,0:T(8,128)(2,1)S(1)}, f32[16,128]{1,0:T(8,128)S(1)}, f32[16,128]{1,0:T(8,128)S(1)}) custom-call(s32[1]{0:T(128)} %bitcast.x_ref, s32[1]{0:T(128)} %bitcast.1.z_ref, f32[8,208,128]{2,1,0:T(8,128)} %get-tuple-element.66.got_ref, f32[208,128]{1,0:T(8,128)} %collective-permute-done.1.one_ref, ...), custom_call_target="tpu_custom_call" | custom-call | flops 50331648 | bytes 4718592 | tf_op jit(solution)/shard_map/pallas_call | solution.py:272
  62.4 25.2 %all_to_all.35.got_ref = f32[8,384,128]{2,1,0:T(8,128)S(1)} all-to-all(f32[8,384,128]{2,1,0:T(8,128)S(1)} %get-tuple-element.44), channel_id=1, replica_groups={{0,4,2,6,1,5,3,7},{8,12,10,14,9,13,11,15},{16,20,18,22,17,21,19,23},{24..., dimensions={0} | all-to-all | bytes 3145728 | tf_op jit(solution)/shard_map/all_to_all | solution.py:294
  87.6 1.2 shard_map.114
  88.8 0.7 copy-done.15
  89.6 0.3 collective-permute-start.6
  89.9 0.5 collective-permute-start.5
  90.4 0.7 collective-permute-start.4
  91.1 2.1 %collective-permute-done.6.three_ref = f32[208,128]{1,0:T(8,128)S(1)} collective-permute-done((f32[208,128]{1,0:T(8,128)S(1)}, f32[208,128]{1,0:T(8,128)S(1)}, u32[]{:S(2)}, u32[]{:S(2)}) %collective-permute-start.6) | collective-permute-done | bytes 106528 | tf_op jit(solution)/shard_map/ppermute | solution.py:290
  93.1 1.8 %collective-permute-done.5.two_ref = f32[208,128]{1,0:T(8,128)S(1)} collective-permute-done((f32[208,128]{1,0:T(8,128)S(1)}, f32[208,128]{1,0:T(8,128)S(1)}, u32[]{:S(2)}, u32[]{:S(2)}) %collective-permute-start.5) | collective-permute-done | bytes 106528 | tf_op jit(solution)/shard_map/ppermute | solution.py:290
  95.0 1.4 collective-permute-done.4.one_ref
  96.4 1.0 shard_map.116
  97.3 4.1 %all-to-all-start.3 = ((f32[8,208,128]{2,1,0:T(8,128)}), f32[8,208,128]{2,1,0:T(8,128)S(1)}, u32[]{:S(2)}, u32[]{:S(2)}) async-start(f32[8,208,128]{2,1,0:T(8,128)} %shard_map.116), calls=%async_computation.3 | async-start | bytes 1703936 | tf_op jit(solution)/shard_map/all_to_all | solution.py:294
  101.4 1.0 copy-done.12
  102.4 1.0 copy-done.14
  103.4 1.0 copy-done.16
  104.4 1.9 %shard_map.115 = (bf16[128,1536]{1,0:T(8,128)(2,1)}, f32[12,192,128]{2,1,0:T(8,128)S(1)}, f32[128,512]{1,0:T(8,128)S(1)}) custom-call(bf16[128,1536]{1,0:T(8,128)(2,1)S(1)} %bitcast.26, bf16[128,512]{1,0:T(8,128)(2,1)S(1)} %bitcast.21, bf16[12,64,128]{2,1,0:T(8,128)(2,1)S(1)} %bitcast.30, f32[12,128,128]{2,1,0:T(8,128)S(1)} %get-tuple-element.42.pq_ref, ...), custom_call_target="tpu_custom_call" | custom-call | flops 352321536 | bytes 6979584 | tf_op jit(solution)/shard_map/pallas_call | solution.py:272
  106.4 1.0 copy-done.4
  107.4 7.0 %all-to-all-done.3.got_ref = f32[8,208,128]{2,1,0:T(8,128)S(1)} async-done(((f32[8,208,128]{2,1,0:T(8,128)}), f32[8,208,128]{2,1,0:T(8,128)S(1)}, u32[]{:S(2)}, u32[]{:S(2)}) %all-to-all-start.3) | async-done | bytes 852000 | tf_op jit(solution)/shard_map/all_to_all | solution.py:294
  114.4 1.3 copy-done.5
  115.7 0.8 shard_map.117
  116.4 0.1 collective-permute-start.7
  116.5 1.7 %collective-permute-done.7 = f32[12,64,128]{2,1,0:T(8,128)S(1)} collective-permute-done((f32[12,64,128]{2,1,0:T(8,128)S(1)}, f32[12,64,128]{2,1,0:T(8,128)S(1)}, u32[]{:S(2)}, u32[]{:S(2)}) %collective-permute-start.7) | collective-permute-done | bytes 393248 | tf_op jit(solution)/shard_map/ppermute | solution.py:353
  118.2 0.1 add.3
  118.3 14.3 %all_to_all.36 = f32[16,48,128]{2,1,0:T(8,128)S(1)} all-to-all(f32[16,48,128]{2,1,0:T(8,128)S(1)} %bitcast.35), channel_id=1, replica_groups=mesh['y'=4,'core'=2,'x'=4,'z'=8] {'y','x'}, dimensions={0} | all-to-all | bytes 786432 | tf_op jit(solution)/shard_map/all_to_all | solution.py:286
  132.7 11.0 %all_to_all.37 = f32[8,48,128]{2,1,0:T(8,128)S(1)} all-to-all(f32[8,48,128]{2,1,0:T(8,128)S(1)} %broadcast_in_dim.28), channel_id=1, replica_groups={{0,4,2,6,1,5,3,7},{8,12,10,14,9,13,11,15},{16,20,18,22,17,21,19,23},{24..., dimensions={0} | all-to-all | bytes 393216 | tf_op jit(solution)/shard_map/all_to_all | solution.py:294
  143.7 11.4 %all_to_all.38 = f32[16,48,128]{2,1,0:T(8,128)S(1)} all-to-all(f32[16,48,128]{2,1,0:T(8,128)S(1)} %broadcast_in_dim.29), channel_id=1, replica_groups=mesh['y'=4,'core'=2,'x'=4,'z'=8] {'y','x'}, dimensions={0} | all-to-all | bytes 786432 | tf_op jit(solution)/shard_map/all_to_all | solution.py:286
  155.1 3.9 %collective-permute-start.8 = (f32[12,64,128]{2,1,0:T(8,128)S(1)}, f32[12,64,128]{2,1,0:T(8,128)S(1)}, u32[]{:S(2)}, u32[]{:S(2)}) collective-permute-start(f32[12,64,128]{2,1,0:T(8,128)S(1)} %bitcast.33), channel_id=1, source_target_pairs={{0,32},{32,0},{1,33},{33,1},{2,34},{34,2},{3,35},{35,3},{4,36},{36... | collective-permute-start | bytes 1179656 | tf_op jit(solution)/shard_map/ppermute | solution.py:360
  159.1 1.1 shard_map.118
  160.1 0.3 collective-permute-done.8
  160.4 0.9 select_bitcast_fusion
  (31 shorter events, 0.2 us)
Async XLA Ops:
  0.6 0.9 copy-start.6
  1.6 0.9 copy-start.9
  2.9 0.9 copy-start
  4.3 27.6 %collective-permute-start = (f32[1,4,128]{2,1,0:T(4,128)S(1)}, f32[1,4,128]{2,1,0:T(4,128)S(1)}, u32[]{:S(2)}, u32[]{:S(2)}) collective-permute-start(f32[1,4,128]{2,1,0:T(4,128)S(1)} %slice.4), channel_id=1, source_target_pairs={{0,32},{1,33},{2,34},{3,35},{4,36},{5,37},{6,38},{7,39},{8,40},{9,... | collective-permute-start | bytes 6152 | tf_op jit(solution)/shard_map/ppermute | solution.py:320
  31.9 22.9 %copy-start.1 = (bf16[1,128,512]{2,1,0:T(8,128)(2,1)S(1)}, bf16[1,128,512]{2,1,0:T(8,128)(2,1)}, u32[]{:S(2)}) copy-start(bf16[1,128,512]{2,1,0:T(8,128)(2,1)} %param.12) | copy-start | bytes 393220
  31.9 22.9 %copy-start.3 = (bf16[1,128,1536]{2,1,0:T(8,128)(2,1)S(1)}, bf16[1,128,1536]{2,1,0:T(8,128)(2,1)}, u32[]{:S(2)}) copy-start(bf16[1,128,1536]{2,1,0:T(8,128)(2,1)} %param.10) | copy-start | bytes 1179652
  31.9 22.9 %copy-start.8 = (bf16[12,128,64]{1,2,0:T(8,128)(2,1)S(1)}, bf16[12,128,64]{1,2,0:T(8,128)(2,1)}, u32[]{:S(2)}) copy-start(bf16[12,128,64]{1,2,0:T(8,128)(2,1)} %param.14) | copy-start | bytes 589828
  49.9 10.3 %copy-start.2 = (bf16[1,128,1536]{2,1,0:T(8,128)(2,1)S(1)}, bf16[1,128,1536]{2,1,0:T(8,128)(2,1)}, u32[]{:S(2)}) copy-start(bf16[1,128,1536]{2,1,0:T(8,128)(2,1)} %param.13) | copy-start | bytes 1179652
  51.1 4.6 %collective-permute-start.3 = (f32[208,128]{1,0:T(8,128)S(1)}, f32[208,128]{1,0:T(8,128)S(1)}, u32[]{:S(2)}, u32[]{:S(2)}) collective-permute-start(f32[208,128]{1,0:T(8,128)S(1)} %shard_map.111), channel_id=1, source_target_pairs={{0,24},{8,0},{16,8},{24,16},{1,25},{9,1},{17,9},{25,17},{2,26},{10... | collective-permute-start | bytes 319496 | tf_op jit(solution)/shard_map/ppermute | solution.py:290
  53.7 5.4 %collective-permute-start.2 = (f32[208,128]{1,0:T(8,128)S(1)}, f32[208,128]{1,0:T(8,128)S(1)}, u32[]{:S(2)}, u32[]{:S(2)}) collective-permute-start(f32[208,128]{1,0:T(8,128)S(1)} %shard_map.111), channel_id=1, source_target_pairs={{0,16},{8,24},{16,0},{24,8},{1,17},{9,25},{17,1},{25,9},{2,18},{10... | collective-permute-start | bytes 319496 | tf_op jit(solution)/shard_map/ppermute | solution.py:290
  54.2 6.0 %collective-permute-start.1 = (f32[208,128]{1,0:T(8,128)S(1)}, f32[208,128]{1,0:T(8,128)}, u32[]{:S(2)}, u32[]{:S(2)}) collective-permute-start(f32[208,128]{1,0:T(8,128)S(1)} %shard_map.111), channel_id=1, source_target_pairs={{0,8},{8,16},{16,24},{24,0},{1,9},{9,17},{17,25},{25,1},{2,10},{10... | collective-permute-start | bytes 319496 | tf_op jit(solution)/shard_map/ppermute | solution.py:290
  55.7 31.9 %copy-start.11 = (bf16[12,128,128]{2,1,0:T(8,128)(2,1)}, bf16[12,128,128]{2,1,0:T(8,128)(2,1)S(1)}, u32[]{:S(2)}) copy-start(bf16[12,128,128]{2,1,0:T(8,128)(2,1)S(1)} %get-tuple-element.48.low_ref) | copy-start | bytes 1179652
  62.4 25.2 %copy-start.13 = (bf16[128,1536]{1,0:T(8,128)(2,1)}, bf16[128,1536]{1,0:T(8,128)(2,1)S(1)}, u32[]{:S(2)}) copy-start(bf16[128,1536]{1,0:T(8,128)(2,1)S(1)} %get-tuple-element.49.gn_ref) | copy-start | bytes 1179652
  88.8 0.7 copy-start.15
  89.6 3.6 %collective-permute-start.6 = (f32[208,128]{1,0:T(8,128)S(1)}, f32[208,128]{1,0:T(8,128)S(1)}, u32[]{:S(2)}, u32[]{:S(2)}) collective-permute-start(f32[208,128]{1,0:T(8,128)S(1)} %get-tuple-element.54.own_ref), channel_id=1, source_target_pairs={{0,24},{8,0},{16,8},{24,16},{1,25},{9,1},{17,9},{25,17},{2,26},{10... | collective-permute-start | bytes 319496 | tf_op jit(solution)/shard_map/ppermute | solution.py:290
  89.9 5.1 %collective-permute-start.5 = (f32[208,128]{1,0:T(8,128)S(1)}, f32[208,128]{1,0:T(8,128)S(1)}, u32[]{:S(2)}, u32[]{:S(2)}) collective-permute-start(f32[208,128]{1,0:T(8,128)S(1)} %get-tuple-element.54.own_ref), channel_id=1, source_target_pairs={{0,16},{8,24},{16,0},{24,8},{1,17},{9,25},{17,1},{25,9},{2,18},{10... | collective-permute-start | bytes 319496 | tf_op jit(solution)/shard_map/ppermute | solution.py:290
  90.4 6.0 %collective-permute-start.4 = (f32[208,128]{1,0:T(8,128)S(1)}, f32[208,128]{1,0:T(8,128)S(1)}, u32[]{:S(2)}, u32[]{:S(2)}) collective-permute-start(f32[208,128]{1,0:T(8,128)S(1)} %get-tuple-element.54.own_ref), channel_id=1, source_target_pairs={{0,8},{8,16},{16,24},{24,0},{1,9},{9,17},{17,25},{25,1},{2,10},{10... | collective-permute-start | bytes 319496 | tf_op jit(solution)/shard_map/ppermute | solution.py:290
  97.3 17.1 %all-to-all-start.3 = ((f32[8,208,128]{2,1,0:T(8,128)}), f32[8,208,128]{2,1,0:T(8,128)S(1)}, u32[]{:S(2)}, u32[]{:S(2)}) async-start(f32[8,208,128]{2,1,0:T(8,128)} %shard_map.116), calls=%async_computation.3 | async-start | bytes 1703936 | tf_op jit(solution)/shard_map/all_to_all | solution.py:294
  101.4 1.0 copy-start.12
  102.4 1.0 copy-start.14
  103.4 1.0 copy-start.16
  104.4 10.0 %copy-start.10 = (bf16[1,128,512]{2,1,0:T(8,128)(2,1)S(1)}, bf16[1,128,512]{2,1,0:T(8,128)(2,1)}, u32[]{:S(2)}) copy-start(bf16[1,128,512]{2,1,0:T(8,128)(2,1)} %param.11) | copy-start | bytes 393220
  106.4 1.0 copy-start.4
  114.4 1.3 copy-start.5
  116.4 1.8 %collective-permute-start.7 = (f32[12,64,128]{2,1,0:T(8,128)S(1)}, f32[12,64,128]{2,1,0:T(8,128)S(1)}, u32[]{:S(2)}, u32[]{:S(2)}) collective-permute-start(f32[12,64,128]{2,1,0:T(8,128)S(1)} %get-tuple-element.62), channel_id=1, source_target_pairs={{0,32},{32,0},{1,33},{33,1},{2,34},{34,2},{3,35},{35,3},{4,36},{36... | collective-permute-start | bytes 1179656 | tf_op jit(solution)/shard_map/ppermute | solution.py:353
  118.3 40.8 %copy-start.7 = (bf16[12,128,64]{1,2,0:T(8,128)(2,1)S(1)}, bf16[12,128,64]{1,2,0:T(8,128)(2,1)}, u32[]{:S(2)}) copy-start(bf16[12,128,64]{1,2,0:T(8,128)(2,1)} %param.15) | copy-start | bytes 589828
  155.1 5.3 %collective-permute-start.8 = (f32[12,64,128]{2,1,0:T(8,128)S(1)}, f32[12,64,128]{2,1,0:T(8,128)S(1)}, u32[]{:S(2)}, u32[]{:S(2)}) collective-permute-start(f32[12,64,128]{2,1,0:T(8,128)S(1)} %bitcast.33), channel_id=1, source_target_pairs={{0,32},{32,0},{1,33},{33,1},{2,34},{34,2},{3,35},{35,3},{4,36},{36... | collective-permute-start | bytes 1179656 | tf_op jit(solution)/shard_map/ppermute | solution.py:360

commit v7 on v6

--- a/solution.py
+++ b/solution.py
@@ -294,6 +294,13 @@
     return lax.all_to_all(blocks, "z", 0, 0, axis_index_groups=[list(RING)], tiled=True)
 
 
+PLANE = (0, 8, 4, 12, 2, 10, 6, 14, 1, 9, 5, 13, 3, 11, 7, 15)
+
+
+def exchange_yx(blocks):
+    return lax.all_to_all(blocks, ("y", "x"), 0, 0, axis_index_groups=[list(PLANE)], tiled=True)
+
+
 def exchange_after(blocks, token):
     return exchange_z(lax.dynamic_update_slice(blocks, token, (0, ROWS + H, 0)))
 
@@ -351,9 +358,9 @@
     )
     swap = [(0, 1), (1, 0)]
     mine = keep + lax.ppermute(give, "core", swap)
-    mine = exchange(mine.reshape(16, -1, DH), ("y", "x")).sum(0)
+    mine = exchange_yx(mine.reshape(16, -1, DH)).sum(0)
     mine = exchange_z(spread(mine, 8)).sum(0)
-    mine = exchange(spread(mine, 16), ("y", "x")).reshape(half)
+    mine = exchange_yx(spread(mine, 16)).reshape(half)
     key_grad, value_grad = run(
         last_kernel, [(narrow, BF16), (narrow, BF16)], (), km, pk, grad_u, back, value_part, macs=2
     )

time: 162 us -> 162 us (level)
  no operation moved by 1% of the time
where the time goes in v7:
time: 162 us
  blocking collectives  79.9 us (49%)
  waiting for transfers between devices  45.1 us (28%)
  starting transfers between devices  14.8 us (9%)
  Pallas kernels  11.3 us (7%)
  local copies, waits for them, and re-layouts  8.83 us (5%)
    all_to_all x3, blocking collectives, exchange_z(): lax.all_to_all(blocks, 'z', 0, 0, axis_index_groups=[list(RING)], tiled=T...  54.1 us
    ppermute x1, waiting for transfers between devices, shards(): token = lax.ppermute(first[:1, ROWS + H:, :], 'core', [(0, 1)])  26.3 us
    all_to_all x2, blocking collectives, exchange_yx(): lax.all_to_all(blocks, ('y', 'x'), 0, 0, axis_index_groups=[list(PLANE)],...  25.8 us
    pallas_call x10, Pallas kernels, run(): pl.pallas_call(kernel, out_shape=tuple((jax.ShapeDtypeStruct(shape, dtype...  11.3 us
    ppermute x6, waiting for transfers between devices, turn(): lax.ppermute(rows, 'x', [(i, (i + step) % NX) for i in range(NX)])  9.76 us
    unnamed x34, local copies, waits for them, and re-layouts  8.78 us
    all_to_all x1, waiting for transfers between devices, exchange_z(): lax.all_to_all(blocks, 'z', 0, 0, axis_index_groups=[list(RING)], tiled=T...  7.01 us
    ppermute x6, starting transfers between devices, turn(): lax.ppermute(rows, 'x', [(i, (i + step) % NX) for i in range(NX)])  5.15 us
  transfers between devices with their start and end apart: 10, of which 9 were waited for; matrix products, arithmetic and copies ran while one was open for 0% of the time, Pallas kernels for 2%

profile of v7, /device:TPU:1, one launch (start us, length us, event | category | flops | bytes accessed | tf_op | source)
XLA Modules:
  0.0 161.6 jit_solution(8901126300645736096)
XLA Ops:
  0.7 0.9 copy-done.6
  1.6 0.9 copy-done.9
  2.5 0.4 shard_map.109.pk_ref
  2.9 0.9 copy-done
  3.8 0.5 shard_map.110
  4.3 1.3 collective-permute-start
  5.6 26.3 %collective-permute-done = f32[1,4,128]{2,1,0:T(4,128)S(1)} collective-permute-done((f32[1,4,128]{2,1,0:T(4,128)S(1)}, f32[1,4,128]{2,1,0:T(4,128)S(1)}, u32[]{:S(2)}, u32[]{:S(2)}) %collective-permute-start) | collective-permute-done | bytes 2080 | tf_op jit(solution)/shard_map/ppermute | solution.py:327
  31.9 17.9 %conditional.3 = (f32[8,208,128]{2,1,0:T(8,128)}) conditional(s32[]{:T(128)} %convert_element_type.4, (f32[8,208,128]{2,1,0:T(8,128)S(1)}, f32[1,4,128]{2,1,0:T(4,128)S(1)}) %tuple.20, f32[8,208,128]{2,1,0:T(8,128)S(1)} %get-tuple-element.65), branch_computations={%region_2.0_spmd, %region_3.0_spmd} | conditional | bytes 1708040 | solution.py:328
  31.9 17.9 %all_to_all.34 = f32[8,208,128]{2,1,0:T(8,128)} all-to-all(f32[8,208,128]{2,1,0:T(8,128)S(1)} %constant_dynamic-update-slice_fusion), channel_id=1, replica_groups={{0,4,2,6,1,5,3,7},{8,12,10,14,9,13,11,15},{16,20,18,22,17,21,19,23},{24..., dimensions={0} | all-to-all | bytes 1703936 | tf_op jit(solution)/shard_map/cond/branch_0_fun/all_to_all | solution.py:294
  49.9 1.2 shard_map.111
  51.1 2.6 %collective-permute-start.3 = (f32[208,128]{1,0:T(8,128)S(1)}, f32[208,128]{1,0:T(8,128)S(1)}, u32[]{:S(2)}, u32[]{:S(2)}) collective-permute-start(f32[208,128]{1,0:T(8,128)S(1)} %shard_map.111), channel_id=1, source_target_pairs={{0,24},{8,0},{16,8},{24,16},{1,25},{9,1},{17,9},{25,17},{2,26},{10... | collective-permute-start | bytes 319496 | tf_op jit(solution)/shard_map/ppermute | solution.py:290
  53.7 0.5 collective-permute-start.2
  54.2 0.6 collective-permute-start.1
  54.8 0.9 shard_map.112
  55.7 0.0 copy-start.11
  55.7 3.3 %collective-permute-done.2.two_ref = f32[208,128]{1,0:T(8,128)S(1)} collective-permute-done((f32[208,128]{1,0:T(8,128)S(1)}, f32[208,128]{1,0:T(8,128)S(1)}, u32[]{:S(2)}, u32[]{:S(2)}) %collective-permute-start.2) | collective-permute-done | bytes 106528 | tf_op jit(solution)/shard_map/ppermute | solution.py:290
  59.0 1.1 collective-permute-done.1.one_ref
  60.2 2.3 %shard_map.113 = (f32[8,384,128]{2,1,0:T(8,128)S(1)}, bf16[128,1536]{1,0:T(8,128)(2,1)S(1)}, f32[16,128]{1,0:T(8,128)S(1)}, f32[16,128]{1,0:T(8,128)S(1)}) custom-call(s32[1]{0:T(128)} %bitcast.x_ref, s32[1]{0:T(128)} %bitcast.1.z_ref, f32[8,208,128]{2,1,0:T(8,128)} %get-tuple-element.66.got_ref, f32[208,128]{1,0:T(8,128)} %collective-permute-done.1.one_ref, ...), custom_call_target="tpu_custom_call" | custom-call | flops 50331648 | bytes 4718592 | tf_op jit(solution)/shard_map/pallas_call | solution.py:272
  62.4 25.2 %all_to_all.35.got_ref = f32[8,384,128]{2,1,0:T(8,128)S(1)} all-to-all(f32[8,384,128]{2,1,0:T(8,128)S(1)} %get-tuple-element.44), channel_id=1, replica_groups={{0,4,2,6,1,5,3,7},{8,12,10,14,9,13,11,15},{16,20,18,22,17,21,19,23},{24..., dimensions={0} | all-to-all | bytes 3145728 | tf_op jit(solution)/shard_map/all_to_all | solution.py:294
  87.6 1.2 shard_map.114
  88.8 0.7 copy-done.15
  89.6 0.3 collective-permute-start.6
  89.9 0.5 collective-permute-start.5
  90.4 0.7 collective-permute-start.4
  91.1 2.1 %collective-permute-done.6.three_ref = f32[208,128]{1,0:T(8,128)S(1)} collective-permute-done((f32[208,128]{1,0:T(8,128)S(1)}, f32[208,128]{1,0:T(8,128)S(1)}, u32[]{:S(2)}, u32[]{:S(2)}) %collective-permute-start.6) | collective-permute-done | bytes 106528 | tf_op jit(solution)/shard_map/ppermute | solution.py:290
  93.1 1.8 %collective-permute-done.5.two_ref = f32[208,128]{1,0:T(8,128)S(1)} collective-permute-done((f32[208,128]{1,0:T(8,128)S(1)}, f32[208,128]{1,0:T(8,128)S(1)}, u32[]{:S(2)}, u32[]{:S(2)}) %collective-permute-start.5) | collective-permute-done | bytes 106528 | tf_op jit(solution)/shard_map/ppermute | solution.py:290
  95.0 1.4 collective-permute-done.4.one_ref
  96.4 1.0 shard_map.116
  97.3 4.1 %all-to-all-start.3 = ((f32[8,208,128]{2,1,0:T(8,128)}), f32[8,208,128]{2,1,0:T(8,128)S(1)}, u32[]{:S(2)}, u32[]{:S(2)}) async-start(f32[8,208,128]{2,1,0:T(8,128)} %shard_map.116), calls=%async_computation.3 | async-start | bytes 1703936 | tf_op jit(solution)/shard_map/all_to_all | solution.py:294
  101.4 1.0 copy-done.12
  102.4 1.0 copy-done.14
  103.4 1.0 copy-done.16
  104.4 1.9 %shard_map.115 = (bf16[128,1536]{1,0:T(8,128)(2,1)}, f32[12,192,128]{2,1,0:T(8,128)S(1)}, f32[128,512]{1,0:T(8,128)S(1)}) custom-call(bf16[128,1536]{1,0:T(8,128)(2,1)S(1)} %bitcast.26, bf16[128,512]{1,0:T(8,128)(2,1)S(1)} %bitcast.21, bf16[12,64,128]{2,1,0:T(8,128)(2,1)S(1)} %bitcast.30, f32[12,128,128]{2,1,0:T(8,128)S(1)} %get-tuple-element.42.pq_ref, ...), custom_call_target="tpu_custom_call" | custom-call | flops 352321536 | bytes 6979584 | tf_op jit(solution)/shard_map/pallas_call | solution.py:272
  106.4 1.0 copy-done.4
  107.4 7.0 %all-to-all-done.3.got_ref = f32[8,208,128]{2,1,0:T(8,128)S(1)} async-done(((f32[8,208,128]{2,1,0:T(8,128)}), f32[8,208,128]{2,1,0:T(8,128)S(1)}, u32[]{:S(2)}, u32[]{:S(2)}) %all-to-all-start.3) | async-done | bytes 852000 | tf_op jit(solution)/shard_map/all_to_all | solution.py:294
  114.4 1.3 copy-done.5
  115.7 0.8 shard_map.117
  116.4 0.1 collective-permute-start.7
  116.5 1.7 %collective-permute-done.7 = f32[12,64,128]{2,1,0:T(8,128)S(1)} collective-permute-done((f32[12,64,128]{2,1,0:T(8,128)S(1)}, f32[12,64,128]{2,1,0:T(8,128)S(1)}, u32[]{:S(2)}, u32[]{:S(2)}) %collective-permute-start.7) | collective-permute-done | bytes 393248 | tf_op jit(solution)/shard_map/ppermute | solution.py:360
  118.2 0.1 add.3
  118.3 0.0 copy-start.7
  118.3 14.2 %all_to_all.36 = f32[16,48,128]{2,1,0:T(8,128)S(1)} all-to-all(f32[16,48,128]{2,1,0:T(8,128)S(1)} %bitcast.35), channel_id=1, replica_groups={{0,128,64,192,16,144,80,208,8,136,72,200,24,152,88,216},{1,129,65,193,1..., dimensions={0} | all-to-all | bytes 786432 | tf_op jit(solution)/shard_map/all_to_all | solution.py:301
  132.6 11.0 %all_to_all.37 = f32[8,48,128]{2,1,0:T(8,128)S(1)} all-to-all(f32[8,48,128]{2,1,0:T(8,128)S(1)} %broadcast_in_dim.28), channel_id=1, replica_groups={{0,4,2,6,1,5,3,7},{8,12,10,14,9,13,11,15},{16,20,18,22,17,21,19,23},{24..., dimensions={0} | all-to-all | bytes 393216 | tf_op jit(solution)/shard_map/all_to_all | solution.py:294
  143.6 11.6 %all_to_all.38 = f32[16,48,128]{2,1,0:T(8,128)S(1)} all-to-all(f32[16,48,128]{2,1,0:T(8,128)S(1)} %broadcast_in_dim.29), channel_id=1, replica_groups={{0,128,64,192,16,144,80,208,8,136,72,200,24,152,88,216},{1,129,65,193,1..., dimensions={0} | all-to-all | bytes 786432 | tf_op jit(solution)/shard_map/all_to_all | solution.py:301
  155.2 4.1 %collective-permute-start.8 = (f32[12,64,128]{2,1,0:T(8,128)S(1)}, f32[12,64,128]{2,1,0:T(8,128)S(1)}, u32[]{:S(2)}, u32[]{:S(2)}) collective-permute-start(f32[12,64,128]{2,1,0:T(8,128)S(1)} %bitcast.33), channel_id=1, source_target_pairs={{0,32},{32,0},{1,33},{33,1},{2,34},{34,2},{3,35},{35,3},{4,36},{36... | collective-permute-start | bytes 1179656 | tf_op jit(solution)/shard_map/ppermute | solution.py:367
  159.3 1.1 shard_map.118
  160.4 0.3 collective-permute-done.8
  160.7 0.9 select_bitcast_fusion
  (31 shorter events, 0.1 us)
Async XLA Ops:
  0.6 0.9 copy-start.6
  1.6 0.9 copy-start.9
  2.9 0.9 copy-start
  4.3 27.6 %collective-permute-start = (f32[1,4,128]{2,1,0:T(4,128)S(1)}, f32[1,4,128]{2,1,0:T(4,128)S(1)}, u32[]{:S(2)}, u32[]{:S(2)}) collective-permute-start(f32[1,4,128]{2,1,0:T(4,128)S(1)} %slice.4), channel_id=1, source_target_pairs={{0,32},{1,33},{2,34},{3,35},{4,36},{5,37},{6,38},{7,39},{8,40},{9,... | collective-permute-start | bytes 6152 | tf_op jit(solution)/shard_map/ppermute | solution.py:327
  31.9 22.9 %copy-start.1 = (bf16[1,128,512]{2,1,0:T(8,128)(2,1)S(1)}, bf16[1,128,512]{2,1,0:T(8,128)(2,1)}, u32[]{:S(2)}) copy-start(bf16[1,128,512]{2,1,0:T(8,128)(2,1)} %param.12) | copy-start | bytes 393220
  31.9 22.9 %copy-start.3 = (bf16[1,128,1536]{2,1,0:T(8,128)(2,1)S(1)}, bf16[1,128,1536]{2,1,0:T(8,128)(2,1)}, u32[]{:S(2)}) copy-start(bf16[1,128,1536]{2,1,0:T(8,128)(2,1)} %param.10) | copy-start | bytes 1179652
  31.9 22.9 %copy-start.8 = (bf16[12,128,64]{1,2,0:T(8,128)(2,1)S(1)}, bf16[12,128,64]{1,2,0:T(8,128)(2,1)}, u32[]{:S(2)}) copy-start(bf16[12,128,64]{1,2,0:T(8,128)(2,1)} %param.14) | copy-start | bytes 589828
  49.9 10.3 %copy-start.2 = (bf16[1,128,1536]{2,1,0:T(8,128)(2,1)S(1)}, bf16[1,128,1536]{2,1,0:T(8,128)(2,1)}, u32[]{:S(2)}) copy-start(bf16[1,128,1536]{2,1,0:T(8,128)(2,1)} %param.13) | copy-start | bytes 1179652
  51.1 4.6 %collective-permute-start.3 = (f32[208,128]{1,0:T(8,128)S(1)}, f32[208,128]{1,0:T(8,128)S(1)}, u32[]{:S(2)}, u32[]{:S(2)}) collective-permute-start(f32[208,128]{1,0:T(8,128)S(1)} %shard_map.111), channel_id=1, source_target_pairs={{0,24},{8,0},{16,8},{24,16},{1,25},{9,1},{17,9},{25,17},{2,26},{10... | collective-permute-start | bytes 319496 | tf_op jit(solution)/shard_map/ppermute | solution.py:290
  53.7 5.4 %collective-permute-start.2 = (f32[208,128]{1,0:T(8,128)S(1)}, f32[208,128]{1,0:T(8,128)S(1)}, u32[]{:S(2)}, u32[]{:S(2)}) collective-permute-start(f32[208,128]{1,0:T(8,128)S(1)} %shard_map.111), channel_id=1, source_target_pairs={{0,16},{8,24},{16,0},{24,8},{1,17},{9,25},{17,1},{25,9},{2,18},{10... | collective-permute-start | bytes 319496 | tf_op jit(solution)/shard_map/ppermute | solution.py:290
  54.2 6.0 %collective-permute-start.1 = (f32[208,128]{1,0:T(8,128)S(1)}, f32[208,128]{1,0:T(8,128)}, u32[]{:S(2)}, u32[]{:S(2)}) collective-permute-start(f32[208,128]{1,0:T(8,128)S(1)} %shard_map.111), channel_id=1, source_target_pairs={{0,8},{8,16},{16,24},{24,0},{1,9},{9,17},{17,25},{25,1},{2,10},{10... | collective-permute-start | bytes 319496 | tf_op jit(solution)/shard_map/ppermute | solution.py:290
  55.7 31.9 %copy-start.11 = (bf16[12,128,128]{2,1,0:T(8,128)(2,1)}, bf16[12,128,128]{2,1,0:T(8,128)(2,1)S(1)}, u32[]{:S(2)}) copy-start(bf16[12,128,128]{2,1,0:T(8,128)(2,1)S(1)} %get-tuple-element.48.low_ref) | copy-start | bytes 1179652
  62.4 25.2 %copy-start.13 = (bf16[128,1536]{1,0:T(8,128)(2,1)}, bf16[128,1536]{1,0:T(8,128)(2,1)S(1)}, u32[]{:S(2)}) copy-start(bf16[128,1536]{1,0:T(8,128)(2,1)S(1)} %get-tuple-element.49.gn_ref) | copy-start | bytes 1179652
  88.8 0.7 copy-start.15
  89.6 3.6 %collective-permute-start.6 = (f32[208,128]{1,0:T(8,128)S(1)}, f32[208,128]{1,0:T(8,128)S(1)}, u32[]{:S(2)}, u32[]{:S(2)}) collective-permute-start(f32[208,128]{1,0:T(8,128)S(1)} %get-tuple-element.54.own_ref), channel_id=1, source_target_pairs={{0,24},{8,0},{16,8},{24,16},{1,25},{9,1},{17,9},{25,17},{2,26},{10... | collective-permute-start | bytes 319496 | tf_op jit(solution)/shard_map/ppermute | solution.py:290
  89.9 5.1 %collective-permute-start.5 = (f32[208,128]{1,0:T(8,128)S(1)}, f32[208,128]{1,0:T(8,128)S(1)}, u32[]{:S(2)}, u32[]{:S(2)}) collective-permute-start(f32[208,128]{1,0:T(8,128)S(1)} %get-tuple-element.54.own_ref), channel_id=1, source_target_pairs={{0,16},{8,24},{16,0},{24,8},{1,17},{9,25},{17,1},{25,9},{2,18},{10... | collective-permute-start | bytes 319496 | tf_op jit(solution)/shard_map/ppermute | solution.py:290
  90.4 6.0 %collective-permute-start.4 = (f32[208,128]{1,0:T(8,128)S(1)}, f32[208,128]{1,0:T(8,128)S(1)}, u32[]{:S(2)}, u32[]{:S(2)}) collective-permute-start(f32[208,128]{1,0:T(8,128)S(1)} %get-tuple-element.54.own_ref), channel_id=1, source_target_pairs={{0,8},{8,16},{16,24},{24,0},{1,9},{9,17},{17,25},{25,1},{2,10},{10... | collective-permute-start | bytes 319496 | tf_op jit(solution)/shard_map/ppermute | solution.py:290
  97.3 17.1 %all-to-all-start.3 = ((f32[8,208,128]{2,1,0:T(8,128)}), f32[8,208,128]{2,1,0:T(8,128)S(1)}, u32[]{:S(2)}, u32[]{:S(2)}) async-start(f32[8,208,128]{2,1,0:T(8,128)} %shard_map.116), calls=%async_computation.3 | async-start | bytes 1703936 | tf_op jit(solution)/shard_map/all_to_all | solution.py:294
  101.4 1.0 copy-start.12
  102.4 1.0 copy-start.14
  103.4 1.0 copy-start.16
  104.4 10.0 %copy-start.10 = (bf16[1,128,512]{2,1,0:T(8,128)(2,1)S(1)}, bf16[1,128,512]{2,1,0:T(8,128)(2,1)}, u32[]{:S(2)}) copy-start(bf16[1,128,512]{2,1,0:T(8,128)(2,1)} %param.11) | copy-start | bytes 393220
  106.4 1.0 copy-start.4
  114.4 1.3 copy-start.5
  116.4 1.8 %collective-permute-start.7 = (f32[12,64,128]{2,1,0:T(8,128)S(1)}, f32[12,64,128]{2,1,0:T(8,128)S(1)}, u32[]{:S(2)}, u32[]{:S(2)}) collective-permute-start(f32[12,64,128]{2,1,0:T(8,128)S(1)} %get-tuple-element.62), channel_id=1, source_target_pairs={{0,32},{32,0},{1,33},{33,1},{2,34},{34,2},{3,35},{35,3},{4,36},{36... | collective-permute-start | bytes 1179656 | tf_op jit(solution)/shard_map/ppermute | solution.py:360
  118.3 41.1 %copy-start.7 = (bf16[12,128,64]{1,2,0:T(8,128)(2,1)S(1)}, bf16[12,128,64]{1,2,0:T(8,128)(2,1)}, u32[]{:S(2)}) copy-start(bf16[12,128,64]{1,2,0:T(8,128)(2,1)} %param.15) | copy-start | bytes 589828
  155.2 5.5 %collective-permute-start.8 = (f32[12,64,128]{2,1,0:T(8,128)S(1)}, f32[12,64,128]{2,1,0:T(8,128)S(1)}, u32[]{:S(2)}, u32[]{:S(2)}) collective-permute-start(f32[12,64,128]{2,1,0:T(8,128)S(1)} %bitcast.33), channel_id=1, source_target_pairs={{0,32},{32,0},{1,33},{33,1},{2,34},{34,2},{3,35},{35,3},{4,36},{36... | collective-permute-start | bytes 1179656 | tf_op jit(solution)/shard_map/ppermute | solution.py:367
